TPU v7x, 32 devices: a whole 2x2x4 slice. The times are simulated.
32 devices in a mesh: dp: 8 (over z, x), seq: 4 (over y, core).
Axes of the slice: x: 2, y: 2, z: 4, core: 2. Of those that a mesh axis runs over, the one named last changes fastest.
Arguments:
- hidden_in: bfloat16 [24576, 1024], P(('dp', 'seq')), may hold values from -6 to 6
- key_bias: float32 [8, 3072], P('dp', 'seq'), may hold values from -4 to 4
- w_qkv: bfloat16 [1024, 3072], P('dp'), may hold values from -0.1875 to 0.1875
- bias_q: bfloat16 [1024], P('dp'), may hold values from -3 to 3
- bias_v: bfloat16 [1024], P('dp'), may hold values from -0.75 to 0.75
- w_out: bfloat16 [1024, 1024], P('dp'), may hold values from -3 to 3
- bias_out: bfloat16 [1024], P('dp'), may hold values from -3 to 3
- gain_attn: bfloat16 [1024], P('dp'), may hold values from 0.25 to 1.75
- shift_attn: bfloat16 [1024], P('dp'), may hold values from -3 to 3
- w_up: bfloat16 [1024, 4096], P('dp'), may hold values from -0.1875 to 0.1875
- bias_up: bfloat16 [4096], P('dp'), may hold values from -3 to 3
- w_down: bfloat16 [4096, 1024], P('dp'), may hold values from -0.09375 to 0.09375
- bias_down: bfloat16 [1024], P('dp'), may hold values from -3 to 3
- gain_ffn: bfloat16 [1024], P('dp'), may hold values from 0.25 to 1.75
- shift_ffn: bfloat16 [1024], P('dp'), may hold values from -3 to 3
- grad_out: bfloat16 [24576, 1024], P(('dp', 'seq')), may hold values from -6 to 6
Outputs:
- output: bfloat16 [24576, 1024], P(('dp', 'seq'))
- grad_in: float32 [24576, 1024], P(('dp', 'seq'))
- grad_w_qkv: float32 [1024, 3072], P('dp')
- grad_bias_q: float32 [1024], P('dp')
- grad_bias_v: float32 [1024], P('dp')
- grad_w_out: float32 [1024, 1024], P('dp')
- grad_bias_out: float32 [1024], P('dp')
- grad_gain_attn: float32 [1024], P('dp')
- grad_shift_attn: float32 [1024], P('dp')
- grad_w_up: float32 [1024, 4096], P('dp')
- grad_bias_up: float32 [4096], P('dp')
- grad_w_down: float32 [4096, 1024], P('dp')
- grad_bias_down: float32 [1024], P('dp')
- grad_gain_ffn: float32 [1024], P('dp')
- grad_shift_ffn: float32 [1024], P('dp')
All inputs are finite; a program needn't handle non-finite values.
Results may differ from a plain program's by a relative error of at most 0.02.
Values may be sent and summed in bfloat16 or wider, within the bound.
A program may use at most 192 MiB of HBM per device.

v0:
```python
import functools

import jax
import jax.numpy as jnp
from jax import lax
from jax.experimental import pallas as pl
from jax.experimental.pallas import tpu as pltpu
from jax.sharding import PartitionSpec as P

HEAD_DIM = 64
LANES = 128
SCALE = HEAD_DIM**-0.5
norm_eps = 1e-05
F32 = jnp.float32
LOW = jnp.bfloat16


def layer_norm(hidden, gain_vec, shift_vec):
    row_mean = jnp.mean(hidden, -1, keepdims=True)
    centered = hidden - row_mean
    row_var = jnp.mean(centered * centered, -1, keepdims=True)
    return centered * lax.rsqrt(row_var + norm_eps) * gain_vec + shift_vec


def gelu_exact(pre_act):
    return jax.nn.gelu(pre_act, approximate=False)


def matmul(left, right):
    return jnp.dot(left, right, preferred_element_type=F32)


def matmul_left(left, right):
    return lax.dot_general(left, right, (((0,), (0,)), ((), ())), preferred_element_type=F32)


def matmul_right(left, right):
    return lax.dot_general(left, right, (((1,), (1,)), ((), ())), preferred_element_type=F32)


def thirds(value):
    first = value.astype(LOW)
    rest = value - first.astype(F32)
    second = rest.astype(LOW)
    third = (rest - second.astype(F32)).astype(LOW)
    return first.astype(F32), second.astype(F32), third.astype(F32)


def head_mask(rows, head):
    lane = lax.broadcasted_iota(jnp.int32, (rows, LANES), 1)
    return (lane < HEAD_DIM) if head == 0 else (lane >= HEAD_DIM)


def fill_keys(k_ref, v_ref, bias_ref, ka_ref, va_ref):
    rows = k_ref.shape[0]
    lane = lax.broadcasted_iota(jnp.int32, (rows, LANES), 1)
    first, second, third = thirds(bias_ref[...])
    extra = jnp.where(
        lane == 0, first, jnp.where(lane == 1, second, jnp.where(lane == 2, third, 1.0))
    )
    ka_ref[:, :LANES] = k_ref[...]
    ka_ref[:, LANES:] = jnp.where(lane < 6, extra, 0.0).astype(LOW)
    va_ref[:, :LANES] = v_ref[...]
    va_ref[:, LANES:] = jnp.where(lane < 3, 1.0, 0.0).astype(LOW)


def forward_kernel(q_ref, k_ref, v_ref, bias_ref, o_ref, qx_ref, ka_ref, va_ref):
    @pl.when(pl.program_id(0) == 0)
    def _():
        fill_keys(k_ref, v_ref, bias_ref, ka_ref, va_ref)

    rows = q_ref.shape[0]
    lane = lax.broadcasted_iota(jnp.int32, (rows, LANES), 1)
    queries = q_ref[...].astype(F32) * SCALE
    ones = jnp.where(lane < 3, 1.0, 0.0)
    outs = []
    for head in range(2):
        masked = jnp.where(head_mask(rows, head), queries, 0.0)
        wide = jnp.concatenate([masked, ones], 1).astype(LOW)
        scores = matmul_right(wide, ka_ref[...])
        row_max = jnp.max(scores, -1, keepdims=True)
        expo = jnp.exp(scores - row_max).astype(LOW)
        both = matmul(expo, va_ref[...])
        total = both[:, LANES : LANES + 1]
        outs.append(both[:, :LANES] / total)
        first, second, third = thirds(row_max + jnp.log(total))
        qx_ref[head] = jnp.where(
            lane == 3, -first, jnp.where(lane == 4, -second, jnp.where(lane == 5, -third, ones))
        ).astype(LOW)
    o_ref[...] = jnp.where(head_mask(rows, 0), outs[0], outs[1]).astype(LOW)


def backward_kernel(
    q_ref, k_ref, v_ref, kt_ref, bias_ref, qx_ref, o_ref, do_ref,
    dq_ref, dk_ref, dv_ref, ka_ref, va_ref, dk_acc, dv_acc, *, chunk,
):
    step = pl.program_id(0)

    @pl.when(step == 0)
    def _():
        fill_keys(k_ref, v_ref, bias_ref, ka_ref, va_ref)
        dk_acc[...] = jnp.zeros_like(dk_acc)
        dv_acc[...] = jnp.zeros_like(dv_acc)

    rows = q_ref.shape[0]
    length = k_ref.shape[0]
    lane = lax.broadcasted_iota(jnp.int32, (rows, LANES), 1)
    queries = q_ref[...].astype(F32) * SCALE
    grads = do_ref[...].astype(F32)
    dots = grads * o_ref[...].astype(F32)
    q_wide, g_wide, q_mask, g_mask = [], [], [], []
    for head in range(2):
        mask = head_mask(rows, head)
        masked = jnp.where(mask, queries, 0.0).astype(LOW)
        g_masked = jnp.where(mask, grads, 0.0).astype(LOW)
        delta = jnp.sum(jnp.where(mask, dots, 0.0), -1, keepdims=True)
        first, second, third = thirds(delta)
        extra = jnp.where(
            lane == 0, -first, jnp.where(lane == 1, -second, jnp.where(lane == 2, -third, 0.0))
        ).astype(LOW)
        q_mask.append(masked)
        g_mask.append(g_masked)
        q_wide.append(jnp.concatenate([masked, qx_ref[head]], 1))
        g_wide.append(jnp.concatenate([g_masked, extra], 1))
    q_rows = jnp.concatenate(q_mask, 0)
    g_rows = jnp.concatenate(g_mask, 0)
    dq_t = [jnp.zeros((LANES, rows), F32) for _ in range(2)]
    for start in range(0, length, chunk):
        part = slice(start, start + chunk)
        p_list, ds_list = [], []
        for head in range(2):
            probs = jnp.exp(matmul_right(ka_ref[part, :], q_wide[head]))
            d_scores = (probs * matmul_right(va_ref[part, :], g_wide[head])).astype(LOW)
            p_list.append(probs.astype(LOW))
            ds_list.append(d_scores)
            dq_t[head] = dq_t[head] + matmul(kt_ref[:, part], d_scores)
        dv_acc[part, :] += matmul(jnp.concatenate(p_list, 1), g_rows)
        dk_acc[part, :] += matmul(jnp.concatenate(ds_list, 1), q_rows)
    row = lax.broadcasted_iota(jnp.int32, (LANES, rows), 0)
    both = jnp.where(row < HEAD_DIM, dq_t[0], dq_t[1]) * SCALE
    dq_ref[...] = both.T.astype(LOW)

    @pl.when(step == pl.num_programs(0) - 1)
    def _():
        dk_ref[...] = dk_acc[...].astype(LOW)
        dv_ref[...] = dv_acc[...].astype(LOW)


def cost(length, matmuls):
    return pl.CostEstimate(
        flops=2 * 2 * matmuls * length * length * 256,
        bytes_accessed=10 * length * LANES * 2,
        transcendentals=2 * length * length,
    )


def attend_forward(queries, keys, values, bias_wide):
    length = queries.shape[0]
    rows = 256
    tile = pl.BlockSpec((rows, LANES), lambda i: (i, 0))
    whole = pl.BlockSpec((length, LANES), lambda i: (0, 0))
    return pl.pallas_call(
        forward_kernel,
        grid=(length // rows,),
        in_specs=[tile, whole, whole, whole],
        out_specs=[tile, pl.BlockSpec((2, rows, LANES), lambda i: (0, i, 0))],
        out_shape=[
            jax.ShapeDtypeStruct((length, LANES), LOW),
            jax.ShapeDtypeStruct((2, length, LANES), LOW),
        ],
        scratch_shapes=[pltpu.VMEM((length, 2 * LANES), LOW)] * 2,
        compiler_params=pltpu.CompilerParams(vmem_limit_bytes=48 * 2**20),
        cost_estimate=cost(length, 2),
    )(queries, keys, values, bias_wide)


def attend_backward(queries, keys, values, bias_wide, q_extra, context, context_grad):
    length = queries.shape[0]
    rows = 256
    chunk = 768 if length % 768 == 0 else 256
    tile = pl.BlockSpec((rows, LANES), lambda i: (i, 0))
    whole = pl.BlockSpec((length, LANES), lambda i: (0, 0))
    return pl.pallas_call(
        functools.partial(backward_kernel, chunk=chunk),
        grid=(length // rows,),
        in_specs=[
            tile, whole, whole, pl.BlockSpec((LANES, length), lambda i: (0, 0)), whole,
            pl.BlockSpec((2, rows, LANES), lambda i: (0, i, 0)), tile, tile,
        ],
        out_specs=[tile, whole, whole],
        out_shape=[jax.ShapeDtypeStruct((length, LANES), LOW)] * 3,
        scratch_shapes=[pltpu.VMEM((length, 2 * LANES), LOW)] * 2
        + [pltpu.VMEM((length, LANES), F32)] * 2,
        compiler_params=pltpu.CompilerParams(vmem_limit_bytes=48 * 2**20),
        cost_estimate=cost(length, 5),
    )(queries, keys, values, keys.T, bias_wide, q_extra, context, context_grad)


def swap(array, name, mask):
    return lax.ppermute(array, name, [(i, i ^ mask) for i in range(lax.axis_size(name))])


def bits(name):
    return lax.axis_size(name).bit_length() - 1


def bit_order(last):
    dp_bits = [("dp", k) for k in reversed(range(bits("dp")))]
    seq_bits = [("seq", k) for k in reversed(range(1, bits("seq")))]
    order = dp_bits + seq_bits
    if last in order:
        order.remove(last)
        order.append(last)
    return order + [("seq", 0)]


def place(name, k):
    return bits("dp") - 1 - k if name == "dp" else bits("dp") + bits("seq") - 1 - k


def my_bit(name, k):
    return (lax.axis_index(name) >> k) & 1


def double(array, name, k):
    other = swap(array, name, 1 << k)
    at = place(name, k)
    return jnp.where(
        my_bit(name, k) == 0,
        jnp.concatenate([array, other], at),
        jnp.concatenate([other, array], at),
    )


def gather_weight(shard, last):
    rows = shard.shape[0] // lax.axis_size("seq")
    own = lax.dynamic_slice_in_dim(shard, lax.axis_index("seq") * rows, rows, 0)
    own = own.reshape((1,) * (bits("dp") + bits("seq")) + own.shape)
    for name, k in bit_order(last):
        own = double(own, name, k)
    return own.reshape(-1, shard.shape[1])


def reduce_weight(grad, last):
    count = bits("dp") + bits("seq")
    rows = grad.shape[0] >> count
    part = grad.astype(LOW).reshape((2,) * count + (rows, grad.shape[1]))
    for name, k in reversed(bit_order(last)):
        mine = my_bit(name, k)
        away = lax.dynamic_index_in_dim(part, 1 - mine, place(name, k))
        keep = lax.dynamic_index_in_dim(part, mine, place(name, k))
        part = (keep.astype(F32) + swap(away, name, 1 << k).astype(F32)).astype(LOW)
    for k in reversed(range(bits("seq"))):
        part = double(part, "seq", k)
    return part.reshape(-1, grad.shape[1]).astype(F32)


def exchange(blocks):
    return [block if t == 0 else swap(block, "seq", t) for t, block in enumerate(blocks)]


def by_index(blocks):
    count = len(blocks)
    me = lax.axis_index("seq")
    return [lax.select_n(me, *[blocks[i ^ j] for i in range(count)]) for j in range(count)]


def columns(array, group, pair, group_width):
    return lax.dynamic_slice_in_dim(array, group * group_width + pair * LANES, LANES, 1)


def local(
    hidden_in, key_bias, w_qkv, bias_q, bias_v, w_out, bias_out, gain_attn, shift_attn,
    w_up, bias_up, w_down, bias_down, gain_ffn, shift_ffn, grad_out,
):
    groups = lax.axis_size("seq")
    me = lax.axis_index("seq")
    tok_rows, width = hidden_in.shape
    group_width = width // groups
    pairs = group_width // LANES
    wide_y, wide_x, wide_z = ("seq", 1), ("dp", 0), ("dp", 1)

    w_q = gather_weight(w_qkv[:, :width], wide_y)
    w_k = gather_weight(w_qkv[:, width : 2 * width], wide_x)
    w_v = gather_weight(w_qkv[:, 2 * width :], wide_z)
    vectors = (
        bias_q, bias_v, bias_out, gain_attn, shift_attn, bias_down, gain_ffn, shift_ffn, bias_up,
    )
    packed = lax.all_gather(jnp.concatenate(vectors), "dp", axis=0).astype(F32)
    fulls, at = [], 0
    for vector in vectors:
        fulls.append(packed[:, at : at + vector.shape[0]].reshape(-1))
        at += vector.shape[0]
    (f_bias_q, f_bias_v, f_bias_out, f_gain_attn, f_shift_attn, f_bias_down, f_gain_ffn,
     f_shift_ffn, f_bias_up) = fulls
    f_w_out = gather_weight(w_out, wide_z)
    f_w_up = gather_weight(w_up, wide_y)
    f_w_down = gather_weight(w_down, wide_x)

    q_rows = (matmul(hidden_in, w_q) + f_bias_q).astype(LOW)
    k_rows = matmul(hidden_in, w_k).astype(LOW)
    v_rows = (matmul(hidden_in, w_v) + f_bias_v).astype(LOW)
    bias_col = jnp.concatenate(exchange([key_bias[0]] * groups))
    bias_wide = jnp.broadcast_to(bias_col[:, None], (bias_col.shape[0], LANES))
    saved, context_parts = [], []
    for pair in range(pairs):
        got = exchange([
            jnp.concatenate(
                [columns(rows, me ^ t, pair, group_width) for rows in (q_rows, k_rows, v_rows)], 1
            )
            for t in range(groups)
        ])
        queries, keys, values = (
            jnp.concatenate([block[:, i * LANES : (i + 1) * LANES] for block in got])
            for i in range(3)
        )
        context, q_extra = attend_forward(queries, keys, values, bias_wide)
        saved.append((queries, keys, values, bias_wide, q_extra, context))
        context_parts.append(by_index(exchange(
            [context[t * tok_rows : (t + 1) * tok_rows] for t in range(groups)]
        )))
    context = jnp.concatenate(
        [context_parts[pair][j] for j in range(groups) for pair in range(pairs)], 1
    )

    attended = hidden_in.astype(F32) + matmul(context, f_w_out) + f_bias_out
    normed = layer_norm(attended, f_gain_attn, f_shift_attn)
    normed_low = normed.astype(LOW)
    pre_act = matmul(normed_low, f_w_up) + f_bias_up
    activ = gelu_exact(pre_act).astype(LOW)
    branch_sum = normed + matmul(activ, f_w_down) + f_bias_down
    output = layer_norm(branch_sum, f_gain_ffn, f_shift_ffn).astype(LOW)

    upstream = grad_out.astype(F32)
    _, norm_back = jax.vjp(layer_norm, branch_sum, f_gain_ffn, f_shift_ffn)
    d_branch, g_gain_ffn, g_shift_ffn = norm_back(upstream)
    g_bias_down = jnp.sum(d_branch, 0)
    d_branch_low = d_branch.astype(LOW)
    g_w_down = matmul_left(activ, d_branch_low).astype(LOW)
    d_activ = matmul_right(d_branch_low, f_w_down)
    _, gelu_back = jax.vjp(gelu_exact, pre_act)
    d_pre = gelu_back(d_activ)[0]
    g_bias_up = jnp.sum(d_pre, 0)
    d_pre_low = d_pre.astype(LOW)
    g_w_up = matmul_left(normed_low, d_pre_low).astype(LOW)
    d_normed = d_branch + matmul_right(d_pre_low, f_w_up)
    _, attn_norm_back = jax.vjp(layer_norm, attended, f_gain_attn, f_shift_attn)
    d_attended, g_gain_attn, g_shift_attn = attn_norm_back(d_normed)
    g_bias_out = jnp.sum(d_attended, 0)
    d_attended_low = d_attended.astype(LOW)
    g_w_out = matmul_left(context, d_attended_low).astype(LOW)
    d_context = matmul_right(d_attended_low, f_w_out).astype(LOW)
    d_context, g_w_down, g_w_up, g_w_out = lax.optimization_barrier(
        (d_context, g_w_down, g_w_up, g_w_out)
    )
    s_w_down = reduce_weight(g_w_down, wide_x)
    s_w_up = reduce_weight(g_w_up, wide_y)
    s_w_out = reduce_weight(g_w_out, wide_z)

    grad_parts = []
    for pair in range(pairs):
        got = jnp.concatenate(exchange(
            [columns(d_context, me ^ t, pair, group_width) for t in range(groups)]
        ))
        d_heads = jnp.concatenate(attend_backward(*saved[pair], got), 1)
        grad_parts.append(by_index(exchange(
            [d_heads[t * tok_rows : (t + 1) * tok_rows] for t in range(groups)]
        )))
    d_q, d_k, d_v = (
        jnp.concatenate(
            [
                grad_parts[pair][j][:, i * LANES : (i + 1) * LANES]
                for j in range(groups)
                for pair in range(pairs)
            ],
            1,
        )
        for i in range(3)
    )
    s_w_q = reduce_weight(matmul_left(hidden_in, d_q), wide_y)
    s_w_k = reduce_weight(matmul_left(hidden_in, d_k), wide_x)
    s_w_v = reduce_weight(matmul_left(hidden_in, d_v), wide_z)
    g_bias_q = jnp.sum(d_q.astype(F32), 0)
    g_bias_v = jnp.sum(d_v.astype(F32), 0)
    grad_in = d_attended + matmul_right(d_q, w_q) + matmul_right(d_k, w_k) + matmul_right(d_v, w_v)

    vector_grads = (
        g_bias_q, g_bias_v, g_bias_out, g_gain_attn, g_shift_attn, g_bias_down, g_gain_ffn,
        g_shift_ffn, g_bias_up,
    )
    shares = lax.axis_size("dp")
    rows = jnp.concatenate([g.reshape(shares, -1) for g in vector_grads], 1).astype(LOW)
    own = lax.dynamic_index_in_dim(
        lax.psum(rows, ("dp", "seq")), lax.axis_index("dp"), 0, False
    ).astype(F32)
    sums, at = [], 0
    for vector in vectors:
        sums.append(own[at : at + vector.shape[0]])
        at += vector.shape[0]
    (s_bias_q, s_bias_v, s_bias_out, s_gain_attn, s_shift_attn, s_bias_down, s_gain_ffn,
     s_shift_ffn, s_bias_up) = sums
    return (
        output, grad_in, jnp.concatenate([s_w_q, s_w_k, s_w_v], 1), s_bias_q, s_bias_v, s_w_out,
        s_bias_out, s_gain_attn, s_shift_attn, s_w_up, s_bias_up, s_w_down, s_bias_down,
        s_gain_ffn, s_shift_ffn,
    )


def solution(mesh):
    tokens = P(("dp", "seq"), None)
    matrix = P("dp", None)
    vector = P("dp")
    return jax.shard_map(
        local,
        mesh=mesh,
        in_specs=(
            tokens, P("dp", "seq"), matrix, vector, vector, matrix, vector, vector, vector,
            matrix, vector, matrix, vector, vector, vector, tokens,
        ),
        out_specs=(
            tokens, tokens, matrix, vector, vector, matrix, vector, vector, vector, matrix,
            vector, matrix, vector, vector, vector,
        ),
        check_vma=False,
    )
```

profile of v0, /device:TPU:11, one launch (start us, length us, event | category | flops | bytes accessed | tf_op | source)
XLA Modules:
  0.0 951.0 jit_solution(752871846108042945)
XLA Ops:
  10.4 24.7 %all-gather.1 = bf16[8,1,1536]{2,1,0:T(2,128)(2,1)S(1)} all-gather(bf16[1,1,1536]{2,1,0:T(2,128)(2,1)S(1)} %reshape.5114), channel_id=2, replica_groups=mesh['dp'=8,'seq'=4] {'dp'}, dimensions={0}, use_global_device_ids=true | all-gather | bytes 27648 | tf_op jit(solution)/shard_map/all_gather | solution.py:289
  45.8 3.4 collective-permute-start.6
  49.4 5.7 collective-permute-start.31
  70.2 2.7 collective-permute-start.37
  73.0 2.5 collective-permute-done.41
  77.8 8.8 collective-permute-done.13
  87.6 17.6 %collective-permute-start.14 = (bf16[2,2,2,2,1,32,1024]{6,5,4,3,2,1,0:T(8,128)(2,1)S(1)}, bf16[2,2,2,2,1,32,1024]{6,5,4,3,2,1,0:T(8,128)(2,1)S(1)}, u32[]{:S(2)}, u32[]{:S(2)}) collective-permute-start(bf16[2,2,2,2,1,32,1024]{6,5,4,3,2,1,0:T(8,128)(2,1)S(1)} %maximum_select_fusion.14), channel_id=1, source_target_pairs={{0,1},{1,0},{2,3},{3,2},{4,5},{5,4},{6,7},{7,6},{8,9},{9,8},{10,11... | collective-permute-start | bytes 3145736 | tf_op jit(solution)/shard_map/ppermute | solution.py:200
  105.6 4.0 collective-permute-start.4
  117.8 2.9 collective-permute-start.43
  131.8 11.9 %collective-permute-start.17 = (bf16[768,384]{0,1:T(8,128)(2,1)S(1)}, bf16[768,384]{0,1:T(8,128)(2,1)S(1)}, u32[]{:S(2)}, u32[]{:S(2)}) collective-permute-start(bf16[768,384]{0,1:T(8,128)(2,1)S(1)} %pad_maximum_fusion.11), channel_id=1, source_target_pairs={{0,3},{1,2},{2,1},{3,0},{4,7},{5,6},{6,5},{7,4},{8,11},{9,10},{10,... | collective-permute-start | bytes 1769480 | tf_op jit(solution)/shard_map/ppermute | solution.py:200
  149.1 32.9 %collective-permute-done.17 = bf16[768,384]{0,1:T(8,128)(2,1)S(1)} collective-permute-done((bf16[768,384]{0,1:T(8,128)(2,1)S(1)}, bf16[768,384]{0,1:T(8,128)(2,1)S(1)}, u32[]{:S(2)}, u32[]{:S(2)}) %collective-permute-start.17) | collective-permute-done | bytes 589856 | tf_op jit(solution)/shard_map/ppermute | solution.py:200
  183.6 11.5 %collective-permute-start.24 = (bf16[768,384]{0,1:T(8,128)(2,1)}, bf16[768,384]{0,1:T(8,128)(2,1)}, u32[]{:S(2)}, u32[]{:S(2)}) collective-permute-start(bf16[768,384]{0,1:T(8,128)(2,1)} %pad_maximum_fusion.12), channel_id=1, source_target_pairs={{0,1},{1,0},{2,3},{3,2},{4,5},{5,4},{6,7},{7,6},{8,9},{9,8},{10,11... | collective-permute-start | bytes 1769480 | tf_op jit(solution)/shard_map/ppermute | solution.py:200
  201.9 38.6 %shard_map.271 = (bf16[3072,128]{1,0:T(8,128)(2,1)S(1)}, bf16[2,3072,128]{2,1,0:T(8,128)(2,1)S(1)}) custom-call(bf16[3072,128]{1,0:T(8,128)(2,1)S(1)} %copy.193.q_ref, bf16[3072,128]{1,0:T(8,128)(2,1)S(1)} %copy.194.k_ref, bf16[3072,128]{1,0:T(8,128)(2,1)S(1)} %copy.195.v_ref, f32[3072,128]{1,0:T(8,128)} %broadcast_in_dim.10.bias_ref), custom_call_target="tpu_custom_call" | custom-call | flops 19327352832 | bytes 7864320 | tf_op jit(solution)/shard_map/pallas_call | solution.py:162
  252.3 2.6 fusion.53
  261.7 4.2 maximum_select_fusion.2
  266.2 38.8 %shard_map.272 = (bf16[3072,128]{1,0:T(8,128)(2,1)S(1)}, bf16[2,3072,128]{2,1,0:T(8,128)(2,1)S(1)}) custom-call(bf16[3072,128]{1,0:T(8,128)(2,1)S(1)} %copy-done.2, bf16[3072,128]{1,0:T(8,128)(2,1)S(1)} %copy-done.4, bf16[3072,128]{1,0:T(8,128)(2,1)S(1)} %copy-done.6, f32[3072,128]{1,0:T(8,128)} %broadcast_in_dim.10.bias_ref), custom_call_target="tpu_custom_call" | custom-call | flops 19327352832 | bytes 7864320 | tf_op jit(solution)/shard_map/pallas_call | solution.py:162
  308.1 3.4 collective-permute-done.28
  311.5 4.6 collective-permute-done.29
  323.3 2.8 maximum_select_fusion.3
  327.2 5.3 maximum_select_fusion
  332.4 37.0 %multiply_convert_fusion = (bf16[768,4096]{1,0:T(8,128)(2,1)S(1)}, f32[768,4096]{1,0:T(8,128)}, f32[768,4096]{1,0:T(8,128)}) fusion(f32[4096]{0:T(1024)S(1)} %bitcast.358, bf16[1024,4096]{1,0:T(8,128)(2,1)S(1)} %bitcast.306, f32[768,1024]{1,0:T(8,128)S(1)} %get-tuple-element.211, f32[1024]{0:T(1024)S(1)} %copy-done.47, f32[1024]{0:T(1024)S(1)} %get-tuple-element.198, ...), kind=kOutput, calls=%fused_computation.3 | convolution fusion | flops 6654001152 | bytes 43022336 | tf_op jit(solution)/shard_map/dot_general | solution.py:30
  369.4 5.5 maximum_select_fusion.1
  374.9 7.1 fusion.73
  385.1 2.5 fusion.59
  387.6 9.3 convolution_convert_fusion.1
  397.0 21.8 %fusion.74 = (bf16[4096]{0:T(1024)(128)(2,1)}, bf16[768,4096]{1,0:T(8,128)(2,1)}) fusion(f32[768,4096]{1,0:T(8,128)} %get-tuple-element.53, bf16[4096,1024]{1,0:T(8,128)(2,1)} %bitcast.309, f32[768,1024]{1,0:T(8,128)} %copy-done.18, f32[768]{0:T(1024)S(1)} %negate_multiply_fusion.2, f32[768,4096]{1,0:T(8,128)} %get-tuple-element.212, f32[4096]{0:T(1024)S(1)} %bitcast.359), kind=kOutput, calls=%fused_computation.383 | convolution fusion | flops 6494351360 | bytes 43019264 | tf_op jit(solution)/shard_map/dot_general | solution.py:38
  418.8 14.3 %multiply_reduce_fusion = (bf16[1024]{0:T(1024)(128)(2,1)}, f32[768]{0:T(1024)S(1)}, bf16[1024]{0:T(1024)(128)(2,1)}, f32[768,1024]{1,0:T(8,128)S(1)}) fusion(f32[768,1024]{1,0:T(8,128)} %copy-done.14, f32[768]{0:T(1024)S(1)} %fusion.44, f32[768]{0:T(1024)S(1)} %broadcast_multiply_fusion.1, f32[1024]{0:T(1024)S(1)} %get-tuple-element.198, ...), kind=kOutput, calls=%fused_computation.35 | convolution fusion | flops 6450312192 | bytes 24137728 | tf_op jit(solution)/shard_map/dot_general | solution.py:38
  433.1 12.4 %convolution_convert_fusion = bf16[1024,4096]{1,0:T(8,128)(2,1)} fusion(bf16[768,4096]{1,0:T(8,128)(2,1)} %get-tuple-element.217, f32[768,1024]{1,0:T(8,128)S(1)} %copy-done.15, f32[1024]{0:T(1024)S(1)} %copy-done.47, f32[1024]{0:T(1024)S(1)} %get-tuple-element.198, f32[768]{0:T(1024)S(1)} %fusion.44, f32[768]{0:T(1024)S(1)} %broadcast_multiply_fusion.1), kind=kOutput, calls=%fused_computation.21 | convolution fusion | flops 6450577408 | bytes 17840128 | tf_op jit(solution)/shard_map/dot_general | solution.py:34
  449.0 3.3 convolution_convert_fusion.5
  462.2 4.7 constant_dynamic-slice_fusion.9
  466.8 4.9 constant_dynamic-slice_fusion.4
  475.1 58.6 %shard_map.273 = (bf16[3072,128]{1,0:T(8,128)(2,1)S(1)}, bf16[3072,128]{1,0:T(8,128)(2,1)S(1)}, bf16[3072,128]{1,0:T(8,128)(2,1)S(1)}) custom-call(bf16[3072,128]{1,0:T(8,128)(2,1)S(1)} %copy.193.q_ref, bf16[3072,128]{1,0:T(8,128)(2,1)S(1)} %copy.194.k_ref, bf16[3072,128]{1,0:T(8,128)(2,1)S(1)} %copy.195.v_ref, bf16[128,3072]{1,0:T(8,128)(2,1)S(1)} %copy-done.8, ...), custom_call_target="tpu_custom_call" | custom-call | flops 48318382080 | bytes 7864320 | tf_op jit(solution)/shard_map/pallas_call | solution.py:183
  538.3 59.0 %shard_map.274 = (bf16[3072,128]{1,0:T(8,128)(2,1)S(1)}, bf16[3072,128]{1,0:T(8,128)(2,1)S(1)}, bf16[3072,128]{1,0:T(8,128)(2,1)S(1)}) custom-call(bf16[3072,128]{1,0:T(8,128)(2,1)S(1)} %copy-done.3, bf16[3072,128]{1,0:T(8,128)(2,1)S(1)} %copy-done.5, bf16[3072,128]{1,0:T(8,128)(2,1)S(1)} %copy-done.7, bf16[128,3072]{1,0:T(8,128)(2,1)S(1)} %copy-done.9, ...), custom_call_target="tpu_custom_call" | custom-call | flops 48318382080 | bytes 7864320 | tf_op jit(solution)/shard_map/pallas_call | solution.py:183
  601.3 12.8 %collective-permute-done.56 = bf16[768,384]{1,0:T(8,128)(2,1)S(1)} collective-permute-done((bf16[768,384]{1,0:T(8,128)(2,1)S(1)}, bf16[768,384]{1,0:T(8,128)(2,1)S(1)}, u32[]{:S(2)}, u32[]{:S(2)}) %collective-permute-start.56) | collective-permute-done | bytes 589856 | tf_op jit(solution)/shard_map/ppermute | solution.py:200
  614.0 12.0 %collective-permute-done.55 = bf16[768,384]{1,0:T(8,128)(2,1)S(1)} collective-permute-done((bf16[768,384]{1,0:T(8,128)(2,1)S(1)}, bf16[768,384]{1,0:T(8,128)(2,1)S(1)}, u32[]{:S(2)}, u32[]{:S(2)}) %collective-permute-start.55) | collective-permute-done | bytes 589856 | tf_op jit(solution)/shard_map/ppermute | solution.py:200
  628.8 3.5 fusion.76
  632.3 3.2 convolution_convert_fusion.3
  635.5 3.5 fusion.75
  639.3 4.6 convolution_convert_fusion.2
  650.0 42.3 %psum.7 = bf16[8,1536]{1,0:T(8,128)(2,1)S(1)} all-reduce(bf16[8,1536]{1,0:T(8,128)(2,1)S(1)} %constant_dynamic-update-slice_fusion.6), channel_id=1, replica_groups=mesh['dp'=8,'seq'=4] {'dp','seq'}, use_global_device_ids=true, to_apply=%region_17.18 | all-reduce | flops 12288 | bytes 49152 | tf_op jit(solution)/shard_map/psum | solution.py:394
  692.3 7.6 add_add_fusion.2
  704.0 8.6 collective-permute-done.79
  712.9 3.0 collective-permute-start.80
  717.1 3.1 collective-permute-done.80
  720.2 3.0 collective-permute-start.57
  725.6 2.9 collective-permute-done.81
  732.0 10.4 %collective-permute-done.82 = bf16[1,1,1,1,1,32,1024]{6,5,4,3,2,1,0:T(8,128)(2,1)S(1)} collective-permute-done((bf16[1,1,1,1,1,32,1024]{6,5,4,3,2,1,0:T(8,128)(2,1)S(1)}, bf16[1,1,1,1,1,32,1024]{6,5,4,3,2,1,0:T(8,128)(2,1)S(1)}, u32[]{:S(2)}, u32[]{:S(2)}) %collective-permute-start.82) | collective-permute-done | bytes 65568 | tf_op jit(solution)/shard_map/ppermute | solution.py:200
  746.1 3.5 collective-permute-start.84
  753.2 2.7 collective-permute-done.65
  757.7 6.0 collective-permute-done.58
  765.0 4.3 collective-permute-done.73
  770.5 4.4 collective-permute-done.66
  775.0 3.7 add_convert_fusion.1
  786.7 2.6 collective-permute-start.61
  792.4 32.6 %collective-permute-done.86 = bf16[2,2,2,1,1,32,4096]{6,5,4,3,2,1,0:T(8,128)(2,1)S(1)} collective-permute-done((bf16[2,2,2,1,1,32,4096]{6,5,4,3,2,1,0:T(8,128)(2,1)S(1)}, bf16[2,2,2,1,1,32,4096]{6,5,4,3,2,1,0:T(8,128)(2,1)S(1)}, u32[]{:S(2)}, u32[]{:S(2)}) %collective-permute-start.86) | collective-permute-done | bytes 2097184 | tf_op jit(solution)/shard_map/ppermute | solution.py:200
  827.0 4.5 add_convert_fusion
  832.3 4.4 collective-permute-start.77
  838.2 8.6 collective-permute-done.87
  847.3 44.4 %collective-permute-done.93 = bf16[2,2,1,2,1,128,1024]{6,5,4,3,2,1,0:T(8,128)(2,1)S(1)} collective-permute-done((bf16[2,2,1,2,1,128,1024]{6,5,4,3,2,1,0:T(8,128)(2,1)S(1)}, bf16[2,2,1,2,1,128,1024]{6,5,4,3,2,1,0:T(8,128)(2,1)S(1)}, u32[]{:S(2)}, u32[]{:S(2)}) %collective-permute-start.93) | collective-permute-done | bytes 2097184 | tf_op jit(solution)/shard_map/ppermute | solution.py:200
  894.3 18.4 %collective-permute-done.94 = bf16[2,2,1,1,1,128,1024]{6,5,4,3,2,1,0:T(8,128)(2,1)S(1)} collective-permute-done((bf16[2,2,1,1,1,128,1024]{6,5,4,3,2,1,0:T(8,128)(2,1)S(1)}, bf16[2,2,1,1,1,128,1024]{6,5,4,3,2,1,0:T(8,128)(2,1)S(1)}, u32[]{:S(2)}, u32[]{:S(2)}) %collective-permute-start.94) | collective-permute-done | bytes 1048608 | tf_op jit(solution)/shard_map/ppermute | solution.py:200
  914.7 6.6 collective-permute-done.95
  922.5 11.5 %collective-permute-start.91 = (bf16[1,1,1,2,1,32,4096]{6,5,4,3,2,1,0:T(8,128)(2,1)S(1)}, bf16[1,1,1,2,1,32,4096]{6,5,4,3,2,1,0:T(8,128)(2,1)S(1)}, u32[]{:S(2)}, u32[]{:S(2)}) collective-permute-start(bf16[1,1,1,2,1,32,4096]{6,5,4,3,2,1,0:T(8,128)(2,1)S(1)} %maximum_select_fusion.34), channel_id=1, source_target_pairs={{0,1},{1,0},{2,3},{3,2},{4,5},{5,4},{6,7},{7,6},{8,9},{9,8},{10,11... | collective-permute-start | bytes 1572872 | tf_op jit(solution)/shard_map/ppermute | solution.py:200
  936.6 3.0 collective-permute-done.97
  939.7 7.5 collective-permute-start.98
  (540 shorter events, 189.4 us)
Async XLA Ops:
  1.5 37.6 %collective-permute-start.20 = (f32[768]{0:T(1024)S(1)}, f32[768]{0:T(1024)S(1)}, u32[]{:S(2)}, u32[]{:S(2)}) collective-permute-start(f32[768]{0:T(1024)S(1)} %reduce.3), channel_id=1, source_target_pairs={{0,3},{1,2},{2,1},{3,0},{4,7},{5,6},{6,5},{7,4},{8,11},{9,10},{10,... | collective-permute-start | bytes 9224 | tf_op jit(solution)/shard_map/ppermute | solution.py:200
  3.4 38.1 %collective-permute-start.19 = (f32[768]{0:T(1024)S(1)}, f32[768]{0:T(1024)S(1)}, u32[]{:S(2)}, u32[]{:S(2)}) collective-permute-start(f32[768]{0:T(1024)S(1)} %reduce.3), channel_id=1, source_target_pairs={{0,2},{1,3},{2,0},{3,1},{4,6},{5,7},{6,4},{7,5},{8,10},{9,11},{10,... | collective-permute-start | bytes 9224 | tf_op jit(solution)/shard_map/ppermute | solution.py:200
  3.6 38.0 %collective-permute-start.18 = (f32[768]{0:T(1024)S(1)}, f32[768]{0:T(1024)S(1)}, u32[]{:S(2)}, u32[]{:S(2)}) collective-permute-start(f32[768]{0:T(1024)S(1)} %reduce.3), channel_id=1, source_target_pairs={{0,1},{1,0},{2,3},{3,2},{4,5},{5,4},{6,7},{7,6},{8,9},{9,8},{10,11... | collective-permute-start | bytes 9224 | tf_op jit(solution)/shard_map/ppermute | solution.py:200
  4.9 55.2 %collective-permute-start.35 = (bf16[1,1,1,1,1,32,4096]{6,5,4,3,2,1,0:T(8,128)(2,1)S(1)}, bf16[1,1,1,1,1,32,4096]{6,5,4,3,2,1,0:T(8,128)(2,1)S(1)}, u32[]{:S(2)}, u32[]{:S(2)}) collective-permute-start(bf16[1,1,1,1,1,32,4096]{6,5,4,3,2,1,0:T(8,128)(2,1)S(1)} %get-tuple-element.108), channel_id=1, source_target_pairs={{0,16},{4,20},{8,24},{12,28},{16,0},{20,4},{24,8},{28,12},{1,17},{... | collective-permute-start | bytes 786440 | tf_op jit(solution)/shard_map/ppermute | solution.py:200
  8.5 35.4 %collective-permute-start.10 = (bf16[1,1,1,1,1,32,1024]{6,5,4,3,2,1,0:T(8,128)(2,1)S(1)}, bf16[1,1,1,1,1,32,1024]{6,5,4,3,2,1,0:T(8,128)(2,1)S(1)}, u32[]{:S(2)}, u32[]{:S(2)}) collective-permute-start(bf16[1,1,1,1,1,32,1024]{6,5,4,3,2,1,0:T(8,128)(2,1)S(1)} %get-tuple-element.184), channel_id=1, source_target_pairs={{0,16},{4,20},{8,24},{12,28},{16,0},{20,4},{24,8},{28,12},{1,17},{... | collective-permute-start | bytes 196616 | tf_op jit(solution)/shard_map/ppermute | solution.py:200
  43.9 17.6 %collective-permute-start.40 = (bf16[1,1,1,1,1,128,1024]{6,5,4,3,2,1,0:T(8,128)(2,1)S(1)}, bf16[1,1,1,1,1,128,1024]{6,5,4,3,2,1,0:T(8,128)(2,1)S(1)}, u32[]{:S(2)}, u32[]{:S(2)}) collective-permute-start(bf16[1,1,1,1,1,128,1024]{6,5,4,3,2,1,0:T(8,128)(2,1)S(1)} %get-tuple-element.104), channel_id=1, source_target_pairs={{0,16},{4,20},{8,24},{12,28},{16,0},{20,4},{24,8},{28,12},{1,17},{... | collective-permute-start | bytes 786440 | tf_op jit(solution)/shard_map/ppermute | solution.py:200
  61.8 13.7 %collective-permute-start.41 = (bf16[2,1,1,1,1,128,1024]{6,5,0,4,3,2,1:T(8,128)(2,1)S(1)}, bf16[2,1,1,1,1,128,1024]{6,5,0,4,3,2,1:T(8,128)(2,1)S(1)}, u32[]{:S(2)}, u32[]{:S(2)}) collective-permute-start(bf16[2,1,1,1,1,128,1024]{6,5,0,4,3,2,1:T(8,128)(2,1)S(1)} %fusion.19), channel_id=1, source_target_pairs={{0,8},{4,12},{8,0},{12,4},{16,24},{20,28},{24,16},{28,20},{1,9},{5... | collective-permute-start | bytes 1572872 | tf_op jit(solution)/shard_map/ppermute | solution.py:200
  63.6 23.0 %collective-permute-start.13 = (bf16[2,1,2,2,1,32,1024]{6,5,4,3,2,1,0:T(8,128)(2,1)S(1)}, bf16[2,1,2,2,1,32,1024]{6,5,4,3,2,1,0:T(8,128)(2,1)S(1)}, u32[]{:S(2)}, u32[]{:S(2)}) collective-permute-start(bf16[2,1,2,2,1,32,1024]{6,5,4,3,2,1,0:T(8,128)(2,1)S(1)} %maximum_select_fusion.27), channel_id=1, source_target_pairs={{0,8},{4,12},{8,0},{12,4},{16,24},{20,28},{24,16},{28,20},{1,9},{5... | collective-permute-start | bytes 1572872 | tf_op jit(solution)/shard_map/ppermute | solution.py:200
  64.4 23.2 %collective-permute-start.8 = (bf16[2,2,1,2,1,32,1024]{6,5,0,4,3,2,1:T(8,128)(2,1)S(1)}, bf16[2,2,1,2,1,32,1024]{6,5,0,4,3,2,1:T(8,128)(2,1)S(1)}, u32[]{:S(2)}, u32[]{:S(2)}) collective-permute-start(bf16[2,2,1,2,1,32,1024]{6,5,0,4,3,2,1:T(8,128)(2,1)S(1)} %maximum_select_fusion.25), channel_id=1, source_target_pairs={{0,4},{4,0},{8,12},{12,8},{16,20},{20,16},{24,28},{28,24},{1,5},{5... | collective-permute-start | bytes 1572872 | tf_op jit(solution)/shard_map/ppermute | solution.py:200
  67.0 38.4 %collective-permute-start.3 = (bf16[2,2,2,1,1,32,1024]{6,5,4,3,2,1,0:T(8,128)(2,1)S(1)}, bf16[2,2,2,1,1,32,1024]{6,5,4,3,2,1,0:T(8,128)(2,1)S(1)}, u32[]{:S(2)}, u32[]{:S(2)}) collective-permute-start(bf16[2,2,2,1,1,32,1024]{6,5,4,3,2,1,0:T(8,128)(2,1)S(1)} %maximum_select_fusion.23), channel_id=1, source_target_pairs={{0,2},{1,3},{2,0},{3,1},{4,6},{5,7},{6,4},{7,5},{8,10},{9,11},{10,... | collective-permute-start | bytes 1572872 | tf_op jit(solution)/shard_map/ppermute | solution.py:200
  70.2 39.7 %collective-permute-start.37 = (bf16[2,2,1,1,1,32,4096]{6,5,4,3,2,1,0:T(8,128)(2,1)S(1)}, bf16[2,2,1,1,1,32,4096]{6,5,4,3,2,1,0:T(8,128)(2,1)S(1)}, u32[]{:S(2)}, u32[]{:S(2)}) collective-permute-start(bf16[2,2,1,1,1,32,4096]{6,5,4,3,2,1,0:T(8,128)(2,1)S(1)} %copy.212), channel_id=1, source_target_pairs={{0,4},{4,0},{8,12},{12,8},{16,20},{20,16},{24,28},{28,24},{1,5},{5... | collective-permute-start | bytes 3145736 | tf_op jit(solution)/shard_map/ppermute | solution.py:200
  75.5 30.1 %collective-permute-start.33 = (bf16[2,1,2,2,1,32,1024]{6,5,4,3,2,1,0:T(8,128)(2,1)S(1)}, bf16[2,1,2,2,1,32,1024]{6,5,4,3,2,1,0:T(8,128)(2,1)S(1)}, u32[]{:S(2)}, u32[]{:S(2)}) collective-permute-start(bf16[2,1,2,2,1,32,1024]{6,5,4,3,2,1,0:T(8,128)(2,1)S(1)} %maximum_select_fusion.29), channel_id=1, source_target_pairs={{0,8},{4,12},{8,0},{12,4},{16,24},{20,28},{24,16},{28,20},{1,9},{5... | collective-permute-start | bytes 1572872 | tf_op jit(solution)/shard_map/ppermute | solution.py:200
  86.6 25.0 %collective-permute-start.42 = (bf16[2,2,1,1,1,128,1024]{6,5,4,3,2,1,0:T(8,128)(2,1)S(1)}, bf16[2,2,1,1,1,128,1024]{6,5,4,3,2,1,0:T(8,128)(2,1)S(1)}, u32[]{:S(2)}, u32[]{:S(2)}) collective-permute-start(bf16[2,2,1,1,1,128,1024]{6,5,4,3,2,1,0:T(8,128)(2,1)S(1)} %copy.215), channel_id=1, source_target_pairs={{0,2},{1,3},{2,0},{3,1},{4,6},{5,7},{6,4},{7,5},{8,10},{9,11},{10,... | collective-permute-start | bytes 3145736 | tf_op jit(solution)/shard_map/ppermute | solution.py:200
  87.6 33.6 %collective-permute-start.14 = (bf16[2,2,2,2,1,32,1024]{6,5,4,3,2,1,0:T(8,128)(2,1)S(1)}, bf16[2,2,2,2,1,32,1024]{6,5,4,3,2,1,0:T(8,128)(2,1)S(1)}, u32[]{:S(2)}, u32[]{:S(2)}) collective-permute-start(bf16[2,2,2,2,1,32,1024]{6,5,4,3,2,1,0:T(8,128)(2,1)S(1)} %maximum_select_fusion.14), channel_id=1, source_target_pairs={{0,1},{1,0},{2,3},{3,2},{4,5},{5,4},{6,7},{7,6},{8,9},{9,8},{10,11... | collective-permute-start | bytes 3145736 | tf_op jit(solution)/shard_map/ppermute | solution.py:200
  105.6 20.1 %collective-permute-start.4 = (bf16[2,2,2,2,1,32,1024]{6,5,4,3,2,1,0:T(8,128)(2,1)S(1)}, bf16[2,2,2,2,1,32,1024]{6,5,4,3,2,1,0:T(8,128)(2,1)S(1)}, u32[]{:S(2)}, u32[]{:S(2)}) collective-permute-start(bf16[2,2,2,2,1,32,1024]{6,5,4,3,2,1,0:T(8,128)(2,1)S(1)} %maximum_select_fusion.12), channel_id=1, source_target_pairs={{0,1},{1,0},{2,3},{3,2},{4,5},{5,4},{6,7},{7,6},{8,9},{9,8},{10,11... | collective-permute-start | bytes 3145736 | tf_op jit(solution)/shard_map/ppermute | solution.py:200
  109.9 36.8 %collective-permute-start.34 = (bf16[2,2,2,2,1,32,1024]{6,5,4,3,2,1,0:T(8,128)(2,1)S(1)}, bf16[2,2,2,2,1,32,1024]{6,5,4,3,2,1,0:T(8,128)(2,1)S(1)}, u32[]{:S(2)}, u32[]{:S(2)}) collective-permute-start(bf16[2,2,2,2,1,32,1024]{6,5,4,3,2,1,0:T(8,128)(2,1)S(1)} %maximum_select_fusion.15), channel_id=1, source_target_pairs={{0,1},{1,0},{2,3},{3,2},{4,5},{5,4},{6,7},{7,6},{8,9},{9,8},{10,11... | collective-permute-start | bytes 3145736 | tf_op jit(solution)/shard_map/ppermute | solution.py:200
  111.6 150.1 %collective-permute-start.38 = (bf16[2,2,2,1,1,32,4096]{6,5,4,3,2,1,0:T(8,128)(2,1)}, bf16[2,2,2,1,1,32,4096]{6,5,4,3,2,1,0:T(8,128)(2,1)}, u32[]{:S(2)}, u32[]{:S(2)}) collective-permute-start(bf16[2,2,2,1,1,32,4096]{6,5,4,3,2,1,0:T(8,128)(2,1)} %maximum_select_fusion.9), channel_id=1, source_target_pairs={{0,2},{1,3},{2,0},{3,1},{4,6},{5,7},{6,4},{7,5},{8,10},{9,11},{10,... | collective-permute-start | bytes 6291464 | tf_op jit(solution)/shard_map/ppermute | solution.py:200
  117.8 203.9 %collective-permute-start.43 = (bf16[2,2,1,2,1,128,1024]{6,5,4,3,2,1,0:T(8,128)(2,1)}, bf16[2,2,1,2,1,128,1024]{6,5,4,3,2,1,0:T(8,128)(2,1)}, u32[]{:S(2)}, u32[]{:S(2)}) collective-permute-start(bf16[2,2,1,2,1,128,1024]{6,5,4,3,2,1,0:T(8,128)(2,1)} %maximum_select_fusion.11), channel_id=1, source_target_pairs={{0,4},{4,0},{8,12},{12,8},{16,20},{20,16},{24,28},{28,24},{1,5},{5... | collective-permute-start | bytes 6291464 | tf_op jit(solution)/shard_map/ppermute | solution.py:200
  131.8 50.2 %collective-permute-start.17 = (bf16[768,384]{0,1:T(8,128)(2,1)S(1)}, bf16[768,384]{0,1:T(8,128)(2,1)S(1)}, u32[]{:S(2)}, u32[]{:S(2)}) collective-permute-start(bf16[768,384]{0,1:T(8,128)(2,1)S(1)} %pad_maximum_fusion.11), channel_id=1, source_target_pairs={{0,3},{1,2},{2,1},{3,0},{4,7},{5,6},{6,5},{7,4},{8,11},{9,10},{10,... | collective-permute-start | bytes 1769480 | tf_op jit(solution)/shard_map/ppermute | solution.py:200
  143.7 38.3 %collective-permute-start.16 = (bf16[768,384]{0,1:T(8,128)(2,1)S(1)}, bf16[768,384]{0,1:T(8,128)(2,1)S(1)}, u32[]{:S(2)}, u32[]{:S(2)}) collective-permute-start(bf16[768,384]{0,1:T(8,128)(2,1)S(1)} %pad_maximum_fusion.10), channel_id=1, source_target_pairs={{0,2},{1,3},{2,0},{3,1},{4,6},{5,7},{6,4},{7,5},{8,10},{9,11},{10,... | collective-permute-start | bytes 1769480 | tf_op jit(solution)/shard_map/ppermute | solution.py:200
  146.7 36.9 %collective-permute-start.15 = (bf16[768,384]{0,1:T(8,128)(2,1)S(1)}, bf16[768,384]{0,1:T(8,128)(2,1)S(1)}, u32[]{:S(2)}, u32[]{:S(2)}) collective-permute-start(bf16[768,384]{0,1:T(8,128)(2,1)S(1)} %pad_maximum_fusion.9), channel_id=1, source_target_pairs={{0,1},{1,0},{2,3},{3,2},{4,5},{5,4},{6,7},{7,6},{8,9},{9,8},{10,11... | collective-permute-start | bytes 1769480 | tf_op jit(solution)/shard_map/ppermute | solution.py:200
  182.0 59.4 %collective-permute-start.26 = (bf16[768,384]{0,1:T(8,128)(2,1)}, bf16[768,384]{0,1:T(8,128)(2,1)}, u32[]{:S(2)}, u32[]{:S(2)}) collective-permute-start(bf16[768,384]{0,1:T(8,128)(2,1)} %pad_maximum_fusion.14), channel_id=1, source_target_pairs={{0,3},{1,2},{2,1},{3,0},{4,7},{5,6},{6,5},{7,4},{8,11},{9,10},{10,... | collective-permute-start | bytes 1769480 | tf_op jit(solution)/shard_map/ppermute | solution.py:200
  182.0 61.9 %collective-permute-start.25 = (bf16[768,384]{0,1:T(8,128)(2,1)}, bf16[768,384]{0,1:T(8,128)(2,1)}, u32[]{:S(2)}, u32[]{:S(2)}) collective-permute-start(bf16[768,384]{0,1:T(8,128)(2,1)} %pad_maximum_fusion.13), channel_id=1, source_target_pairs={{0,2},{1,3},{2,0},{3,1},{4,6},{5,7},{6,4},{7,5},{8,10},{9,11},{10,... | collective-permute-start | bytes 1769480 | tf_op jit(solution)/shard_map/ppermute | solution.py:200
  183.6 63.2 %collective-permute-start.24 = (bf16[768,384]{0,1:T(8,128)(2,1)}, bf16[768,384]{0,1:T(8,128)(2,1)}, u32[]{:S(2)}, u32[]{:S(2)}) collective-permute-start(bf16[768,384]{0,1:T(8,128)(2,1)} %pad_maximum_fusion.12), channel_id=1, source_target_pairs={{0,1},{1,0},{2,3},{3,2},{4,5},{5,4},{6,7},{7,6},{8,9},{9,8},{10,11... | collective-permute-start | bytes 1769480 | tf_op jit(solution)/shard_map/ppermute | solution.py:200
  241.4 63.8 %collective-permute-start.22 = (bf16[768,128]{1,0:T(8,128)(2,1)}, bf16[768,128]{1,0:T(8,128)(2,1)S(1)}, u32[]{:S(2)}, u32[]{:S(2)}) collective-permute-start(bf16[768,128]{1,0:T(8,128)(2,1)} %get-tuple-element.118), channel_id=1, source_target_pairs={{0,2},{1,3},{2,0},{3,1},{4,6},{5,7},{6,4},{7,5},{8,10},{9,11},{10,... | collective-permute-start | bytes 589832 | tf_op jit(solution)/shard_map/ppermute | solution.py:200
  244.0 62.0 %collective-permute-start.23 = (bf16[768,128]{1,0:T(8,128)(2,1)}, bf16[768,128]{1,0:T(8,128)(2,1)S(1)}, u32[]{:S(2)}, u32[]{:S(2)}) collective-permute-start(bf16[768,128]{1,0:T(8,128)(2,1)} %get-tuple-element.117), channel_id=1, source_target_pairs={{0,3},{1,2},{2,1},{3,0},{4,7},{5,6},{6,5},{7,4},{8,11},{9,10},{10,... | collective-permute-start | bytes 589832 | tf_op jit(solution)/shard_map/ppermute | solution.py:200
  246.8 60.3 %collective-permute-start.21 = (bf16[768,128]{1,0:T(8,128)(2,1)}, bf16[768,128]{1,0:T(8,128)(2,1)}, u32[]{:S(2)}, u32[]{:S(2)}) collective-permute-start(bf16[768,128]{1,0:T(8,128)(2,1)} %get-tuple-element.116), channel_id=1, source_target_pairs={{0,1},{1,0},{2,3},{3,2},{4,5},{5,4},{6,7},{7,6},{8,9},{9,8},{10,11... | collective-permute-start | bytes 589832 | tf_op jit(solution)/shard_map/ppermute | solution.py:200
  265.9 61.3 %collective-permute-start.39 = (bf16[2,2,2,2,1,32,4096]{6,5,4,3,2,1,0:T(8,128)(2,1)S(1)}, bf16[2,2,2,2,1,32,4096]{6,5,4,3,2,1,0:T(8,128)(2,1)}, u32[]{:S(2)}, u32[]{:S(2)}) collective-permute-start(bf16[2,2,2,2,1,32,4096]{6,5,4,3,2,1,0:T(8,128)(2,1)S(1)} %maximum_select_fusion.2), channel_id=1, source_target_pairs={{0,1},{1,0},{2,3},{3,2},{4,5},{5,4},{6,7},{7,6},{8,9},{9,8},{10,11... | collective-permute-start | bytes 12582920 | tf_op jit(solution)/shard_map/ppermute | solution.py:200
  326.1 43.3 %collective-permute-start.44 = (bf16[2,2,2,2,1,128,1024]{6,5,4,3,2,1,0:T(8,128)(2,1)S(1)}, bf16[2,2,2,2,1,128,1024]{6,5,4,3,2,1,0:T(8,128)(2,1)}, u32[]{:S(2)}, u32[]{:S(2)}) collective-permute-start(bf16[2,2,2,2,1,128,1024]{6,5,4,3,2,1,0:T(8,128)(2,1)S(1)} %maximum_select_fusion.3), channel_id=1, source_target_pairs={{0,1},{1,0},{2,3},{3,2},{4,5},{5,4},{6,7},{7,6},{8,9},{9,8},{10,11... | collective-permute-start | bytes 12582920 | tf_op jit(solution)/shard_map/ppermute | solution.py:200
  455.7 16.1 %collective-permute-start.47 = (bf16[768,128]{1,0:T(8,128)(2,1)}, bf16[768,128]{1,0:T(8,128)(2,1)}, u32[]{:S(2)}, u32[]{:S(2)}) collective-permute-start(bf16[768,128]{1,0:T(8,128)(2,1)} %get-tuple-element.73), channel_id=1, source_target_pairs={{0,3},{1,2},{2,1},{3,0},{4,7},{5,6},{6,5},{7,4},{8,11},{9,10},{10,... | collective-permute-start | bytes 589832 | tf_op jit(solution)/shard_map/ppermute | solution.py:200
  455.8 16.8 %collective-permute-start.46 = (bf16[768,128]{1,0:T(8,128)(2,1)}, bf16[768,128]{1,0:T(8,128)(2,1)}, u32[]{:S(2)}, u32[]{:S(2)}) collective-permute-start(bf16[768,128]{1,0:T(8,128)(2,1)} %get-tuple-element.74), channel_id=1, source_target_pairs={{0,2},{1,3},{2,0},{3,1},{4,6},{5,7},{6,4},{7,5},{8,10},{9,11},{10,... | collective-permute-start | bytes 589832 | tf_op jit(solution)/shard_map/ppermute | solution.py:200
  457.0 15.6 %collective-permute-start.45 = (bf16[768,128]{1,0:T(8,128)(2,1)}, bf16[768,128]{1,0:T(8,128)(2,1)}, u32[]{:S(2)}, u32[]{:S(2)}) collective-permute-start(bf16[768,128]{1,0:T(8,128)(2,1)} %get-tuple-element.75), channel_id=1, source_target_pairs={{0,1},{1,0},{2,3},{3,2},{4,5},{5,4},{6,7},{7,6},{8,9},{9,8},{10,11... | collective-permute-start | bytes 589832 | tf_op jit(solution)/shard_map/ppermute | solution.py:200
  457.8 76.7 %collective-permute-start.53 = (bf16[768,128]{1,0:T(8,128)(2,1)S(1)}, bf16[768,128]{1,0:T(8,128)(2,1)S(1)}, u32[]{:S(2)}, u32[]{:S(2)}) collective-permute-start(bf16[768,128]{1,0:T(8,128)(2,1)S(1)} %get-tuple-element.70), channel_id=1, source_target_pairs={{0,3},{1,2},{2,1},{3,0},{4,7},{5,6},{6,5},{7,4},{8,11},{9,10},{10,... | collective-permute-start | bytes 589832 | tf_op jit(solution)/shard_map/ppermute | solution.py:200
  457.8 76.8 %collective-permute-start.52 = (bf16[768,128]{1,0:T(8,128)(2,1)S(1)}, bf16[768,128]{1,0:T(8,128)(2,1)}, u32[]{:S(2)}, u32[]{:S(2)}) collective-permute-start(bf16[768,128]{1,0:T(8,128)(2,1)S(1)} %get-tuple-element.71), channel_id=1, source_target_pairs={{0,2},{1,3},{2,0},{3,1},{4,6},{5,7},{6,4},{7,5},{8,10},{9,11},{10,... | collective-permute-start | bytes 589832 | tf_op jit(solution)/shard_map/ppermute | solution.py:200
  471.8 63.0 %collective-permute-start.51 = (bf16[768,128]{1,0:T(8,128)(2,1)S(1)}, bf16[768,128]{1,0:T(8,128)(2,1)S(1)}, u32[]{:S(2)}, u32[]{:S(2)}) collective-permute-start(bf16[768,128]{1,0:T(8,128)(2,1)S(1)} %get-tuple-element.72), channel_id=1, source_target_pairs={{0,1},{1,0},{2,3},{3,2},{4,5},{5,4},{6,7},{7,6},{8,9},{9,8},{10,11... | collective-permute-start | bytes 589832 | tf_op jit(solution)/shard_map/ppermute | solution.py:200
  472.6 227.4 %collective-permute-start.78 = (bf16[2,2,2,2,1,32,1024]{6,5,4,3,2,1,0:T(8,128)(2,1)}, bf16[2,2,2,2,1,32,1024]{6,5,4,3,2,1,0:T(8,128)(2,1)}, u32[]{:S(2)}, u32[]{:S(2)}) collective-permute-start(bf16[2,2,2,2,1,32,1024]{6,5,4,3,2,1,0:T(8,128)(2,1)} %constant_dynamic-slice_fusion.14), channel_id=1, source_target_pairs={{0,1},{1,0},{2,3},{3,2},{4,5},{5,4},{6,7},{7,6},{8,9},{9,8},{10,11... | collective-permute-start | bytes 3145736 | tf_op jit(solution)/shard_map/ppermute | solution.py:200
  472.6 302.3 %collective-permute-start.85 = (bf16[2,2,2,2,1,32,4096]{6,5,4,3,2,1,0:T(8,128)(2,1)}, bf16[2,2,2,2,1,32,4096]{6,5,4,3,2,1,0:T(8,128)(2,1)}, u32[]{:S(2)}, u32[]{:S(2)}) collective-permute-start(bf16[2,2,2,2,1,32,4096]{6,5,4,3,2,1,0:T(8,128)(2,1)} %constant_dynamic-slice_fusion.9), channel_id=1, source_target_pairs={{0,1},{1,0},{2,3},{3,2},{4,5},{5,4},{6,7},{7,6},{8,9},{9,8},{10,11... | collective-permute-start | bytes 12582920 | tf_op jit(solution)/shard_map/ppermute | solution.py:200
  534.5 63.6 %collective-permute-start.48 = (bf16[768,384]{1,0:T(8,128)(2,1)S(1)}, bf16[768,384]{1,0:T(8,128)(2,1)S(1)}, u32[]{:S(2)}, u32[]{:S(2)}) collective-permute-start(bf16[768,384]{1,0:T(8,128)(2,1)S(1)} %get-tuple-element.66), channel_id=1, source_target_pairs={{0,1},{1,0},{2,3},{3,2},{4,5},{5,4},{6,7},{7,6},{8,9},{9,8},{10,11... | collective-permute-start | bytes 1769480 | tf_op jit(solution)/shard_map/ppermute | solution.py:200
  534.6 63.8 %collective-permute-start.50 = (bf16[768,384]{1,0:T(8,128)(2,1)S(1)}, bf16[768,384]{1,0:T(8,128)(2,1)S(1)}, u32[]{:S(2)}, u32[]{:S(2)}) collective-permute-start(bf16[768,384]{1,0:T(8,128)(2,1)S(1)} %get-tuple-element.67), channel_id=1, source_target_pairs={{0,3},{1,2},{2,1},{3,0},{4,7},{5,6},{6,5},{7,4},{8,11},{9,10},{10,... | collective-permute-start | bytes 1769480 | tf_op jit(solution)/shard_map/ppermute | solution.py:200
  534.7 63.8 %collective-permute-start.49 = (bf16[768,384]{1,0:T(8,128)(2,1)S(1)}, bf16[768,384]{1,0:T(8,128)(2,1)S(1)}, u32[]{:S(2)}, u32[]{:S(2)}) collective-permute-start(bf16[768,384]{1,0:T(8,128)(2,1)S(1)} %get-tuple-element.68), channel_id=1, source_target_pairs={{0,2},{1,3},{2,0},{3,1},{4,6},{5,7},{6,4},{7,5},{8,10},{9,11},{10,... | collective-permute-start | bytes 1769480 | tf_op jit(solution)/shard_map/ppermute | solution.py:200
  598.5 15.6 %collective-permute-start.56 = (bf16[768,384]{1,0:T(8,128)(2,1)S(1)}, bf16[768,384]{1,0:T(8,128)(2,1)S(1)}, u32[]{:S(2)}, u32[]{:S(2)}) collective-permute-start(bf16[768,384]{1,0:T(8,128)(2,1)S(1)} %get-tuple-element.64), channel_id=1, source_target_pairs={{0,3},{1,2},{2,1},{3,0},{4,7},{5,6},{6,5},{7,4},{8,11},{9,10},{10,... | collective-permute-start | bytes 1769480 | tf_op jit(solution)/shard_map/ppermute | solution.py:200
  598.5 27.5 %collective-permute-start.55 = (bf16[768,384]{1,0:T(8,128)(2,1)S(1)}, bf16[768,384]{1,0:T(8,128)(2,1)S(1)}, u32[]{:S(2)}, u32[]{:S(2)}) collective-permute-start(bf16[768,384]{1,0:T(8,128)(2,1)S(1)} %get-tuple-element.65), channel_id=1, source_target_pairs={{0,2},{1,3},{2,0},{3,1},{4,6},{5,7},{6,4},{7,5},{8,10},{9,11},{10,... | collective-permute-start | bytes 1769480 | tf_op jit(solution)/shard_map/ppermute | solution.py:200
  600.6 226.5 %collective-permute-start.92 = (bf16[2,2,2,2,1,128,1024]{6,5,4,3,2,1,0:T(8,128)(2,1)}, bf16[2,2,2,2,1,128,1024]{6,5,4,3,2,1,0:T(8,128)(2,1)}, u32[]{:S(2)}, u32[]{:S(2)}) collective-permute-start(bf16[2,2,2,2,1,128,1024]{6,5,4,3,2,1,0:T(8,128)(2,1)} %constant_dynamic-slice_fusion.4), channel_id=1, source_target_pairs={{0,1},{1,0},{2,3},{3,2},{4,5},{5,4},{6,7},{7,6},{8,9},{9,8},{10,11... | collective-permute-start | bytes 12582920 | tf_op jit(solution)/shard_map/ppermute | solution.py:200
  646.7 76.6 %collective-permute-start.71 = (bf16[2,2,2,2,1,32,1024]{6,5,4,3,2,1,0:T(8,128)(2,1)}, bf16[2,2,2,2,1,32,1024]{6,5,4,3,2,1,0:T(8,128)(2,1)}, u32[]{:S(2)}, u32[]{:S(2)}) collective-permute-start(bf16[2,2,2,2,1,32,1024]{6,5,4,3,2,1,0:T(8,128)(2,1)} %constant_dynamic-slice_fusion.20), channel_id=1, source_target_pairs={{0,1},{1,0},{2,3},{3,2},{4,5},{5,4},{6,7},{7,6},{8,9},{9,8},{10,11... | collective-permute-start | bytes 3145736 | tf_op jit(solution)/shard_map/ppermute | solution.py:200
  649.8 79.0 %collective-permute-start.64 = (bf16[2,2,2,2,1,32,1024]{6,5,4,3,2,1,0:T(8,128)(2,1)}, bf16[2,2,2,2,1,32,1024]{6,5,4,3,2,1,0:T(8,128)(2,1)}, u32[]{:S(2)}, u32[]{:S(2)}) collective-permute-start(bf16[2,2,2,2,1,32,1024]{6,5,4,3,2,1,0:T(8,128)(2,1)} %constant_dynamic-slice_fusion.25), channel_id=1, source_target_pairs={{0,1},{1,0},{2,3},{3,2},{4,5},{5,4},{6,7},{7,6},{8,9},{9,8},{10,11... | collective-permute-start | bytes 3145736 | tf_op jit(solution)/shard_map/ppermute | solution.py:200
  720.2 25.9 %collective-permute-start.57 = (bf16[2,2,2,2,1,32,1024]{6,5,4,3,2,1,0:T(8,128)(2,1)S(1)}, bf16[2,2,2,2,1,32,1024]{6,5,4,3,2,1,0:T(8,128)(2,1)S(1)}, u32[]{:S(2)}, u32[]{:S(2)}) collective-permute-start(bf16[2,2,2,2,1,32,1024]{6,5,4,3,2,1,0:T(8,128)(2,1)S(1)} %constant_dynamic-slice_fusion.30), channel_id=1, source_target_pairs={{0,1},{1,0},{2,3},{3,2},{4,5},{5,4},{6,7},{7,6},{8,9},{9,8},{10,11... | collective-permute-start | bytes 3145736 | tf_op jit(solution)/shard_map/ppermute | solution.py:200
  728.5 24.1 %collective-permute-start.72 = (bf16[2,1,2,2,1,32,1024]{6,5,4,3,2,1,0:T(8,128)(2,1)S(1)}, bf16[2,1,2,2,1,32,1024]{6,5,4,3,2,1,0:T(8,128)(2,1)S(1)}, u32[]{:S(2)}, u32[]{:S(2)}) collective-permute-start(bf16[2,1,2,2,1,32,1024]{6,5,4,3,2,1,0:T(8,128)(2,1)S(1)} %constant_dynamic-slice_fusion.19), channel_id=1, source_target_pairs={{0,8},{4,12},{8,0},{12,4},{16,24},{20,28},{24,16},{28,20},{1,9},{5... | collective-permute-start | bytes 1572872 | tf_op jit(solution)/shard_map/ppermute | solution.py:200
  728.9 13.6 %collective-permute-start.82 = (bf16[1,1,1,1,1,32,1024]{6,5,4,3,2,1,0:T(8,128)(2,1)S(1)}, bf16[1,1,1,1,1,32,1024]{6,5,4,3,2,1,0:T(8,128)(2,1)S(1)}, u32[]{:S(2)}, u32[]{:S(2)}) collective-permute-start(bf16[1,1,1,1,1,32,1024]{6,5,4,3,2,1,0:T(8,128)(2,1)S(1)} %constant_dynamic-slice_fusion.10), channel_id=1, source_target_pairs={{0,16},{4,20},{8,24},{12,28},{16,0},{20,4},{24,8},{28,12},{1,17},{... | collective-permute-start | bytes 196616 | tf_op jit(solution)/shard_map/ppermute | solution.py:200
  750.5 13.1 %collective-permute-start.58 = (bf16[2,2,2,1,1,32,1024]{6,5,4,3,2,1,0:T(8,128)(2,1)S(1)}, bf16[2,2,2,1,1,32,1024]{6,5,4,3,2,1,0:T(8,128)(2,1)S(1)}, u32[]{:S(2)}, u32[]{:S(2)}) collective-permute-start(bf16[2,2,2,1,1,32,1024]{6,5,4,3,2,1,0:T(8,128)(2,1)S(1)} %constant_dynamic-slice_fusion.29), channel_id=1, source_target_pairs={{0,2},{1,3},{2,0},{3,1},{4,6},{5,7},{6,4},{7,5},{8,10},{9,11},{10,... | collective-permute-start | bytes 1572872 | tf_op jit(solution)/shard_map/ppermute | solution.py:200
  752.9 16.4 %collective-permute-start.73 = (bf16[2,1,2,1,1,32,1024]{6,5,4,3,2,1,0:T(8,128)(2,1)S(1)}, bf16[2,1,2,1,1,32,1024]{6,5,4,3,2,1,0:T(8,128)(2,1)S(1)}, u32[]{:S(2)}, u32[]{:S(2)}) collective-permute-start(bf16[2,1,2,1,1,32,1024]{6,5,4,3,2,1,0:T(8,128)(2,1)S(1)} %constant_dynamic-slice_fusion.18), channel_id=1, source_target_pairs={{0,2},{1,3},{2,0},{3,1},{4,6},{5,7},{6,4},{7,5},{8,10},{9,11},{10,... | collective-permute-start | bytes 786440 | tf_op jit(solution)/shard_map/ppermute | solution.py:200
  756.2 18.7 %collective-permute-start.66 = (bf16[2,2,1,1,1,32,1024]{6,5,4,3,2,1,0:T(8,128)(2,1)S(1)}, bf16[2,2,1,1,1,32,1024]{6,5,4,3,2,1,0:T(8,128)(2,1)S(1)}, u32[]{:S(2)}, u32[]{:S(2)}) collective-permute-start(bf16[2,2,1,1,1,32,1024]{6,5,4,3,2,1,0:T(8,128)(2,1)S(1)} %constant_dynamic-slice_fusion.23), channel_id=1, source_target_pairs={{0,2},{1,3},{2,0},{3,1},{4,6},{5,7},{6,4},{7,5},{8,10},{9,11},{10,... | collective-permute-start | bytes 786440 | tf_op jit(solution)/shard_map/ppermute | solution.py:200
  763.9 16.5 %collective-permute-start.59 = (bf16[2,2,1,1,1,32,1024]{6,5,4,3,2,1,0:T(8,128)(2,1)S(1)}, bf16[2,2,1,1,1,32,1024]{6,5,4,3,2,1,0:T(8,128)(2,1)S(1)}, u32[]{:S(2)}, u32[]{:S(2)}) collective-permute-start(bf16[2,2,1,1,1,32,1024]{6,5,4,3,2,1,0:T(8,128)(2,1)S(1)} %constant_dynamic-slice_fusion.28), channel_id=1, source_target_pairs={{0,4},{4,0},{8,12},{12,8},{16,20},{20,16},{24,28},{28,24},{1,5},{5... | collective-permute-start | bytes 786440 | tf_op jit(solution)/shard_map/ppermute | solution.py:200
  769.4 12.6 %collective-permute-start.74 = (bf16[2,1,1,1,1,32,1024]{6,5,4,3,2,1,0:T(8,128)(2,1)S(1)}, bf16[2,1,1,1,1,32,1024]{6,5,4,3,2,1,0:T(8,128)(2,1)S(1)}, u32[]{:S(2)}, u32[]{:S(2)}) collective-permute-start(bf16[2,1,1,1,1,32,1024]{6,5,4,3,2,1,0:T(8,128)(2,1)S(1)} %constant_dynamic-slice_fusion.17), channel_id=1, source_target_pairs={{0,4},{4,0},{8,12},{12,8},{16,20},{20,16},{24,28},{28,24},{1,5},{5... | collective-permute-start | bytes 393224 | tf_op jit(solution)/shard_map/ppermute | solution.py:200
  779.0 46.0 %collective-permute-start.86 = (bf16[2,2,2,1,1,32,4096]{6,5,4,3,2,1,0:T(8,128)(2,1)S(1)}, bf16[2,2,2,1,1,32,4096]{6,5,4,3,2,1,0:T(8,128)(2,1)S(1)}, u32[]{:S(2)}, u32[]{:S(2)}) collective-permute-start(bf16[2,2,2,1,1,32,4096]{6,5,4,3,2,1,0:T(8,128)(2,1)S(1)} %constant_dynamic-slice_fusion.8), channel_id=1, source_target_pairs={{0,2},{1,3},{2,0},{3,1},{4,6},{5,7},{6,4},{7,5},{8,10},{9,11},{10,... | collective-permute-start | bytes 6291464 | tf_op jit(solution)/shard_map/ppermute | solution.py:200
  789.4 42.9 %collective-permute-start.76 = (bf16[1,1,1,1,1,32,1024]{6,5,4,3,2,1,0:T(8,128)(2,1)S(1)}, bf16[1,1,1,1,1,32,1024]{6,5,4,3,2,1,0:T(8,128)(2,1)S(1)}, u32[]{:S(2)}, u32[]{:S(2)}) collective-permute-start(bf16[1,1,1,1,1,32,1024]{6,5,4,3,2,1,0:T(8,128)(2,1)S(1)} %add_convert_fusion.32), channel_id=1, source_target_pairs={{0,2},{1,3},{2,0},{3,1},{4,6},{5,7},{6,4},{7,5},{8,10},{9,11},{10,... | collective-permute-start | bytes 196616 | tf_op jit(solution)/shard_map/ppermute | solution.py:200
  789.9 46.8 %collective-permute-start.69 = (bf16[1,1,1,1,1,32,1024]{6,5,4,3,2,1,0:T(8,128)(2,1)S(1)}, bf16[1,1,1,1,1,32,1024]{6,5,4,3,2,1,0:T(8,128)(2,1)S(1)}, u32[]{:S(2)}, u32[]{:S(2)}) collective-permute-start(bf16[1,1,1,1,1,32,1024]{6,5,4,3,2,1,0:T(8,128)(2,1)S(1)} %add_convert_fusion.33), channel_id=1, source_target_pairs={{0,2},{1,3},{2,0},{3,1},{4,6},{5,7},{6,4},{7,5},{8,10},{9,11},{10,... | collective-permute-start | bytes 196616 | tf_op jit(solution)/shard_map/ppermute | solution.py:200
  792.1 44.8 %collective-permute-start.62 = (bf16[1,1,1,1,1,32,1024]{6,5,4,3,2,1,0:T(8,128)(2,1)S(1)}, bf16[1,1,1,1,1,32,1024]{6,5,4,3,2,1,0:T(8,128)(2,1)S(1)}, u32[]{:S(2)}, u32[]{:S(2)}) collective-permute-start(bf16[1,1,1,1,1,32,1024]{6,5,4,3,2,1,0:T(8,128)(2,1)S(1)} %add_convert_fusion.34), channel_id=1, source_target_pairs={{0,2},{1,3},{2,0},{3,1},{4,6},{5,7},{6,4},{7,5},{8,10},{9,11},{10,... | collective-permute-start | bytes 196616 | tf_op jit(solution)/shard_map/ppermute | solution.py:200
  825.9 20.9 %collective-permute-start.87 = (bf16[2,2,1,1,1,32,4096]{6,5,4,3,2,1,0:T(8,128)(2,1)S(1)}, bf16[2,2,1,1,1,32,4096]{6,5,4,3,2,1,0:T(8,128)(2,1)S(1)}, u32[]{:S(2)}, u32[]{:S(2)}) collective-permute-start(bf16[2,2,1,1,1,32,4096]{6,5,4,3,2,1,0:T(8,128)(2,1)S(1)} %constant_dynamic-slice_fusion.7), channel_id=1, source_target_pairs={{0,4},{4,0},{8,12},{12,8},{16,20},{20,16},{24,28},{28,24},{1,5},{5... | collective-permute-start | bytes 3145736 | tf_op jit(solution)/shard_map/ppermute | solution.py:200
  831.8 59.9 %collective-permute-start.93 = (bf16[2,2,1,2,1,128,1024]{6,5,4,3,2,1,0:T(8,128)(2,1)S(1)}, bf16[2,2,1,2,1,128,1024]{6,5,4,3,2,1,0:T(8,128)(2,1)S(1)}, u32[]{:S(2)}, u32[]{:S(2)}) collective-permute-start(bf16[2,2,1,2,1,128,1024]{6,5,4,3,2,1,0:T(8,128)(2,1)S(1)} %constant_dynamic-slice_fusion.3), channel_id=1, source_target_pairs={{0,4},{4,0},{8,12},{12,8},{16,20},{20,16},{24,28},{28,24},{1,5},{5... | collective-permute-start | bytes 6291464 | tf_op jit(solution)/shard_map/ppermute | solution.py:200
  847.1 46.9 %collective-permute-start.88 = (bf16[2,1,1,1,1,32,4096]{6,5,4,3,2,1,0:T(8,128)(2,1)S(1)}, bf16[2,1,1,1,1,32,4096]{6,5,4,3,2,1,0:T(8,128)(2,1)S(1)}, u32[]{:S(2)}, u32[]{:S(2)}) collective-permute-start(bf16[2,1,1,1,1,32,4096]{6,5,4,3,2,1,0:T(8,128)(2,1)S(1)} %constant_dynamic-slice_fusion.6), channel_id=1, source_target_pairs={{0,8},{4,12},{8,0},{12,4},{16,24},{20,28},{24,16},{28,20},{1,9},{5... | collective-permute-start | bytes 1572872 | tf_op jit(solution)/shard_map/ppermute | solution.py:200
  892.8 20.0 %collective-permute-start.94 = (bf16[2,2,1,1,1,128,1024]{6,5,4,3,2,1,0:T(8,128)(2,1)S(1)}, bf16[2,2,1,1,1,128,1024]{6,5,4,3,2,1,0:T(8,128)(2,1)S(1)}, u32[]{:S(2)}, u32[]{:S(2)}) collective-permute-start(bf16[2,2,1,1,1,128,1024]{6,5,4,3,2,1,0:T(8,128)(2,1)S(1)} %constant_dynamic-slice_fusion.2), channel_id=1, source_target_pairs={{0,2},{1,3},{2,0},{3,1},{4,6},{5,7},{6,4},{7,5},{8,10},{9,11},{10,... | collective-permute-start | bytes 3145736 | tf_op jit(solution)/shard_map/ppermute | solution.py:200
  894.2 19.1 %collective-permute-start.89 = (bf16[1,1,1,1,1,32,4096]{6,5,4,3,2,1,0:T(8,128)(2,1)S(1)}, bf16[1,1,1,1,1,32,4096]{6,5,4,3,2,1,0:T(8,128)(2,1)S(1)}, u32[]{:S(2)}, u32[]{:S(2)}) collective-permute-start(bf16[1,1,1,1,1,32,4096]{6,5,4,3,2,1,0:T(8,128)(2,1)S(1)} %constant_dynamic-slice_fusion.5), channel_id=1, source_target_pairs={{0,16},{4,20},{8,24},{12,28},{16,0},{20,4},{24,8},{28,12},{1,17},{... | collective-permute-start | bytes 786440 | tf_op jit(solution)/shard_map/ppermute | solution.py:200
  921.6 12.4 %collective-permute-start.96 = (bf16[1,1,1,1,1,128,1024]{6,5,4,3,2,1,0:T(8,128)(2,1)S(1)}, bf16[1,1,1,1,1,128,1024]{6,5,4,3,2,1,0:T(8,128)(2,1)S(1)}, u32[]{:S(2)}, u32[]{:S(2)}) collective-permute-start(bf16[1,1,1,1,1,128,1024]{6,5,4,3,2,1,0:T(8,128)(2,1)S(1)} %constant_dynamic-slice_fusion), channel_id=1, source_target_pairs={{0,16},{4,20},{8,24},{12,28},{16,0},{20,4},{24,8},{28,12},{1,17},{... | collective-permute-start | bytes 786440 | tf_op jit(solution)/shard_map/ppermute | solution.py:200
  922.5 24.7 %collective-permute-start.91 = (bf16[1,1,1,2,1,32,4096]{6,5,4,3,2,1,0:T(8,128)(2,1)S(1)}, bf16[1,1,1,2,1,32,4096]{6,5,4,3,2,1,0:T(8,128)(2,1)S(1)}, u32[]{:S(2)}, u32[]{:S(2)}) collective-permute-start(bf16[1,1,1,2,1,32,4096]{6,5,4,3,2,1,0:T(8,128)(2,1)S(1)} %maximum_select_fusion.34), channel_id=1, source_target_pairs={{0,1},{1,0},{2,3},{3,2},{4,5},{5,4},{6,7},{7,6},{8,9},{9,8},{10,11... | collective-permute-start | bytes 1572872 | tf_op jit(solution)/shard_map/ppermute | solution.py:200
  (104 other events, 1000.7 us)
where the time goes:
time: 959 us; the launch traced here: 951 us
  waiting for transfers between devices  243 us (25%)
  Pallas kernels  195 us (20%)
  starting transfers between devices  160 us (17%)
  matrix products  139 us (14%)
  other arithmetic  82.8 us (9%)
  blocking collectives  67 us (7%)
  local copies, waits for them, and re-layouts  60.1 us (6%)
    ppermute x99, waiting for transfers between devices, swap(): lax.ppermute(array, name, [(i, i ^ mask) for i in range(lax.axis_size(nam...  243 us
    ppermute x99, starting transfers between devices, swap(): lax.ppermute(array, name, [(i, i ^ mask) for i in range(lax.axis_size(nam...  160 us
    pallas_call x2, Pallas kernels, attend_backward(): pl.pallas_call(functools.partial(backward_kernel, chunk=chunk), grid=(len...  118 us
    pallas_call x2, Pallas kernels, attend_forward(): pl.pallas_call(forward_kernel, grid=(length // rows,), in_specs=[tile, wh...  77.4 us
    dot_general x6, matrix products, matmul_right(): lax.dot_general(left, right, (((1,), (1,)), ((), ())), preferred_element_...  52.6 us
    dot_general x6, matrix products, matmul(): return jnp.dot(left, right, preferred_element_type=F32)  51.8 us
    psum x1, blocking collectives, local(): lax.psum(rows, ('dp', 'seq'))  42.3 us
    dot_general x6, matrix products, matmul_left(): lax.dot_general(left, right, (((0,), (0,)), ((), ())), preferred_element_...  34.6 us
  transfers between devices with their start and end apart: 99, of which 32 were waited for; matrix products, arithmetic and copies ran while one was open for 20% of the time, Pallas kernels for 21%

commit v1 on v0

--- a/solution.py
+++ b/solution.py
@@ -64,30 +64,429 @@
     va_ref[:, LANES:] = jnp.where(lane < 3, 1.0, 0.0).astype(LOW)
 
 
-def forward_kernel(q_ref, k_ref, v_ref, bias_ref, o_ref, qx_ref, ka_ref, va_ref):
-    @pl.when(pl.program_id(0) == 0)
-    def _():
-        fill_keys(k_ref, v_ref, bias_ref, ka_ref, va_ref)
-
-    rows = q_ref.shape[0]
-    lane = lax.broadcasted_iota(jnp.int32, (rows, LANES), 1)
-    queries = q_ref[...].astype(F32) * SCALE
-    ones = jnp.where(lane < 3, 1.0, 0.0)
-    outs = []
-    for head in range(2):
-        masked = jnp.where(head_mask(rows, head), queries, 0.0)
-        wide = jnp.concatenate([masked, ones], 1).astype(LOW)
-        scores = matmul_right(wide, ka_ref[...])
-        row_max = jnp.max(scores, -1, keepdims=True)
-        expo = jnp.exp(scores - row_max).astype(LOW)
-        both = matmul(expo, va_ref[...])
-        total = both[:, LANES : LANES + 1]
-        outs.append(both[:, :LANES] / total)
-        first, second, third = thirds(row_max + jnp.log(total))
-        qx_ref[head] = jnp.where(
-            lane == 3, -first, jnp.where(lane == 4, -second, jnp.where(lane == 5, -third, ones))
-        ).astype(LOW)
-    o_ref[...] = jnp.where(head_mask(rows, 0), outs[0], outs[1]).astype(LOW)
+def send_to(src, dst, send_sem, recv_sem, dp, seq):
+    return pltpu.make_async_remote_copy(
+        src_ref=src, dst_ref=dst, send_sem=send_sem, recv_sem=recv_sem,
+        device_id=(dp, seq), device_id_type=pl.DeviceIdType.MESH,
+    )
+
+
+class Peers:
+    def __init__(self, n, g):
+        self.n, self.g, self.nz, self.ny = n, g, n // 2, g // 2
+        self.d = lax.axis_index("dp")
+        self.s = lax.axis_index("seq")
+        self.z, self.x = self.d // 2, lax.rem(self.d, 2)
+        self.y, self.c = self.s // 2, lax.rem(self.s, 2)
+        self.xpeer = self.z * 2 + 1 - self.x
+        self.cpeer = self.y * 2 + 1 - self.c
+
+    def z_to(self, k):
+        return lax.rem(self.z + k, self.nz) * 2 + self.x
+
+    def z_from(self, k):
+        return lax.rem(self.z + self.nz - k, self.nz) * 2 + self.x
+
+    def side(self, dp):
+        return (dp // 2) * 2 + 1 - self.x
+
+    def y_to(self, k):
+        return lax.rem(self.s + 2 * k, self.g)
+
+    def y_from(self, k):
+        return lax.rem(self.s + self.g - 2 * k, self.g)
+
+    def s_to(self, k):
+        return lax.rem(self.s + k, self.g)
+
+    def s_from(self, k):
+        return lax.rem(self.s + self.g - k, self.g)
+
+    def barrier(self):
+        sem = pltpu.get_barrier_semaphore()
+        targets = [(self.z_to(k), self.s) for k in range(1, self.nz)]
+        targets.append((self.xpeer, self.s))
+        targets += [(self.d, self.s_to(k)) for k in range(1, self.g)]
+        for target in targets:
+            pl.semaphore_signal(
+                sem, inc=1, device_id=target, device_id_type=pl.DeviceIdType.MESH
+            )
+        pl.semaphore_wait(sem, len(targets))
+
+
+def pieces_of(half):
+    return 2 if half % 64 == 0 and half >= 64 else 1
+
+
+def weight_pieces(shapes):
+    out = []
+    for index, rows in enumerate(shapes):
+        half = rows // 2
+        count = pieces_of(half) if index else 1
+        for part in range(count):
+            out.append((index, part * (half // count), half // count))
+    return out
+
+
+def forward_kernel(
+    hid_ref, wch_ref, kb_ref, wo_ref, wu_ref, wd_ref,
+    ctx_out, own_ctx, q_out, k_out, v_out, qx_out, hid_out, wq_out, vec_out, wo_out, wu_out, wd_out,
+    hid, wch, wq, kb, q_s, k_s, v_s, ka, va, ctx, qx,
+    loc, hy, hc, hf, kbs, wz, wx, pz, px, pc, cs, kx,
+    *, n, g, rows,
+):
+    me = Peers(n, g)
+    d, s, nz, ny = me.d, me.s, me.nz, me.ny
+    tok, width = hid_ref.shape
+    length = tok * g
+    deep = width // n
+    gw = width // g
+    pairs = gw // LANES
+    cut = tok // 3
+    shards = (wo_ref, wu_ref, wd_ref)
+    fulls = (wo_out, wu_out, wd_out)
+    pieces = weight_pieces([ref.shape[0] for ref in shards])
+    me.barrier()
+
+    local = [
+        pltpu.make_async_copy(hid_ref, hid.at[s], loc.at[0]),
+        pltpu.make_async_copy(wch_ref, wch.at[d], loc.at[1]),
+        pltpu.make_async_copy(kb_ref, kb.at[s], loc.at[2]),
+    ]
+    keep = [
+        pltpu.make_async_copy(shards[i], fulls[i].at[d], loc.at[3 + i]) for i in range(3)
+    ]
+
+    def y_copy(k, part, slot):
+        span = pl.ds(part * cut, cut)
+        return send_to(
+            hid_ref.at[span], hid.at[slot, span], hy.at[0, k, part], hy.at[1, k, part], d,
+            me.y_to(k),
+        )
+
+    def c_copy(slot):
+        return send_to(hid_ref, hid.at[slot], hc.at[0], hc.at[1], d, me.cpeer)
+
+    def f_copy(k, part, slot):
+        span = pl.ds(part * cut, cut)
+        return send_to(
+            hid.at[slot, span], hid.at[slot, span], hf.at[0, k, part], hf.at[1, k, part], d,
+            me.cpeer,
+        )
+
+    def kb_copy(k, slot):
+        return send_to(kb_ref, kb.at[slot], kbs.at[0, k], kbs.at[1, k], d, me.s_to(k))
+
+    def wz_copy(k, slot):
+        return send_to(wch_ref, wch.at[slot], wz.at[0, k], wz.at[1, k], me.z_to(k), s)
+
+    def wx_copy(k, src, slot):
+        return send_to(src, wch.at[slot], wx.at[0, k], wx.at[1, k], me.xpeer, s)
+
+    def c_of_y(k):
+        return me.y_from(k) // 2 * 2 + 1 - me.c
+
+    for copy in local:
+        copy.start()
+    for k in range(1, nz):
+        wz_copy(k, d).start()
+    wx_copy(0, wch_ref, d).start()
+    for k in range(1, g):
+        kb_copy(k, s).start()
+    for part in range(3):
+        for k in range(1, ny):
+            y_copy(k, part, s).start()
+    c_copy(s).start()
+    for copy in keep:
+        copy.start()
+
+    def span_of(p):
+        index, off, size = pieces[p]
+        return index, pl.ds(pl.multiple_of(me.c * (shards[index].shape[0] // 2) + off, 16), size)
+
+    def other_span(p):
+        index, off, size = pieces[p]
+        return index, pl.ds(
+            pl.multiple_of((1 - me.c) * (shards[index].shape[0] // 2) + off, 16), size
+        )
+
+    def pz_copy(p, k, slot):
+        index, span = span_of(p)
+        return send_to(
+            shards[index].at[span], fulls[index].at[slot, span], pz.at[0, p, k], pz.at[1, p, k],
+            me.z_to(k), s,
+        )
+
+    def px_copy(p, k, slot):
+        index, span = span_of(p)
+        src = shards[index].at[span] if k == 0 else fulls[index].at[slot, span]
+        return send_to(
+            src, fulls[index].at[slot, span], px.at[0, p, k], px.at[1, p, k], me.xpeer, s
+        )
+
+    def pc_copy(p, k, side, slot, mine):
+        index, span = span_of(p) if mine else other_span(p)
+        return send_to(
+            fulls[index].at[slot, span], fulls[index].at[slot, span], pc.at[0, p, k, side],
+            pc.at[1, p, k, side], d, me.cpeer,
+        )
+
+    def piece_send(p):
+        for k in range(1, nz):
+            pz_copy(p, k, d).start()
+        px_copy(p, 0, d).start()
+
+    def piece_pass(p):
+        for k in range(1, nz):
+            slot = me.z_from(k)
+            pz_copy(p, k, slot).wait_recv()
+            px_copy(p, k, slot).start()
+            pc_copy(p, k, 0, slot, True).start()
+
+    def piece_share(p):
+        for k in range(nz):
+            slot = me.side(me.z_from(k)) if k else me.xpeer
+            px_copy(p, k, slot).wait_recv()
+            pc_copy(p, k, 1, slot, True).start()
+
+    def piece_end(p):
+        for k in range(1, nz):
+            pc_copy(p, k, 0, me.z_from(k), False).wait_recv()
+        for k in range(nz):
+            pc_copy(p, k, 1, me.side(me.z_from(k)) if k else me.xpeer, False).wait_recv()
+        for k in range(1, nz):
+            pz_copy(p, k, d).wait_send()
+            pc_copy(p, k, 0, me.z_from(k), True).wait_send()
+        for k in range(nz):
+            px_copy(p, k, me.z_from(k) if k else d).wait_send()
+            pc_copy(p, k, 1, me.side(me.z_from(k)) if k else me.xpeer, True).wait_send()
+
+    for k in range(1, nz):
+        slot = me.z_from(k)
+        wz_copy(k, slot).wait_recv()
+        wx_copy(k, wch.at[slot], slot).start()
+    for k in range(nz):
+        slot = me.side(me.z_from(k)) if k else me.xpeer
+        wx_copy(k, wch_ref, slot).wait_recv()
+    for copy in local:
+        copy.wait()
+    piece_send(0)
+    if len(pieces) > 1:
+        piece_send(1)
+    for j in range(n):
+        wq[j * deep : (j + 1) * deep, :] = wch[j, :deep, :]
+    bias_row = jnp.sum(wch[:, deep : deep + 16, :].astype(F32)[:, 0:1, :], 0)
+    saves = [
+        pltpu.make_async_copy(wq, wq_out, loc.at[6]),
+        pltpu.make_async_copy(wch.at[:, pl.ds(deep, 16)], vec_out, loc.at[7]),
+    ]
+    for copy in saves:
+        copy.start()
+
+    tiles = tok // cut
+
+    def project(step, carry):
+        rel = step // tiles
+        part = lax.rem(step, tiles)
+
+        @pl.when(step == tiles)
+        def _():
+            c_copy(me.cpeer).wait_recv()
+
+        for k in range(1, ny):
+            @pl.when(step == 2 * k * tiles)
+            def _(k=k):
+                for sub in range(3):
+                    y_copy(k, sub, me.y_from(k)).wait_recv()
+                    f_copy(k, sub, me.y_from(k)).start()
+
+            @pl.when(step == (2 * k + 1) * tiles)
+            def _(k=k):
+                for sub in range(3):
+                    f_copy(k, sub, c_of_y(k)).wait_recv()
+
+        y_at = lax.rem(me.y + ny - rel // 2, ny)
+        c_at = lax.rem(me.c + rel, 2)
+        slot = y_at * 2 + c_at
+        got = matmul(hid[slot, pl.ds(part * cut, cut), :], wq[...]) + bias_row
+        got = got.astype(LOW)
+        span = pl.ds(pl.multiple_of(slot * tok + part * cut, cut), cut)
+        for index, ref in enumerate((q_s, k_s, v_s)):
+            for pair in range(pairs):
+                at = index * gw + pair * LANES
+                ref[pair, span, :] = got[:, at : at + LANES]
+        return carry
+
+    lax.fori_loop(0, g * tiles, project, 0)
+    for k in range(1, g):
+        kb_copy(k, me.s_from(k)).wait_recv()
+    more = [
+        pltpu.make_async_copy(hid, hid_out, loc.at[8]),
+        pltpu.make_async_copy(q_s, q_out, loc.at[9]),
+        pltpu.make_async_copy(k_s, k_out, loc.at[10]),
+        pltpu.make_async_copy(v_s, v_out, loc.at[11]),
+    ]
+    for copy in more:
+        copy.start()
+    saves += more
+
+    blocks = length // rows
+    per = tok // rows
+    steps = pairs * blocks
+
+    def ctx_copy(pair, k, source):
+        span = pl.ds(pl.multiple_of(me.s_to(k) * tok, tok), tok)
+        return send_to(
+            ctx.at[pair, span],
+            ctx_out.at[:, pl.ds(pl.multiple_of(source * gw + pair * LANES, LANES), LANES)],
+            cs.at[0, pair, k], cs.at[1, pair, k], d, me.s_to(k),
+        )
+
+    def ctx_keep(pair):
+        return pltpu.make_async_copy(
+            ctx.at[pair, pl.ds(pl.multiple_of(s * tok, tok), tok)],
+            ctx_out.at[:, pl.ds(pl.multiple_of(s * gw + pair * LANES, LANES), LANES)],
+            kx.at[pair],
+        )
+
+    events = {}
+    every = max(1, steps // (len(pieces) + 1))
+    for p in range(len(pieces)):
+        if p >= 2:
+            events.setdefault((p - 2) * every, []).append(lambda p=p: piece_send(p))
+        events.setdefault((p + 1) * every - 1, []).append(lambda p=p: piece_pass(p))
+        events.setdefault((p + 1) * every + 1, []).append(lambda p=p: piece_share(p))
+    late = [e for t in sorted(events) if t >= steps for e in events[t]]
+
+    def attend(step, carry):
+        pair = step // blocks
+        turn = lax.rem(step, blocks)
+        k_own = lax.rem(1 + turn // per, g)
+        owner = lax.rem(s + k_own, g)
+        block = owner * per + lax.rem(turn, per)
+        for t in sorted(events):
+            if t < steps:
+                @pl.when(step == t)
+                def _(t=t):
+                    for event in events[t]:
+                        event()
+
+        @pl.when(turn == 0)
+        def _():
+            lane = lax.broadcasted_iota(jnp.int32, (tok, LANES), 1)
+            for j in range(g):
+                span = slice(j * tok, (j + 1) * tok)
+                column = jnp.broadcast_to(kb[j, 0:1, :], (LANES, tok)).T
+                first, second, third = thirds(column)
+                extra = jnp.where(
+                    lane == 0, first,
+                    jnp.where(lane == 1, second, jnp.where(lane == 2, third, 1.0)),
+                )
+                ka[span, :LANES] = k_s[pair, span, :]
+                ka[span, LANES:] = jnp.where(lane < 6, extra, 0.0).astype(LOW)
+                va[span, :LANES] = v_s[pair, span, :]
+                va[span, LANES:] = jnp.where(lane < 3, 1.0, 0.0).astype(LOW)
+
+        span = pl.ds(pl.multiple_of(block * rows, rows), rows)
+        lane = lax.broadcasted_iota(jnp.int32, (rows, LANES), 1)
+        queries = q_s[pair, span, :].astype(F32) * SCALE
+        ones = jnp.where(lane < 3, 1.0, 0.0)
+        outs = []
+        for head in range(2):
+            masked = jnp.where(head_mask(rows, head), queries, 0.0)
+            wide = jnp.concatenate([masked, ones], 1).astype(LOW)
+            scores = matmul_right(wide, ka[...])
+            row_max = jnp.max(scores, -1, keepdims=True)
+            expo = jnp.exp(scores - row_max).astype(LOW)
+            both = matmul(expo, va[...])
+            total = both[:, LANES : LANES + 1]
+            outs.append(both[:, :LANES] / total)
+            first, second, third = thirds(row_max + jnp.log(total))
+            qx[pair, head, span, :] = jnp.where(
+                lane == 3, -first,
+                jnp.where(lane == 4, -second, jnp.where(lane == 5, -third, ones)),
+            ).astype(LOW)
+        ctx[pair, span, :] = jnp.where(head_mask(rows, 0), outs[0], outs[1]).astype(LOW)
+
+        for p in range(pairs):
+            for k in range(1, g):
+                @pl.when(step == p * blocks + k * per - 1)
+                def _(p=p, k=k):
+                    ctx_copy(p, k, s).start()
+
+            @pl.when(step == (p + 1) * blocks - 1)
+            def _(p=p):
+                ctx_keep(p).start()
+        return carry
+
+    lax.fori_loop(0, steps, attend, 0)
+    last = [
+        pltpu.make_async_copy(qx, qx_out, loc.at[12]),
+        pltpu.make_async_copy(ctx, own_ctx, loc.at[13]),
+    ]
+    for copy in last:
+        copy.start()
+    for event in late:
+        event()
+    for k in range(1, g):
+        kb_copy(k, s).wait_send()
+    for k in range(1, ny):
+        for part in range(3):
+            y_copy(k, part, s).wait_send()
+            f_copy(k, part, me.y_from(k)).wait_send()
+    c_copy(s).wait_send()
+    for k in range(1, nz):
+        wz_copy(k, d).wait_send()
+        slot = me.z_from(k)
+        wx_copy(k, wch.at[slot], slot).wait_send()
+    wx_copy(0, wch_ref, d).wait_send()
+    for pair in range(pairs):
+        ctx_keep(pair).wait()
+        for k in range(1, g):
+            ctx_copy(pair, k, me.s_from(k)).wait_recv()
+            ctx_copy(pair, k, s).wait_send()
+    for p in range(len(pieces)):
+        piece_end(p)
+    for copy in saves + last + keep:
+        copy.wait()
+
+
+def attend_forward(hidden, chunk, bias_rows, w_out, w_up, w_down):
+    n, g = lax.axis_size("dp"), lax.axis_size("seq")
+    tok, width = hidden.shape
+    length, gw, deep = tok * g, width // g, width // n
+    pairs = gw // LANES
+    count = len(weight_pieces([w.shape[0] for w in (w_out, w_up, w_down)]))
+    anyw = pl.BlockSpec(memory_space=pl.ANY)
+    low = lambda *shape: jax.ShapeDtypeStruct(shape, LOW)
+    out_shape = [
+        low(tok, width), low(pairs, length, LANES), low(pairs, length, LANES),
+        low(pairs, length, LANES), low(pairs, length, LANES), low(pairs, 2, length, LANES),
+        low(g, tok, width), low(width, 3 * gw), low(n, 16, 3 * gw),
+        low(n, *w_out.shape), low(n, *w_up.shape), low(n, *w_down.shape),
+    ]
+    dma = lambda *shape: pltpu.SemaphoreType.DMA(shape)
+    nz, ny = n // 2, max(g // 2, 2)
+    vmem = lambda shape, kind=LOW: pltpu.VMEM(shape, kind)
+    return pl.pallas_call(
+        functools.partial(forward_kernel, n=n, g=g, rows=256),
+        in_specs=[anyw] * 6,
+        out_specs=[anyw] * 12,
+        out_shape=out_shape,
+        scratch_shapes=[
+            vmem((g, tok, width)), vmem((n, deep + 16, 3 * gw)), vmem((width, 3 * gw)),
+            vmem((g, 8, tok), F32), vmem((pairs, length, LANES)), vmem((pairs, length, LANES)),
+            vmem((pairs, length, LANES)), vmem((length, 2 * LANES)), vmem((length, 2 * LANES)),
+            vmem((pairs, length, LANES)), vmem((pairs, 2, length, LANES)),
+            dma(14), dma(2, ny, 3), dma(2), dma(2, ny, 3), dma(2, g), dma(2, nz), dma(2, nz),
+            dma(2, count, nz), dma(2, count, nz), dma(2, count, nz, 2), dma(2, pairs, g),
+            dma(pairs),
+        ],
+        compiler_params=pltpu.CompilerParams(
+            vmem_limit_bytes=56 * 2**20, collective_id=0, has_side_effects=True
+        ),
+        cost_estimate=cost(length, 4),
+    )(hidden, chunk, bias_rows, w_out, w_up, w_down)
 
 
 def backward_kernel(
@@ -154,26 +553,6 @@
     )
 
 
-def attend_forward(queries, keys, values, bias_wide):
-    length = queries.shape[0]
-    rows = 256
-    tile = pl.BlockSpec((rows, LANES), lambda i: (i, 0))
-    whole = pl.BlockSpec((length, LANES), lambda i: (0, 0))
-    return pl.pallas_call(
-        forward_kernel,
-        grid=(length // rows,),
-        in_specs=[tile, whole, whole, whole],
-        out_specs=[tile, pl.BlockSpec((2, rows, LANES), lambda i: (0, i, 0))],
-        out_shape=[
-            jax.ShapeDtypeStruct((length, LANES), LOW),
-            jax.ShapeDtypeStruct((2, length, LANES), LOW),
-        ],
-        scratch_shapes=[pltpu.VMEM((length, 2 * LANES), LOW)] * 2,
-        compiler_params=pltpu.CompilerParams(vmem_limit_bytes=48 * 2**20),
-        cost_estimate=cost(length, 2),
-    )(queries, keys, values, bias_wide)
-
-
 def attend_backward(queries, keys, values, bias_wide, q_extra, context, context_grad):
     length = queries.shape[0]
     rows = 256
@@ -232,15 +611,6 @@
     )
 
 
-def gather_weight(shard, last):
-    rows = shard.shape[0] // lax.axis_size("seq")
-    own = lax.dynamic_slice_in_dim(shard, lax.axis_index("seq") * rows, rows, 0)
-    own = own.reshape((1,) * (bits("dp") + bits("seq")) + own.shape)
-    for name, k in bit_order(last):
-        own = double(own, name, k)
-    return own.reshape(-1, shard.shape[1])
-
-
 def reduce_weight(grad, last):
     count = bits("dp") + bits("seq")
     rows = grad.shape[0] >> count
@@ -255,6 +625,31 @@
     return part.reshape(-1, grad.shape[1]).astype(F32)
 
 
+def scatter(part, name, order):
+    tail = part.shape[1:]
+    part = part.reshape((2,) * bits(name) + tail)
+    for k in order:
+        at = bits(name) - 1 - k
+        mine = my_bit(name, k)
+        away = lax.dynamic_index_in_dim(part, 1 - mine, at)
+        keep = lax.dynamic_index_in_dim(part, mine, at)
+        part = keep.astype(F32) + swap(away.astype(LOW), name, 1 << k).astype(F32)
+    return part.reshape(tail)
+
+
+def gather_seq(part):
+    part = part.reshape((1,) * bits("seq") + part.shape)
+    for k in reversed(range(bits("seq"))):
+        other = swap(part, "seq", 1 << k)
+        at = bits("seq") - 1 - k
+        part = jnp.where(
+            my_bit("seq", k) == 0,
+            jnp.concatenate([part, other], at),
+            jnp.concatenate([other, part], at),
+        )
+    return part.reshape((-1,) + part.shape[bits("seq"):])
+
+
 def exchange(blocks):
     return [block if t == 0 else swap(block, "seq", t) for t, block in enumerate(blocks)]
 
@@ -267,6 +662,12 @@
 
 def columns(array, group, pair, group_width):
     return lax.dynamic_slice_in_dim(array, group * group_width + pair * LANES, LANES, 1)
+
+
+def own_columns(piece, width, group_width):
+    at = lax.axis_index("dp") * piece.shape[0]
+    row = lax.dynamic_update_slice_in_dim(jnp.zeros((width,), LOW), piece, at, 0)
+    return lax.dynamic_slice_in_dim(row, lax.axis_index("seq") * group_width, group_width, 0)
 
 
 def local(
@@ -279,49 +680,39 @@
     group_width = width // groups
     pairs = group_width // LANES
     wide_y, wide_x, wide_z = ("seq", 1), ("dp", 0), ("dp", 1)
-
-    w_q = gather_weight(w_qkv[:, :width], wide_y)
-    w_k = gather_weight(w_qkv[:, width : 2 * width], wide_x)
-    w_v = gather_weight(w_qkv[:, 2 * width :], wide_z)
+    deep = w_qkv.shape[0]
+
     vectors = (
         bias_q, bias_v, bias_out, gain_attn, shift_attn, bias_down, gain_ffn, shift_ffn, bias_up,
     )
-    packed = lax.all_gather(jnp.concatenate(vectors), "dp", axis=0).astype(F32)
+    packed = jnp.concatenate(vectors)
+    fill = -packed.shape[0] % (3 * group_width)
+    packed = jnp.pad(packed, (0, fill)).reshape(-1, 3 * group_width)
+    first_row = jnp.concatenate([
+        own_columns(bias_q, width, group_width), jnp.zeros((group_width,), LOW),
+        own_columns(bias_v, width, group_width),
+    ])[None]
+    own_w = jnp.concatenate(
+        [lax.dynamic_slice_in_dim(w_qkv, i * width + me * group_width, group_width, 1) for i in range(3)], 1
+    )
+    blank = jnp.zeros((16 - 1 - packed.shape[0], 3 * group_width), LOW)
+    chunk = jnp.concatenate([own_w, first_row, packed, blank], 0)
+    bias_rows = jnp.broadcast_to(key_bias, (8, tok_rows))
+    (context, own_context, q_all, k_all, v_all, q_extra, hidden_all, w_heads, vec_all, f_w_out,
+     f_w_up, f_w_down) = attend_forward(hidden_in, chunk, bias_rows, w_out, w_up, w_down)
+    f_w_out = f_w_out.reshape(-1, w_out.shape[1])
+    f_w_up = f_w_up.reshape(-1, w_up.shape[1])
+    f_w_down = f_w_down.reshape(-1, w_down.shape[1])
+    hidden_all = hidden_all.reshape(-1, width)
+    packed = vec_all[:, 1 : 1 + packed.shape[0]].reshape(vec_all.shape[0], -1).astype(F32)
     fulls, at = [], 0
     for vector in vectors:
         fulls.append(packed[:, at : at + vector.shape[0]].reshape(-1))
         at += vector.shape[0]
     (f_bias_q, f_bias_v, f_bias_out, f_gain_attn, f_shift_attn, f_bias_down, f_gain_ffn,
      f_shift_ffn, f_bias_up) = fulls
-    f_w_out = gather_weight(w_out, wide_z)
-    f_w_up = gather_weight(w_up, wide_y)
-    f_w_down = gather_weight(w_down, wide_x)
-
-    q_rows = (matmul(hidden_in, w_q) + f_bias_q).astype(LOW)
-    k_rows = matmul(hidden_in, w_k).astype(LOW)
-    v_rows = (matmul(hidden_in, w_v) + f_bias_v).astype(LOW)
-    bias_col = jnp.concatenate(exchange([key_bias[0]] * groups))
+    bias_col = jnp.concatenate(by_index(exchange([key_bias[0]] * groups)))
     bias_wide = jnp.broadcast_to(bias_col[:, None], (bias_col.shape[0], LANES))
-    saved, context_parts = [], []
-    for pair in range(pairs):
-        got = exchange([
-            jnp.concatenate(
-                [columns(rows, me ^ t, pair, group_width) for rows in (q_rows, k_rows, v_rows)], 1
-            )
-            for t in range(groups)
-        ])
-        queries, keys, values = (
-            jnp.concatenate([block[:, i * LANES : (i + 1) * LANES] for block in got])
-            for i in range(3)
-        )
-        context, q_extra = attend_forward(queries, keys, values, bias_wide)
-        saved.append((queries, keys, values, bias_wide, q_extra, context))
-        context_parts.append(by_index(exchange(
-            [context[t * tok_rows : (t + 1) * tok_rows] for t in range(groups)]
-        )))
-    context = jnp.concatenate(
-        [context_parts[pair][j] for j in range(groups) for pair in range(pairs)], 1
-    )
 
     attended = hidden_in.astype(F32) + matmul(context, f_w_out) + f_bias_out
     normed = layer_norm(attended, f_gain_attn, f_shift_attn)
@@ -357,32 +748,31 @@
     s_w_up = reduce_weight(g_w_up, wide_y)
     s_w_out = reduce_weight(g_w_out, wide_z)
 
-    grad_parts = []
+    grads = [[], [], []]
     for pair in range(pairs):
-        got = jnp.concatenate(exchange(
+        got = jnp.concatenate(by_index(exchange(
             [columns(d_context, me ^ t, pair, group_width) for t in range(groups)]
-        ))
-        d_heads = jnp.concatenate(attend_backward(*saved[pair], got), 1)
-        grad_parts.append(by_index(exchange(
-            [d_heads[t * tok_rows : (t + 1) * tok_rows] for t in range(groups)]
         )))
-    d_q, d_k, d_v = (
-        jnp.concatenate(
-            [
-                grad_parts[pair][j][:, i * LANES : (i + 1) * LANES]
-                for j in range(groups)
-                for pair in range(pairs)
-            ],
-            1,
-        )
-        for i in range(3)
-    )
-    s_w_q = reduce_weight(matmul_left(hidden_in, d_q), wide_y)
-    s_w_k = reduce_weight(matmul_left(hidden_in, d_k), wide_x)
-    s_w_v = reduce_weight(matmul_left(hidden_in, d_v), wide_z)
-    g_bias_q = jnp.sum(d_q.astype(F32), 0)
-    g_bias_v = jnp.sum(d_v.astype(F32), 0)
-    grad_in = d_attended + matmul_right(d_q, w_q) + matmul_right(d_k, w_k) + matmul_right(d_v, w_v)
+        done = attend_backward(
+            q_all[pair], k_all[pair], v_all[pair], bias_wide, q_extra[pair], own_context[pair], got
+        )
+        for i in range(3):
+            grads[i].append(done[i])
+    d_heads = jnp.concatenate(grads[0] + grads[1] + grads[2], 1)
+    d_in = matmul_right(d_heads, w_heads).astype(LOW).reshape(groups, tok_rows, width)
+    grad_in = d_attended + scatter(d_in, "seq", range(bits("seq")))
+    g_w_heads = matmul_left(hidden_all, d_heads).astype(LOW)
+    s_w_heads = scatter(
+        g_w_heads.reshape(-1, deep, 3 * group_width), "dp", range(bits("dp"))
+    ).astype(LOW)
+    s_w_qkv = gather_seq(s_w_heads).reshape(groups, deep, 3, group_width)
+    s_w_qkv = s_w_qkv.transpose(1, 2, 0, 3).reshape(deep, -1).astype(F32)
+    head_sums = jnp.sum(d_heads.astype(F32), 0)
+    zero = jnp.zeros((width,), F32)
+    g_bias_q = lax.dynamic_update_slice_in_dim(zero, head_sums[:group_width], me * group_width, 0)
+    g_bias_v = lax.dynamic_update_slice_in_dim(
+        zero, head_sums[2 * group_width :], me * group_width, 0
+    )
 
     vector_grads = (
         g_bias_q, g_bias_v, g_bias_out, g_gain_attn, g_shift_attn, g_bias_down, g_gain_ffn,
@@ -400,7 +790,7 @@
     (s_bias_q, s_bias_v, s_bias_out, s_gain_attn, s_shift_attn, s_bias_down, s_gain_ffn,
      s_shift_ffn, s_bias_up) = sums
     return (
-        output, grad_in, jnp.concatenate([s_w_q, s_w_k, s_w_v], 1), s_bias_q, s_bias_v, s_w_out,
+        output, grad_in, s_w_qkv, s_bias_q, s_bias_v, s_w_out,
         s_bias_out, s_gain_attn, s_shift_attn, s_w_up, s_bias_up, s_w_down, s_bias_down,
         s_gain_ffn, s_shift_ffn,
     )

time: 959 us -> 768 us (0.80)
  waiting for transfers between devices: 243 us -> 131 us
  starting transfers between devices: 160 us -> 51.3 us
  Pallas kernels: 195 us -> 286 us
  other arithmetic: 82.8 us -> 51.4 us
  blocking collectives: 67 us -> 47.3 us
  matrix products: 139 us -> 124 us
    ppermute x99 -> x37, waiting for transfers between devices: 243 us -> 131 us  [swap(): lax.ppermute(array, name, [(i, i ^ mask) for i in range(lax.axis_size(nam...]
    ppermute x99 -> x37, starting transfers between devices: 160 us -> 51.3 us  [swap(): lax.ppermute(array, name, [(i, i ^ mask) for i in range(lax.axis_size(nam...]
    pallas_call x2 -> x1, Pallas kernels: 77.4 us -> 169 us  [attend_forward(): pl.pallas_call(functools.partial(forward_kernel, n=n, g=g, rows=256), in_...]
    select_n x42 -> x6, other arithmetic: 25.4 us -> 0.49 us  [double(): jnp.where(my_bit(name, k) == 0, jnp.concatenate([array, other], at), jnp....]
    all_gather x1 -> x0, blocking collectives: 24.7 us -> none  [local(): packed = lax.all_gather(jnp.concatenate(vectors), 'dp', axis=0).astype(F32)]
    concatenate x33 -> x6, other arithmetic: 17.3 us -> 2.75 us  [the longest x2 1.89 us: local(): jnp.concatenate(by_index(exchange([columns(d_context, me ^ t, pair, group...]
    concatenate x14 -> x3, local copies, waits for them, and re-layouts: 10.9 us -> 0.95 us  [the longest x1 0.69 us: local(): packed = jnp.concatenate(vectors)]
    slice x11 -> x0, local copies, waits for them, and re-layouts: 9.66 us -> none  [the longest x6 7.28 us: local(): block[:, i * LANES:(i + 1) * LANES]]
  transfers between devices with their start and end apart: 99 -> 37, of which waited for: 32 -> 14; matrix products, arithmetic and copies ran while one was open for 20% -> 31% of each run, Pallas kernels for 21% -> 38%
where the time goes in v1:
time: 768 us; the launch traced here: 759 us
  Pallas kernels  286 us (37%)
  waiting for transfers between devices  131 us (17%)
  matrix products  124 us (16%)
  local copies, waits for them, and re-layouts  67.1 us (9%)
  other arithmetic  51.4 us (7%)
  starting transfers between devices  51.3 us (7%)
  blocking collectives  47.3 us (6%)
    pallas_call x1, Pallas kernels, attend_forward(): pl.pallas_call(functools.partial(forward_kernel, n=n, g=g, rows=256), in_...  169 us
    ppermute x37, waiting for transfers between devices, swap(): lax.ppermute(array, name, [(i, i ^ mask) for i in range(lax.axis_size(nam...  131 us
    pallas_call x2, Pallas kernels, attend_backward(): pl.pallas_call(functools.partial(backward_kernel, chunk=chunk), grid=(len...  117 us
    dot_general x3, matrix products, matmul(): return jnp.dot(left, right, preferred_element_type=F32)  52.1 us
    ppermute x37, starting transfers between devices, swap(): lax.ppermute(array, name, [(i, i ^ mask) for i in range(lax.axis_size(nam...  51.3 us
    psum x1, blocking collectives, local(): lax.psum(rows, ('dp', 'seq'))  47.3 us
    dot_general x4, matrix products, matmul_right(): lax.dot_general(left, right, (((1,), (1,)), ((), ())), preferred_element_...  43.3 us
    dot_general x4, matrix products, matmul_left(): lax.dot_general(left, right, (((0,), (0,)), ((), ())), preferred_element_...  28.6 us
  transfers between devices with their start and end apart: 37, of which 14 were waited for; matrix products, arithmetic and copies ran while one was open for 31% of the time, Pallas kernels for 38%

profile of v1, /device:TPU:11, one launch (start us, length us, event | category | flops | bytes accessed | tf_op | source)
XLA Modules:
  0.0 759.0 jit_solution(17171076392561125124)
XLA Ops:
  16.6 168.6 %shard_map.271 = (bf16[768,1024]{1,0:T(8,128)(2,1)}, bf16[2,3072,128]{2,1,0:T(8,128)(2,1)}, bf16[2,3072,128]{2,1,0:T(8,128)(2,1)}, bf16[2,3072,128]{2,1,0:T(8,12...) custom-call(bf16[768,1024]{1,0:T(8,128)(2,1)} %hid_ref.1, ...), custom_call_target="tpu_custom_call" | custom-call | flops 38654705664 | bytes 7864320 | tf_op jit(solution)/shard_map/pallas_call | solution.py:471
  186.2 4.1 fusion.27
  191.4 38.6 %multiply_convert_fusion = (bf16[768,4096]{1,0:T(8,128)(2,1)}, f32[768,4096]{1,0:T(8,128)}, f32[768,4096]{1,0:T(8,128)}) fusion(f32[4096]{0:T(1024)S(1)} %bitcast.139, bf16[1024,4096]{1,0:T(8,128)(2,1)S(1)} %bitcast.145, f32[768,1024]{1,0:T(8,128)S(1)} %get-tuple-element.138, f32[1024]{0:T(1024)S(1)} %get-tuple-element.122, ...), kind=kOutput, calls=%fused_computation.3 | convolution fusion | flops 6654001152 | bytes 43022336 | tf_op jit(solution)/shard_map/dot_general | solution.py:30
  230.0 9.4 %fusion.28 = (f32[768]{0:T(1024)S(1)}, f32[768,1024]{1,0:T(8,128)S(1)}) fusion(f32[1024]{0:T(1024)S(1)} %get-tuple-element.121, bf16[768,4096]{1,0:T(8,128)(2,1)} %get-tuple-element.83, bf16[4096,1024]{1,0:T(8,128)(2,1)S(1)} %bitcast.149, f32[1024]{0:T(1024)S(1)} %get-tuple-element.122, f32[1024]{0:T(1024)S(1)} %get-tuple-element.123, ...), kind=kOutput, calls=%fused_computation.192 | convolution fusion | flops 6447954944 | bytes 20993024 | tf_op jit(solution)/shard_map/dot_general | solution.py:30
  240.8 1.8 fusion.9
  242.6 2.6 fusion.25
  245.2 9.8 %convolution_convert_fusion.1 = bf16[4096,1024]{1,0:T(8,128)(2,1)} fusion(bf16[768,4096]{1,0:T(8,128)(2,1)S(1)} %bitcast.156, f32[768,1024]{1,0:T(8,128)S(1)} %get-tuple-element.82, f32[768]{0:T(1024)S(1)} %negate_multiply_fusion.2), kind=kOutput, calls=%fused_computation.21 | convolution fusion | flops 6448218112 | bytes 17828864 | tf_op jit(solution)/shard_map/dot_general | solution.py:34
  255.0 21.1 %fusion.29 = (bf16[4096]{0:T(1024)(128)(2,1)S(1)}, bf16[768,4096]{1,0:T(8,128)(2,1)}) fusion(f32[768,4096]{1,0:T(8,128)} %get-tuple-element.84, bf16[4096,1024]{1,0:T(8,128)(2,1)} %bitcast.146, f32[768,1024]{1,0:T(8,128)} %copy-done.10, f32[768]{0:T(1024)S(1)} %negate_multiply_fusion.2, f32[768,4096]{1,0:T(8,128)} %get-tuple-element.139, ...), kind=kOutput, calls=%fused_computation.193 | convolution fusion | flops 6494351360 | bytes 43019264 | tf_op jit(solution)/shard_map/dot_general | solution.py:38
  276.0 13.1 %multiply_reduce_fusion = (bf16[1024]{0:T(1024)(128)(2,1)}, f32[768]{0:T(1024)S(1)}, bf16[1024]{0:T(1024)(128)(2,1)}, f32[768,1024]{1,0:T(8,128)S(1)}) fusion(f32[768,1024]{1,0:T(8,128)S(1)} %get-tuple-element.138, f32[768]{0:T(1024)S(1)} %fusion.18, f32[768]{0:T(1024)S(1)} %broadcast_multiply_fusion.1, f32[1024]{0:T(1024)S(1)} %get-tuple-element.123, ...), kind=kOutput, calls=%fused_computation.35 | convolution fusion | flops 6450312192 | bytes 24137728 | tf_op jit(solution)/shard_map/dot_general | solution.py:38
  289.1 10.2 %convolution_convert_fusion = bf16[1024,4096]{1,0:T(8,128)(2,1)} fusion(bf16[768,4096]{1,0:T(8,128)(2,1)S(1)} %copy-done.32, f32[768,1024]{1,0:T(8,128)S(1)} %get-tuple-element.138, f32[1024]{0:T(1024)S(1)} %get-tuple-element.122, f32[1024]{0:T(1024)S(1)} %get-tuple-element.123, f32[768]{0:T(1024)S(1)} %fusion.18, f32[768]{0:T(1024)S(1)} %broadcast_multiply_fusion.1), kind=kOutput, calls=%fused_computation.20 | convolution fusion | flops 6450577408 | bytes 17840128 | tf_op jit(solution)/shard_map/dot_general | solution.py:34
  300.9 3.1 convolution_convert_fusion.5
  304.1 3.3 convolution_convert_fusion.3
  307.3 2.0 constant_dynamic-slice_fusion.20
  309.4 7.5 collective-permute-start.8
  319.6 1.6 copy.42
  321.1 3.1 slice_bitcast_fusion.8
  324.2 1.9 slice_bitcast_fusion
  326.1 2.3 constant_dynamic-slice_fusion.14
  328.4 4.7 constant_dynamic-slice_fusion.9
  333.1 4.9 constant_dynamic-slice_fusion.4
  339.4 2.3 copy.43.k_ref
  341.7 2.3 copy.45.k_ref
  344.1 2.3 reduce
  350.3 1.7 collective-permute-start.5
  353.0 1.6 broadcast_in_dim.54.bias_ref
  354.6 58.5 %shard_map.273 = (bf16[3072,128]{1,0:T(8,128)(2,1)S(1)}, bf16[3072,128]{1,0:T(8,128)(2,1)S(1)}, bf16[3072,128]{1,0:T(8,128)(2,1)S(1)}) custom-call(bf16[3072,128]{1,0:T(8,128)(2,1)S(1)} %copy-done.3, bf16[3072,128]{1,0:T(8,128)(2,1)S(1)} %copy-done.1, bf16[3072,128]{1,0:T(8,128)(2,1)S(1)} %get-tuple-element.146.v_ref, ...), custom_call_target="tpu_custom_call" | custom-call | flops 48318382080 | bytes 7864320 | tf_op jit(solution)/shard_map/pallas_call | solution.py:562
  415.8 58.3 %shard_map.272 = (bf16[3072,128]{1,0:T(8,128)(2,1)S(1)}, bf16[3072,128]{1,0:T(8,128)(2,1)S(1)}, bf16[3072,128]{1,0:T(8,128)(2,1)S(1)}) custom-call(bf16[3072,128]{1,0:T(8,128)(2,1)S(1)} %copy-done.2, bf16[3072,128]{1,0:T(8,128)(2,1)S(1)} %copy-done, bf16[3072,128]{1,0:T(8,128)(2,1)S(1)} %get-tuple-element.145.v_ref, ...), custom_call_target="tpu_custom_call" | custom-call | flops 48318382080 | bytes 7864320 | tf_op jit(solution)/shard_map/pallas_call | solution.py:562
  475.9 6.0 convolution_convert_fusion.2
  481.9 2.2 constant_dynamic-slice_fusion.18
  485.8 5.4 convolution_convert_fusion.4
  494.4 3.1 convert_reduce_fusion
  497.6 1.7 add_convert_fusion.9
  501.4 2.3 copy.50
  503.7 8.7 %collective-permute-done.11 = bf16[2,2,1,128,768]{3,4,2,1,0:T(8,128)(2,1)} collective-permute-done((bf16[2,2,1,128,768]{3,4,2,1,0:T(8,128)(2,1)}, bf16[2,2,1,128,768]{3,4,2,1,0:T(8,128)(2,1)}, u32[]{:S(2)}, u32[]{:S(2)}) %collective-permute-start.11) | collective-permute-done | bytes 786464 | tf_op jit(solution)/shard_map/ppermute | solution.py:579
  512.4 1.5 convert_add_fusion.1
  517.1 4.9 collective-permute-done.18
  523.2 1.5 collective-permute-done.12
  526.3 7.5 collective-permute-start.20
  533.9 5.7 collective-permute-done.20
  540.7 3.2 collective-permute-done.13
  546.3 3.2 collective-permute-done.14
  549.6 1.9 collective-permute-start.15
  551.6 3.5 convert_add_fusion
  555.1 2.7 copy-done.4
  560.2 3.7 add_convert_fusion.1
  564.0 1.6 constant_dynamic-slice_fusion.8
  568.3 3.2 copy.49
  571.5 5.8 add_convert_fusion
  578.6 16.9 %collective-permute-done.10 = bf16[1,1,768,1024]{3,2,1,0:T(8,128)(2,1)} collective-permute-done((bf16[1,1,768,1024]{3,2,1,0:T(8,128)(2,1)}, bf16[1,1,768,1024]{3,2,1,0:T(8,128)(2,1)}, u32[]{:S(2)}, u32[]{:S(2)}) %collective-permute-start.10) | collective-permute-done | bytes 1572896 | tf_op jit(solution)/shard_map/ppermute | solution.py:579
  595.5 3.7 add_reduce_fusion
  599.2 41.2 %collective-permute-done.24 = bf16[2,2,2,1,1,32,4096]{6,5,4,3,2,1,0:T(8,128)(2,1)} collective-permute-done((bf16[2,2,2,1,1,32,4096]{6,5,4,3,2,1,0:T(8,128)(2,1)}, bf16[2,2,2,1,1,32,4096]{6,5,4,3,2,1,0:T(8,128)(2,1)}, u32[]{:S(2)}, u32[]{:S(2)}) %collective-permute-start.24) | collective-permute-done | bytes 2097184 | tf_op jit(solution)/shard_map/ppermute | solution.py:579
  640.4 2.4 add_convert_fusion.3
  645.9 20.9 %collective-permute-done.25 = bf16[2,2,1,1,1,32,4096]{6,5,4,3,2,1,0:T(8,128)(2,1)S(1)} collective-permute-done((bf16[2,2,1,1,1,32,4096]{6,5,4,3,2,1,0:T(8,128)(2,1)S(1)}, bf16[2,2,1,1,1,32,4096]{6,5,4,3,2,1,0:T(8,128)(2,1)S(1)}, u32[]{:S(2)}, u32[]{:S(2)}) %collective-permute-start.25) | collective-permute-done | bytes 1048608 | tf_op jit(solution)/shard_map/ppermute | solution.py:579
  667.1 1.6 collective-permute-start.26
  670.7 8.4 %collective-permute-done.26 = bf16[2,1,1,1,1,32,4096]{6,5,4,3,2,1,0:T(8,128)(2,1)S(1)} collective-permute-done((bf16[2,1,1,1,1,32,4096]{6,5,4,3,2,1,0:T(8,128)(2,1)S(1)}, bf16[2,1,1,1,1,32,4096]{6,5,4,3,2,1,0:T(8,128)(2,1)S(1)}, u32[]{:S(2)}, u32[]{:S(2)}) %collective-permute-start.26) | collective-permute-done | bytes 524320 | tf_op jit(solution)/shard_map/ppermute | solution.py:579
  679.3 2.9 collective-permute-start.27
  682.2 12.5 %collective-permute-done.33 = bf16[2,1,1,1,1,128,1024]{6,5,4,3,2,1,0:T(8,128)(2,1)S(1)} collective-permute-done((bf16[2,1,1,1,1,128,1024]{6,5,4,3,2,1,0:T(8,128)(2,1)S(1)}, bf16[2,1,1,1,1,128,1024]{6,5,4,3,2,1,0:T(8,128)(2,1)S(1)}, u32[]{:S(2)}, u32[]{:S(2)}) %collective-permute-start.33) | collective-permute-done | bytes 524320 | tf_op jit(solution)/shard_map/ppermute | solution.py:579
  695.0 2.8 collective-permute-start.34
  699.0 47.3 %psum.7 = bf16[8,1536]{1,0:T(8,128)(2,1)S(1)} all-reduce(bf16[8,1536]{1,0:T(8,128)(2,1)S(1)} %constant_dynamic-update-slice_fusion.6), channel_id=1, replica_groups=mesh['dp'=8,'seq'=4] {'dp','seq'}, use_global_device_ids=true, to_apply=%region_16.17 | all-reduce | flops 12288 | bytes 49152 | tf_op jit(solution)/shard_map/psum | solution.py:784
  747.2 2.3 collective-permute-start.29
  750.7 1.8 collective-permute-done.35
  752.5 2.8 collective-permute-start.36
  755.5 1.6 bitcast_convert_fusion.1
  757.2 1.6 bitcast_convert_fusion
  (271 shorter events, 66.8 us)
Async XLA Ops:
  1.9 345.0 %collective-permute-start.1 = (f32[768]{0:T(1024)}, f32[768]{0:T(1024)}, u32[]{:S(2)}, u32[]{:S(2)}) collective-permute-start(f32[768]{0:T(1024)} %reduce.1), channel_id=1, source_target_pairs={{0,2},{1,3},{2,0},{3,1},{4,6},{5,7},{6,4},{7,5},{8,10},{9,11},{10,... | collective-permute-start | bytes 9224 | tf_op jit(solution)/shard_map/ppermute | solution.py:579
  3.2 343.8 %collective-permute-start.2 = (f32[768]{0:T(1024)}, f32[768]{0:T(1024)}, u32[]{:S(2)}, u32[]{:S(2)}) collective-permute-start(f32[768]{0:T(1024)} %reduce.1), channel_id=1, source_target_pairs={{0,3},{1,2},{2,1},{3,0},{4,7},{5,6},{6,5},{7,4},{8,11},{9,10},{10,... | collective-permute-start | bytes 9224 | tf_op jit(solution)/shard_map/ppermute | solution.py:579
  4.2 343.2 %collective-permute-start = (f32[768]{0:T(1024)}, f32[768]{0:T(1024)}, u32[]{:S(2)}, u32[]{:S(2)}) collective-permute-start(f32[768]{0:T(1024)} %reduce.1), channel_id=1, source_target_pairs={{0,1},{1,0},{2,3},{3,2},{4,5},{5,4},{6,7},{7,6},{8,9},{9,8},{10,11... | collective-permute-start | bytes 9224 | tf_op jit(solution)/shard_map/ppermute | solution.py:579
  16.6 169.6 %copy-start.30 = (bf16[768,1024]{1,0:T(8,128)(2,1)S(1)}, bf16[768,1024]{1,0:T(8,128)(2,1)}, u32[]{:S(2)}) copy-start(bf16[768,1024]{1,0:T(8,128)(2,1)} %hid_ref.1) | copy-start | bytes 4718596
  186.2 43.8 %slice-start.8 = ((s8[8388608]{0:T(1024)(128)(4,1)}), s8[4194304]{0:T(1024)(128)(4,1)S(1)}, s32[]{:S(2)}) async-start(s8[8388608]{0:T(1024)(128)(4,1)} %bitcast.147), calls=%async_computation.8 | async-start | bytes 8388608
  191.4 38.6 %slice-start.9 = ((s8[8388608]{0:T(1024)(128)(4,1)}), s8[4194304]{0:T(1024)(128)(4,1)S(1)}, s32[]{:S(2)}) async-start(s8[8388608]{0:T(1024)(128)(4,1)} %bitcast.147), calls=%async_computation.9 | async-start | bytes 8388608
  245.1 9.8 %copy-start.10 = (f32[768,1024]{1,0:T(8,128)}, f32[768,1024]{1,0:T(8,128)S(1)}, u32[]{:S(2)}) copy-start(f32[768,1024]{1,0:T(8,128)S(1)} %get-tuple-element.82) | copy-start | bytes 9437188
  276.0 13.1 %copy-start.32 = (bf16[768,4096]{1,0:T(8,128)(2,1)S(1)}, bf16[768,4096]{1,0:T(8,128)(2,1)}, u32[]{:S(2)}) copy-start(bf16[768,4096]{1,0:T(8,128)(2,1)} %get-tuple-element.144) | copy-start | bytes 18874372
  289.1 10.2 %copy-start.21 = (f32[768]{0:T(1024)S(1)}, f32[768]{0:T(1024)}, u32[]{:S(2)}) copy-start(f32[768]{0:T(1024)} %copy-done.20) | copy-start | bytes 9220
  304.1 12.8 %copy-start.11 = (f32[768,1024]{1,0:T(8,128)S(1)}, f32[768,1024]{1,0:T(8,128)}, u32[]{:S(2)}) copy-start(f32[768,1024]{1,0:T(8,128)} %copy-done.10) | copy-start | bytes 9437188
  309.3 39.0 %collective-permute-start.7 = (bf16[768,128]{1,0:T(8,128)(2,1)}, bf16[768,128]{1,0:T(8,128)(2,1)S(1)}, u32[]{:S(2)}, u32[]{:S(2)}) collective-permute-start(bf16[768,128]{1,0:T(8,128)(2,1)} %get-tuple-element.103), channel_id=1, source_target_pairs={{0,2},{1,3},{2,0},{3,1},{4,6},{5,7},{6,4},{7,5},{8,10},{9,11},{10,... | collective-permute-start | bytes 589832 | tf_op jit(solution)/shard_map/ppermute | solution.py:579
  309.4 38.9 %collective-permute-start.8 = (bf16[768,128]{1,0:T(8,128)(2,1)}, bf16[768,128]{1,0:T(8,128)(2,1)S(1)}, u32[]{:S(2)}, u32[]{:S(2)}) collective-permute-start(bf16[768,128]{1,0:T(8,128)(2,1)} %get-tuple-element.104), channel_id=1, source_target_pairs={{0,3},{1,2},{2,1},{3,0},{4,7},{5,6},{6,5},{7,4},{8,11},{9,10},{10,... | collective-permute-start | bytes 589832 | tf_op jit(solution)/shard_map/ppermute | solution.py:579
  346.9 7.7 %copy-start.1 = (bf16[3072,128]{1,0:T(8,128)(2,1)S(1)}, bf16[3072,128]{1,0:T(8,128)(2,1)}, u32[]{:S(2)}) copy-start(bf16[3072,128]{1,0:T(8,128)(2,1)} %copy.45.k_ref) | copy-start | bytes 2359300
  346.9 7.7 %copy-start.3 = (bf16[3072,128]{1,0:T(8,128)(2,1)S(1)}, bf16[3072,128]{1,0:T(8,128)(2,1)}, u32[]{:S(2)}) copy-start(bf16[3072,128]{1,0:T(8,128)(2,1)} %get-tuple-element.114.q_ref) | copy-start | bytes 2359300
  346.9 1.7 collective-permute-start.6
  347.0 150.6 %collective-permute-start.16 = (bf16[2,2,2,2,1,32,1024]{6,5,4,3,2,1,0:T(8,128)(2,1)}, bf16[2,2,2,2,1,32,1024]{6,5,4,3,2,1,0:T(8,128)(2,1)}, u32[]{:S(2)}, u32[]{:S(2)}) collective-permute-start(bf16[2,2,2,2,1,32,1024]{6,5,4,3,2,1,0:T(8,128)(2,1)} %constant_dynamic-slice_fusion.14), channel_id=1, source_target_pairs={{0,1},{1,0},{2,3},{3,2},{4,5},{5,4},{6,7},{7,6},{8,9},{9,8},{10,11... | collective-permute-start | bytes 3145736 | tf_op jit(solution)/shard_map/ppermute | solution.py:579
  347.5 212.7 %collective-permute-start.23 = (bf16[2,2,2,2,1,32,4096]{6,5,4,3,2,1,0:T(8,128)(2,1)}, bf16[2,2,2,2,1,32,4096]{6,5,4,3,2,1,0:T(8,128)(2,1)}, u32[]{:S(2)}, u32[]{:S(2)}) collective-permute-start(bf16[2,2,2,2,1,32,4096]{6,5,4,3,2,1,0:T(8,128)(2,1)} %constant_dynamic-slice_fusion.9), channel_id=1, source_target_pairs={{0,1},{1,0},{2,3},{3,2},{4,5},{5,4},{6,7},{7,6},{8,9},{9,8},{10,11... | collective-permute-start | bytes 12582920 | tf_op jit(solution)/shard_map/ppermute | solution.py:579
  350.1 63.1 %collective-permute-start.4 = (bf16[768,128]{1,0:T(8,128)(2,1)S(1)}, bf16[768,128]{1,0:T(8,128)(2,1)S(1)}, u32[]{:S(2)}, u32[]{:S(2)}) collective-permute-start(bf16[768,128]{1,0:T(8,128)(2,1)S(1)} %get-tuple-element.101), channel_id=1, source_target_pairs={{0,2},{1,3},{2,0},{3,1},{4,6},{5,7},{6,4},{7,5},{8,10},{9,11},{10,... | collective-permute-start | bytes 589832 | tf_op jit(solution)/shard_map/ppermute | solution.py:579
  350.3 63.4 %collective-permute-start.5 = (bf16[768,128]{1,0:T(8,128)(2,1)S(1)}, bf16[768,128]{1,0:T(8,128)(2,1)S(1)}, u32[]{:S(2)}, u32[]{:S(2)}) collective-permute-start(bf16[768,128]{1,0:T(8,128)(2,1)S(1)} %get-tuple-element.100), channel_id=1, source_target_pairs={{0,3},{1,2},{2,1},{3,0},{4,7},{5,6},{6,5},{7,4},{8,11},{9,10},{10,... | collective-permute-start | bytes 589832 | tf_op jit(solution)/shard_map/ppermute | solution.py:579
  351.9 61.7 %collective-permute-start.3 = (bf16[768,128]{1,0:T(8,128)(2,1)S(1)}, bf16[768,128]{1,0:T(8,128)(2,1)S(1)}, u32[]{:S(2)}, u32[]{:S(2)}) collective-permute-start(bf16[768,128]{1,0:T(8,128)(2,1)S(1)} %get-tuple-element.102), channel_id=1, source_target_pairs={{0,1},{1,0},{2,3},{3,2},{4,5},{5,4},{6,7},{7,6},{8,9},{9,8},{10,11... | collective-permute-start | bytes 589832 | tf_op jit(solution)/shard_map/ppermute | solution.py:579
  413.2 158.3 %collective-permute-start.30 = (bf16[2,2,2,2,1,128,1024]{6,5,4,3,2,1,0:T(8,128)(2,1)}, bf16[2,2,2,2,1,128,1024]{6,5,4,3,2,1,0:T(8,128)(2,1)}, u32[]{:S(2)}, u32[]{:S(2)}) collective-permute-start(bf16[2,2,2,2,1,128,1024]{6,5,4,3,2,1,0:T(8,128)(2,1)} %constant_dynamic-slice_fusion.4), channel_id=1, source_target_pairs={{0,1},{1,0},{2,3},{3,2},{4,5},{5,4},{6,7},{7,6},{8,9},{9,8},{10,11... | collective-permute-start | bytes 12582920 | tf_op jit(solution)/shard_map/ppermute | solution.py:579
  474.5 11.3 %slice-start.10 = ((s8[6291456]{0:T(1024)(128)(4,1)}), s8[4194304]{0:T(1024)(128)(4,1)S(1)}, s32[]{:S(2)}) async-start(s8[6291456]{0:T(1024)(128)(4,1)} %bitcast.150), calls=%async_computation.10 | async-start | bytes 8388608
  475.3 10.5 %copy-start.12 = (bf16[3072,768]{1,0:T(8,128)(2,1)}, bf16[3072,768]{1,0:T(8,128)(2,1)S(1)}, u32[]{:S(2)}) copy-start(bf16[3072,768]{1,0:T(8,128)(2,1)S(1)} %constant_dynamic-update-slice_fusion) | copy-start | bytes 14155780
  475.9 9.9 %slice-start.11 = ((s8[6291456]{0:T(1024)(128)(4,1)}), s8[2097152]{0:T(1024)(128)(4,1)S(1)}, s32[]{:S(2)}) async-start(s8[6291456]{0:T(1024)(128)(4,1)} %bitcast.150), calls=%async_computation.11 | async-start | bytes 4194304
  485.6 65.9 %collective-permute-start.9 = (bf16[2,1,768,1024]{3,2,1,0:T(8,128)(2,1)}, bf16[2,1,768,1024]{3,2,1,0:T(8,128)(2,1)}, u32[]{:S(2)}, u32[]{:S(2)}) collective-permute-start(bf16[2,1,768,1024]{3,2,1,0:T(8,128)(2,1)} %constant_dynamic-slice_fusion.18), channel_id=1, source_target_pairs={{0,1},{1,0},{2,3},{3,2},{4,5},{5,4},{6,7},{7,6},{8,9},{9,8},{10,11... | collective-permute-start | bytes 9437192 | tf_op jit(solution)/shard_map/ppermute | solution.py:579
  493.3 19.1 %collective-permute-start.11 = (bf16[2,2,1,128,768]{3,4,2,1,0:T(8,128)(2,1)}, bf16[2,2,1,128,768]{3,4,2,1,0:T(8,128)(2,1)}, u32[]{:S(2)}, u32[]{:S(2)}) collective-permute-start(bf16[2,2,1,128,768]{3,4,2,1,0:T(8,128)(2,1)} %copy.51), channel_id=1, source_target_pairs={{0,4},{4,0},{8,12},{12,8},{16,20},{20,16},{24,28},{28,24},{1,5},{5... | collective-permute-start | bytes 2359304 | tf_op jit(solution)/shard_map/ppermute | solution.py:579
  499.3 52.3 %slice-start.4 = ((s8[6291456]{0:T(1024)(128)(4,1)}), s8[2097152]{0:T(1024)(128)(4,1)S(1)}, s32[]{:S(2)}) async-start(s8[6291456]{0:T(1024)(128)(4,1)} %bitcast.130), calls=%async_computation.4 | async-start | bytes 4194304
  500.1 13.8 %collective-permute-start.17 = (bf16[2,1,2,2,1,32,1024]{6,5,4,3,2,1,0:T(8,128)(2,1)}, bf16[2,1,2,2,1,32,1024]{6,5,4,3,2,1,0:T(8,128)(2,1)}, u32[]{:S(2)}, u32[]{:S(2)}) collective-permute-start(bf16[2,1,2,2,1,32,1024]{6,5,4,3,2,1,0:T(8,128)(2,1)} %constant_dynamic-slice_fusion.13), channel_id=1, source_target_pairs={{0,8},{4,12},{8,0},{12,4},{16,24},{20,28},{24,16},{28,20},{1,9},{5... | collective-permute-start | bytes 1572872 | tf_op jit(solution)/shard_map/ppermute | solution.py:579
  515.2 36.3 %slice-start.5 = ((s8[6291456]{0:T(1024)(128)(4,1)}), s8[4194304]{0:T(1024)(128)(4,1)S(1)}, s32[]{:S(2)}) async-start(s8[6291456]{0:T(1024)(128)(4,1)} %bitcast.130), calls=%async_computation.5 | async-start | bytes 8388608
  515.3 6.7 collective-permute-start.18
  515.5 9.2 %collective-permute-start.12 = (bf16[2,1,1,128,768]{3,4,2,1,0:T(8,128)(2,1)S(1)}, bf16[2,1,1,128,768]{3,4,2,1,0:T(8,128)(2,1)S(1)}, u32[]{:S(2)}, u32[]{:S(2)}) collective-permute-start(bf16[2,1,1,128,768]{3,4,2,1,0:T(8,128)(2,1)S(1)} %dynamic-slice_convert_fusion.1), channel_id=1, source_target_pairs={{0,8},{4,12},{8,0},{12,4},{16,24},{20,28},{24,16},{28,20},{1,9},{5... | collective-permute-start | bytes 1179656 | tf_op jit(solution)/shard_map/ppermute | solution.py:579
  522.1 4.2 collective-permute-start.19
  524.7 35.5 %slice-start.2 = ((s8[8388608]{0:T(1024)(128)(4,1)}), s8[4194304]{0:T(1024)(128)(4,1)S(1)}, s32[]{:S(2)}) async-start(s8[8388608]{0:T(1024)(128)(4,1)} %bitcast.125), calls=%async_computation.2 | async-start | bytes 8388608
  526.3 13.2 %collective-permute-start.20 = (bf16[1,1,1,1,1,32,1024]{6,5,4,3,2,1,0:T(8,128)(2,1)S(1)}, bf16[1,1,1,1,1,32,1024]{6,5,4,3,2,1,0:T(8,128)(2,1)S(1)}, u32[]{:S(2)}, u32[]{:S(2)}) collective-permute-start(bf16[1,1,1,1,1,32,1024]{6,5,4,3,2,1,0:T(8,128)(2,1)S(1)} %constant_dynamic-slice_fusion.10), channel_id=1, source_target_pairs={{0,16},{4,20},{8,24},{12,28},{16,0},{20,4},{24,8},{28,12},{1,17},{... | collective-permute-start | bytes 196616 | tf_op jit(solution)/shard_map/ppermute | solution.py:579
  533.8 10.1 %collective-permute-start.13 = (bf16[1,1,1,128,768]{3,4,2,1,0:T(8,128)(2,1)S(1)}, bf16[1,1,1,128,768]{3,4,2,1,0:T(8,128)(2,1)S(1)}, u32[]{:S(2)}, u32[]{:S(2)}) collective-permute-start(bf16[1,1,1,128,768]{3,4,2,1,0:T(8,128)(2,1)S(1)} %dynamic-slice_convert_fusion.2), channel_id=1, source_target_pairs={{0,16},{4,20},{8,24},{12,28},{16,0},{20,4},{24,8},{28,12},{1,17},{... | collective-permute-start | bytes 589832 | tf_op jit(solution)/shard_map/ppermute | solution.py:579
  539.6 5.5 collective-permute-start.21
  544.0 5.5 collective-permute-start.14
  545.1 6.4 collective-permute-start.22
  549.6 17.2 %collective-permute-start.15 = (bf16[2,1,128,768]{2,3,1,0:T(8,128)(2,1)S(1)}, bf16[2,1,128,768]{2,3,1,0:T(8,128)(2,1)S(1)}, u32[]{:S(2)}, u32[]{:S(2)}) collective-permute-start(bf16[2,1,128,768]{2,3,1,0:T(8,128)(2,1)S(1)} %maximum_select_fusion.5), channel_id=1, source_target_pairs={{0,1},{1,0},{2,3},{3,2},{4,5},{5,4},{6,7},{7,6},{8,9},{9,8},{10,11... | collective-permute-start | bytes 1179656 | tf_op jit(solution)/shard_map/ppermute | solution.py:579
  551.5 8.7 %slice-start.3 = ((s8[8388608]{0:T(1024)(128)(4,1)}), s8[4194304]{0:T(1024)(128)(4,1)S(1)}, s32[]{:S(2)}) async-start(s8[8388608]{0:T(1024)(128)(4,1)} %bitcast.125), calls=%async_computation.3 | async-start | bytes 8388608
  559.1 36.3 %collective-permute-start.10 = (bf16[1,1,768,1024]{3,2,1,0:T(8,128)(2,1)}, bf16[1,1,768,1024]{3,2,1,0:T(8,128)(2,1)}, u32[]{:S(2)}, u32[]{:S(2)}) collective-permute-start(bf16[1,1,768,1024]{3,2,1,0:T(8,128)(2,1)} %dynamic-slice_convert_fusion), channel_id=1, source_target_pairs={{0,2},{1,3},{2,0},{3,1},{4,6},{5,7},{6,4},{7,5},{8,10},{9,11},{10,... | collective-permute-start | bytes 4718600 | tf_op jit(solution)/shard_map/ppermute | solution.py:579
  565.5 74.9 %collective-permute-start.24 = (bf16[2,2,2,1,1,32,4096]{6,5,4,3,2,1,0:T(8,128)(2,1)}, bf16[2,2,2,1,1,32,4096]{6,5,4,3,2,1,0:T(8,128)(2,1)}, u32[]{:S(2)}, u32[]{:S(2)}) collective-permute-start(bf16[2,2,2,1,1,32,4096]{6,5,4,3,2,1,0:T(8,128)(2,1)} %constant_dynamic-slice_fusion.8), channel_id=1, source_target_pairs={{0,2},{1,3},{2,0},{3,1},{4,6},{5,7},{6,4},{7,5},{8,10},{9,11},{10,... | collective-permute-start | bytes 6291464 | tf_op jit(solution)/shard_map/ppermute | solution.py:579
  568.3 27.1 %slice-start = ((s8[6291456]{0:T(1024)(128)(4,1)}), s8[2097152]{0:T(1024)(128)(4,1)S(1)}, s32[]{:S(2)}) async-start(s8[6291456]{0:T(1024)(128)(4,1)} %bitcast.120), calls=%async_computation | async-start | bytes 4194304
  571.5 24.0 %slice-start.1 = ((s8[6291456]{0:T(1024)(128)(4,1)}), s8[4194304]{0:T(1024)(128)(4,1)S(1)}, s32[]{:S(2)}) async-start(s8[6291456]{0:T(1024)(128)(4,1)} %bitcast.120), calls=%async_computation.1 | async-start | bytes 8388608
  577.3 18.2 %copy-start.9 = (f32[768,1024]{1,0:T(8,128)S(1)}, f32[768,1024]{1,0:T(8,128)}, u32[]{:S(2)}) copy-start(f32[768,1024]{1,0:T(8,128)} %copy-done.8) | copy-start | bytes 9437188
  577.3 18.2 %copy-start.24 = (f32[768]{0:T(1024)S(1)}, f32[768]{0:T(1024)}, u32[]{:S(2)}) copy-start(f32[768]{0:T(1024)} %copy-done.23) | copy-start | bytes 9220
  577.5 21.7 %copy-start.29 = (bf16[1024]{0:T(1024)(128)(2,1)S(1)}, bf16[1024]{0:T(1024)(128)(2,1)}, u32[]{:S(2)}) copy-start(bf16[1024]{0:T(1024)(128)(2,1)} %get-tuple-element.74) | copy-start | bytes 6148
  577.5 62.9 %copy-start.6 = (bf16[2,2,2,2,1,32,4096]{6,5,4,3,2,1,0:T(8,128)(2,1)S(1)}, bf16[2,2,2,2,1,32,4096]{6,5,4,3,2,1,0:T(8,128)(2,1)}, u32[]{:S(2)}) copy-start(bf16[2,2,2,2,1,32,4096]{6,5,4,3,2,1,0:T(8,128)(2,1)} %copy-done.5) | copy-start | bytes 12582916
  577.5 66.5 %collective-permute-start.31 = (bf16[2,2,1,2,1,128,1024]{6,5,4,3,2,1,0:T(8,128)(2,1)S(1)}, bf16[2,2,1,2,1,128,1024]{6,5,4,3,2,1,0:T(8,128)(2,1)S(1)}, u32[]{:S(2)}, u32[]{:S(2)}) collective-permute-start(bf16[2,2,1,2,1,128,1024]{6,5,4,3,2,1,0:T(8,128)(2,1)S(1)} %constant_dynamic-slice_fusion.3), channel_id=1, source_target_pairs={{0,4},{4,0},{8,12},{12,8},{16,20},{20,16},{24,28},{28,24},{1,5},{5... | collective-permute-start | bytes 6291464 | tf_op jit(solution)/shard_map/ppermute | solution.py:579
  599.2 44.8 %copy-start.28 = (bf16[1024]{0:T(1024)(128)(2,1)S(1)}, bf16[1024]{0:T(1024)(128)(2,1)}, u32[]{:S(2)}) copy-start(bf16[1024]{0:T(1024)(128)(2,1)} %get-tuple-element.78) | copy-start | bytes 6148
  599.2 44.8 %copy-start.27 = (bf16[1024]{0:T(1024)(128)(2,1)S(1)}, bf16[1024]{0:T(1024)(128)(2,1)}, u32[]{:S(2)}) copy-start(bf16[1024]{0:T(1024)(128)(2,1)} %add_reduce_fusion.1) | copy-start | bytes 6148
  599.2 44.8 %copy-start.25 = (bf16[1024]{0:T(1024)(128)(2,1)S(1)}, bf16[1024]{0:T(1024)(128)(2,1)}, u32[]{:S(2)}) copy-start(bf16[1024]{0:T(1024)(128)(2,1)} %get-tuple-element.76) | copy-start | bytes 6148
  642.9 23.9 %collective-permute-start.25 = (bf16[2,2,1,1,1,32,4096]{6,5,4,3,2,1,0:T(8,128)(2,1)S(1)}, bf16[2,2,1,1,1,32,4096]{6,5,4,3,2,1,0:T(8,128)(2,1)S(1)}, u32[]{:S(2)}, u32[]{:S(2)}) collective-permute-start(bf16[2,2,1,1,1,32,4096]{6,5,4,3,2,1,0:T(8,128)(2,1)S(1)} %constant_dynamic-slice_fusion.7), channel_id=1, source_target_pairs={{0,4},{4,0},{8,12},{12,8},{16,20},{20,16},{24,28},{28,24},{1,5},{5... | collective-permute-start | bytes 3145736 | tf_op jit(solution)/shard_map/ppermute | solution.py:579
  645.0 23.7 %copy-start.26 = (bf16[1024]{0:T(1024)(128)(2,1)S(1)}, bf16[1024]{0:T(1024)(128)(2,1)}, u32[]{:S(2)}) copy-start(bf16[1024]{0:T(1024)(128)(2,1)} %reduce) | copy-start | bytes 6148
  645.1 23.7 %collective-permute-start.32 = (bf16[2,2,1,1,1,128,1024]{6,5,4,3,2,1,0:T(8,128)(2,1)S(1)}, bf16[2,2,1,1,1,128,1024]{6,5,4,3,2,1,0:T(8,128)(2,1)S(1)}, u32[]{:S(2)}, u32[]{:S(2)}) collective-permute-start(bf16[2,2,1,1,1,128,1024]{6,5,4,3,2,1,0:T(8,128)(2,1)S(1)} %constant_dynamic-slice_fusion.2), channel_id=1, source_target_pairs={{0,2},{1,3},{2,0},{3,1},{4,6},{5,7},{6,4},{7,5},{8,10},{9,11},{10,... | collective-permute-start | bytes 3145736 | tf_op jit(solution)/shard_map/ppermute | solution.py:579
  667.1 12.0 %collective-permute-start.26 = (bf16[2,1,1,1,1,32,4096]{6,5,4,3,2,1,0:T(8,128)(2,1)S(1)}, bf16[2,1,1,1,1,32,4096]{6,5,4,3,2,1,0:T(8,128)(2,1)S(1)}, u32[]{:S(2)}, u32[]{:S(2)}) collective-permute-start(bf16[2,1,1,1,1,32,4096]{6,5,4,3,2,1,0:T(8,128)(2,1)S(1)} %constant_dynamic-slice_fusion.6), channel_id=1, source_target_pairs={{0,8},{4,12},{8,0},{12,4},{16,24},{20,28},{24,16},{28,20},{1,9},{5... | collective-permute-start | bytes 1572872 | tf_op jit(solution)/shard_map/ppermute | solution.py:579
  669.2 29.8 %copy-start.22 = (bf16[8,512]{1,0:T(8,128)(2,1)S(1)}, bf16[8,512]{1,0:T(8,128)(2,1)}, u32[]{:S(2)}) copy-start(bf16[8,512]{1,0:T(8,128)(2,1)} %reshape.601) | copy-start | bytes 24580
  669.2 25.5 %collective-permute-start.33 = (bf16[2,1,1,1,1,128,1024]{6,5,4,3,2,1,0:T(8,128)(2,1)S(1)}, bf16[2,1,1,1,1,128,1024]{6,5,4,3,2,1,0:T(8,128)(2,1)S(1)}, u32[]{:S(2)}, u32[]{:S(2)}) collective-permute-start(bf16[2,1,1,1,1,128,1024]{6,5,4,3,2,1,0:T(8,128)(2,1)S(1)} %constant_dynamic-slice_fusion.1), channel_id=1, source_target_pairs={{0,8},{4,12},{8,0},{12,4},{16,24},{20,28},{24,16},{28,20},{1,9},{5... | collective-permute-start | bytes 1572872 | tf_op jit(solution)/shard_map/ppermute | solution.py:579
  679.3 18.5 %collective-permute-start.27 = (bf16[1,1,1,1,1,32,4096]{6,5,4,3,2,1,0:T(8,128)(2,1)S(1)}, bf16[1,1,1,1,1,32,4096]{6,5,4,3,2,1,0:T(8,128)(2,1)S(1)}, u32[]{:S(2)}, u32[]{:S(2)}) collective-permute-start(bf16[1,1,1,1,1,32,4096]{6,5,4,3,2,1,0:T(8,128)(2,1)S(1)} %constant_dynamic-slice_fusion.5), channel_id=1, source_target_pairs={{0,16},{4,20},{8,24},{12,28},{16,0},{20,4},{24,8},{28,12},{1,17},{... | collective-permute-start | bytes 786440 | tf_op jit(solution)/shard_map/ppermute | solution.py:579
  695.0 51.3 %collective-permute-start.34 = (bf16[1,1,1,1,1,128,1024]{6,5,4,3,2,1,0:T(8,128)(2,1)S(1)}, bf16[1,1,1,1,1,128,1024]{6,5,4,3,2,1,0:T(8,128)(2,1)S(1)}, u32[]{:S(2)}, u32[]{:S(2)}) collective-permute-start(bf16[1,1,1,1,1,128,1024]{6,5,4,3,2,1,0:T(8,128)(2,1)S(1)} %constant_dynamic-slice_fusion), channel_id=1, source_target_pairs={{0,16},{4,20},{8,24},{12,28},{16,0},{20,4},{24,8},{28,12},{1,17},{... | collective-permute-start | bytes 786440 | tf_op jit(solution)/shard_map/ppermute | solution.py:579
  697.9 49.2 %collective-permute-start.28 = (bf16[1,1,1,1,1,32,4096]{6,5,4,3,2,1,0:T(8,128)(2,1)S(1)}, bf16[1,1,1,1,1,32,4096]{6,5,4,3,2,1,0:T(8,128)(2,1)S(1)}, u32[]{:S(2)}, u32[]{:S(2)}) collective-permute-start(bf16[1,1,1,1,1,32,4096]{6,5,4,3,2,1,0:T(8,128)(2,1)S(1)} %add_convert_fusion.14), channel_id=1, source_target_pairs={{0,2},{1,3},{2,0},{3,1},{4,6},{5,7},{6,4},{7,5},{8,10},{9,11},{10,... | collective-permute-start | bytes 786440 | tf_op jit(solution)/shard_map/ppermute | solution.py:579
  746.4 6.1 collective-permute-start.35
  747.2 8.1 %collective-permute-start.29 = (bf16[1,1,1,2,1,32,4096]{6,5,4,3,2,1,0:T(8,128)(2,1)S(1)}, bf16[1,1,1,2,1,32,4096]{6,5,4,3,2,1,0:T(8,128)(2,1)S(1)}, u32[]{:S(2)}, u32[]{:S(2)}) collective-permute-start(bf16[1,1,1,2,1,32,4096]{6,5,4,3,2,1,0:T(8,128)(2,1)S(1)} %maximum_select_fusion.3), channel_id=1, source_target_pairs={{0,1},{1,0},{2,3},{3,2},{4,5},{5,4},{6,7},{7,6},{8,9},{9,8},{10,11... | collective-permute-start | bytes 1572872 | tf_op jit(solution)/shard_map/ppermute | solution.py:579
  752.5 4.5 collective-permute-start.36
  (22 other events, 68.0 us)

commit v2 on v1

--- a/solution.py
+++ b/solution.py
@@ -49,19 +49,6 @@
 def head_mask(rows, head):
     lane = lax.broadcasted_iota(jnp.int32, (rows, LANES), 1)
     return (lane < HEAD_DIM) if head == 0 else (lane >= HEAD_DIM)
-
-
-def fill_keys(k_ref, v_ref, bias_ref, ka_ref, va_ref):
-    rows = k_ref.shape[0]
-    lane = lax.broadcasted_iota(jnp.int32, (rows, LANES), 1)
-    first, second, third = thirds(bias_ref[...])
-    extra = jnp.where(
-        lane == 0, first, jnp.where(lane == 1, second, jnp.where(lane == 2, third, 1.0))
-    )
-    ka_ref[:, :LANES] = k_ref[...]
-    ka_ref[:, LANES:] = jnp.where(lane < 6, extra, 0.0).astype(LOW)
-    va_ref[:, :LANES] = v_ref[...]
-    va_ref[:, LANES:] = jnp.where(lane < 3, 1.0, 0.0).astype(LOW)
 
 
 def send_to(src, dst, send_sem, recv_sem, dp, seq):
@@ -130,7 +117,7 @@
 
 def forward_kernel(
     hid_ref, wch_ref, kb_ref, wo_ref, wu_ref, wd_ref,
-    ctx_out, own_ctx, q_out, k_out, v_out, qx_out, hid_out, wq_out, vec_out, wo_out, wu_out, wd_out,
+    ctx_out, own_ctx, q_out, ka_out, v_out, qx_out, hid_out, wq_out, vec_out, wo_out, wu_out, wd_out,
     hid, wch, wq, kb, q_s, k_s, v_s, ka, va, ctx, qx,
     loc, hy, hc, hf, kbs, wz, wx, pz, px, pc, cs, kx,
     *, n, g, rows,
@@ -323,7 +310,6 @@
     more = [
         pltpu.make_async_copy(hid, hid_out, loc.at[8]),
         pltpu.make_async_copy(q_s, q_out, loc.at[9]),
-        pltpu.make_async_copy(k_s, k_out, loc.at[10]),
         pltpu.make_async_copy(v_s, v_out, loc.at[11]),
     ]
     for copy in more:
@@ -348,6 +334,9 @@
             ctx_out.at[:, pl.ds(pl.multiple_of(s * gw + pair * LANES, LANES), LANES)],
             kx.at[pair],
         )
+
+    def ka_keep(pair):
+        return pltpu.make_async_copy(ka, ka_out.at[pair], loc.at[10])
 
     events = {}
     every = max(1, steps // (len(pieces) + 1))
@@ -370,6 +359,10 @@
                 def _(t=t):
                     for event in events[t]:
                         event()
+
+        @pl.when((turn == 0) & (step > 0))
+        def _():
+            ka_keep(pair - 1).wait()
 
         @pl.when(turn == 0)
         def _():
@@ -386,6 +379,7 @@
                 ka[span, LANES:] = jnp.where(lane < 6, extra, 0.0).astype(LOW)
                 va[span, :LANES] = v_s[pair, span, :]
                 va[span, LANES:] = jnp.where(lane < 3, 1.0, 0.0).astype(LOW)
+            ka_keep(pair).start()
 
         span = pl.ds(pl.multiple_of(block * rows, rows), rows)
         lane = lax.broadcasted_iota(jnp.int32, (rows, LANES), 1)
@@ -420,6 +414,7 @@
         return carry
 
     lax.fori_loop(0, steps, attend, 0)
+    ka_keep(pairs - 1).wait()
     last = [
         pltpu.make_async_copy(qx, qx_out, loc.at[12]),
         pltpu.make_async_copy(ctx, own_ctx, loc.at[13]),
@@ -461,7 +456,7 @@
     low = lambda *shape: jax.ShapeDtypeStruct(shape, LOW)
     out_shape = [
         low(tok, width), low(pairs, length, LANES), low(pairs, length, LANES),
-        low(pairs, length, LANES), low(pairs, length, LANES), low(pairs, 2, length, LANES),
+        low(pairs, length, 2 * LANES), low(pairs, length, LANES), low(pairs, 2, length, LANES),
         low(g, tok, width), low(width, 3 * gw), low(n, 16, 3 * gw),
         low(n, *w_out.shape), low(n, *w_up.shape), low(n, *w_down.shape),
     ]
@@ -489,60 +484,455 @@
     )(hidden, chunk, bias_rows, w_out, w_up, w_down)
 
 
+def piece_rows(n):
+    return max(16, 512 // n)
+
+
+def grad_pieces(shapes, n, wide):
+    out = []
+    for index, (rows, cols) in enumerate(shapes):
+        half = rows // 2
+        size = min(half, piece_rows(n))
+        for off in range(0, half, size):
+            for col in range(0, cols, wide):
+                out.append((index, off, col))
+    return out
+
+
 def backward_kernel(
-    q_ref, k_ref, v_ref, kt_ref, bias_ref, qx_ref, o_ref, do_ref,
-    dq_ref, dk_ref, dv_ref, ka_ref, va_ref, dk_acc, dv_acc, *, chunk,
+    dctx_ref, q_ref, ka_ref, v_ref, qx_ref, o_ref, hid_ref, wq_ref, vec_ref, go_ref, gu_ref,
+    gd_ref,
+    din_out, sum_out, sq_out, c_land, x_land,
+    q_s, ka, va, kt, qx, o_s, do_s, dh, dk_acc, dv_acc, hid, wq, vec,
+    part_c, part_k, part_y, part_b, din, own_b, c_b, s_b, x_b, t_b, z_b, u_b, y_b, f_b,
+    q_b, xq, tq, zq, rq,
+    loc, ld, sd, sk, sy, sc, sx, sz, sg, sf, sl, sxq, szq, sgq,
+    *, n, g, rows, chunk,
 ):
-    step = pl.program_id(0)
-
-    @pl.when(step == 0)
-    def _():
-        fill_keys(k_ref, v_ref, bias_ref, ka_ref, va_ref)
-        dk_acc[...] = jnp.zeros_like(dk_acc)
-        dv_acc[...] = jnp.zeros_like(dv_acc)
-
-    rows = q_ref.shape[0]
-    length = k_ref.shape[0]
-    lane = lax.broadcasted_iota(jnp.int32, (rows, LANES), 1)
-    queries = q_ref[...].astype(F32) * SCALE
-    grads = do_ref[...].astype(F32)
-    dots = grads * o_ref[...].astype(F32)
-    q_wide, g_wide, q_mask, g_mask = [], [], [], []
-    for head in range(2):
-        mask = head_mask(rows, head)
-        masked = jnp.where(mask, queries, 0.0).astype(LOW)
-        g_masked = jnp.where(mask, grads, 0.0).astype(LOW)
-        delta = jnp.sum(jnp.where(mask, dots, 0.0), -1, keepdims=True)
-        first, second, third = thirds(delta)
-        extra = jnp.where(
-            lane == 0, -first, jnp.where(lane == 1, -second, jnp.where(lane == 2, -third, 0.0))
-        ).astype(LOW)
-        q_mask.append(masked)
-        g_mask.append(g_masked)
-        q_wide.append(jnp.concatenate([masked, qx_ref[head]], 1))
-        g_wide.append(jnp.concatenate([g_masked, extra], 1))
-    q_rows = jnp.concatenate(q_mask, 0)
-    g_rows = jnp.concatenate(g_mask, 0)
-    dq_t = [jnp.zeros((LANES, rows), F32) for _ in range(2)]
-    for start in range(0, length, chunk):
-        part = slice(start, start + chunk)
-        p_list, ds_list = [], []
+    me = Peers(n, g)
+    d, s, nz, ny = me.d, me.s, me.nz, me.ny
+    tok, width = dctx_ref.shape
+    length = tok * g
+    deep = width // n
+    gw = width // g
+    pairs = gw // LANES
+    grads = (go_ref, gu_ref, gd_ref)
+    wide = own_b.shape[3]
+    size = own_b.shape[2]
+    pieces = grad_pieces([ref.shape[1:] for ref in grads], n, wide)
+    count = len(pieces)
+    blocks = length // rows
+    per = tok // rows
+    steps = pairs * blocks
+    me.barrier()
+
+    def dctx_copy(pair, k, slot):
+        cols = pl.ds(pl.multiple_of(me.s_to(k) * gw + pair * LANES, LANES), LANES)
+        return send_to(
+            dctx_ref.at[:, cols], do_s.at[pair, pl.ds(pl.multiple_of(slot * tok, tok), tok)],
+            sd.at[0, pair, k], sd.at[1, pair, k], d, me.s_to(k),
+        )
+
+    def dctx_own(pair):
+        cols = pl.ds(pl.multiple_of(s * gw + pair * LANES, LANES), LANES)
+        return pltpu.make_async_copy(
+            dctx_ref.at[:, cols], do_s.at[pair, pl.ds(pl.multiple_of(s * tok, tok), tok)],
+            sl.at[pair],
+        )
+
+    def pair_loads(pair):
+        return [
+            pltpu.make_async_copy(q_ref.at[pair], q_s, loc.at[0]),
+            pltpu.make_async_copy(ka_ref.at[pair], ka, loc.at[1]),
+            pltpu.make_async_copy(v_ref.at[pair], va.at[:, pl.ds(0, LANES)], loc.at[2]),
+            pltpu.make_async_copy(qx_ref.at[pair], qx, loc.at[3]),
+            pltpu.make_async_copy(o_ref.at[pair], o_s, loc.at[4]),
+        ]
+
+    tail_loads = [
+        pltpu.make_async_copy(hid_ref, hid, loc.at[5]),
+        pltpu.make_async_copy(wq_ref, wq, loc.at[6]),
+        pltpu.make_async_copy(vec_ref, vec, loc.at[7]),
+    ]
+
+    def part_of(p, core):
+        index, off, col = pieces[p]
+        ref = grads[index]
+        row = pl.multiple_of(core * (ref.shape[1] // 2) + off, 16)
+        return ref.at[:, pl.ds(row, size), pl.ds(col, wide)]
+
+    def core_copy(p):
+        return send_to(
+            part_of(p, 1 - me.c), c_land.at[p], sc.at[0, p], sc.at[1, p], d, me.cpeer
+        )
+
+    def core_landed(p):
+        return send_to(
+            c_land.at[p], c_land.at[p], sc.at[0, p], sc.at[1, p], d, me.cpeer
+        )
+
+    def own_load(p):
+        return pltpu.make_async_copy(part_of(p, me.c), own_b.at[p % 2], ld.at[0, p % 2])
+
+    def side_copy(p):
+        slot = lax.rem(p, 3)
+        return send_to(
+            s_b.at[slot, pl.ds(0, nz)], x_land.at[p], sx.at[0, p], sx.at[1, p], me.xpeer, s
+        )
+
+    def line_copy(p, k):
+        slot = lax.rem(p, 3)
+        return send_to(
+            t_b.at[slot, lax.rem(me.z + k, nz)], z_b.at[p, k], sz.at[0, p, k], sz.at[1, p, k],
+            me.z_to(k), s,
+        )
+
+    def up_copy(p, k):
+        return send_to(
+            u_b.at[p], y_b.at[p, k], sy.at[0, p, k], sy.at[1, p, k], d, me.y_to(k)
+        )
+
+    def fin_copy(p):
+        return send_to(
+            f_b.at[p], sum_out.at[p, me.c], sf.at[0, p], sf.at[1, p], d, me.cpeer
+        )
+
+    def fin_landed(p):
+        return send_to(
+            f_b.at[p], sum_out.at[p, 1 - me.c], sf.at[0, p], sf.at[1, p], d, me.cpeer
+        )
+
+    def fin_keep(p):
+        return pltpu.make_async_copy(f_b.at[p], sum_out.at[p, me.c], sg.at[p])
+
+    def e2_load(p):
+        own_load(p).start()
+        core_landed(p).wait_recv()
+        pltpu.make_async_copy(c_land.at[p], c_b.at[p % 2], ld.at[1, p % 2]).start()
+
+    def e2(p):
+        slot, two = lax.rem(p, 3), lax.rem(p, 2)
+        pltpu.make_async_copy(c_land.at[p], own_b.at[two], ld.at[0, two]).wait()
+        pltpu.make_async_copy(c_land.at[p], c_b.at[two], ld.at[1, two]).wait()
+
+        @pl.when(p >= 3)
+        def _():
+            side_copy(p - 3).wait_send()
+
+        def add(j, carry):
+            for part in range(2):
+                at = 2 * j + (1 - me.x if part == 0 else me.x)
+                total = own_b[two, at].astype(F32) + c_b[two, at].astype(F32)
+                s_b[slot, part * nz + j] = total.astype(LOW)
+            return carry
+
+        lax.fori_loop(0, nz, add, 0)
+        side_copy(p).start()
+
+    def e3(p):
+        slot = lax.rem(p, 3)
+        side_copy(p).wait_recv()
+        load = pltpu.make_async_copy(x_land.at[p], x_b, loc.at[8])
+        load.start()
+
+        @pl.when(p >= 3)
+        def _():
+            for k in range(1, nz):
+                line_copy(p - 3, k).wait_send()
+
+        load.wait()
+
+        def add(j, carry):
+            total = s_b[slot, nz + j].astype(F32) + x_b[j].astype(F32)
+            t_b[slot, j] = total.astype(LOW)
+            return carry
+
+        lax.fori_loop(0, nz, add, 0)
+        for k in range(1, nz):
+            line_copy(p, k).start()
+
+    def e4(p):
+        slot = lax.rem(p, 3)
+        for k in range(1, nz):
+            line_copy(p, k).wait_recv()
+        total = t_b[slot, me.z].astype(F32)
+        for k in range(1, nz):
+            total = total + z_b[p, k].astype(F32)
+        u_b[p] = total.astype(LOW)
+        for k in range(1, ny):
+            up_copy(p, k).start()
+
+    def e5(p):
+        for k in range(1, ny):
+            up_copy(p, k).wait_recv()
+        total = u_b[p].astype(F32)
+        for k in range(1, ny):
+            total = total + y_b[p, k].astype(F32)
+        f_b[p] = total.astype(LOW)
+        fin_copy(p).start()
+        fin_keep(p).start()
+
+    for pair in range(pairs):
+        dctx_own(pair).start()
+        for k in range(1, g):
+            dctx_copy(pair, k, s).start()
+    for copy in tail_loads:
+        copy.start()
+    for p in range(count):
+        core_copy(p).start()
+    lane_l = lax.broadcasted_iota(jnp.int32, (tok, LANES), 1)
+    for j in range(g):
+        va[j * tok : (j + 1) * tok, LANES:] = jnp.where(lane_l < 3, 1.0, 0.0).astype(LOW)
+
+    def t2(p):
+        return 2 * p + 2
+
+    def t3(p):
+        return (5 * p) // 2 + 6
+
+    def attend(step, carry):
+        pair = step // blocks
+        turn = lax.rem(step, blocks)
+        rel = turn // per
+        owner = lax.rem(s + g - rel, g)
+        block = owner * per + lax.rem(turn, per)
+
+        @pl.when(turn == 0)
+        def _():
+            loads = pair_loads(pair)
+            for copy in loads:
+                copy.start()
+            dk_acc[...] = jnp.zeros_like(dk_acc)
+            dv_acc[...] = jnp.zeros_like(dv_acc)
+            dctx_own(pair).wait()
+            for copy in loads:
+                copy.wait()
+            for j in range(length // chunk):
+                part = slice(j * chunk, (j + 1) * chunk)
+                kt[:, part] = ka[part, :LANES].astype(F32).T.astype(LOW)
+
+        for p in range(count):
+            @pl.when(step == t2(p) - 1)
+            def _(p=p):
+                e2_load(p)
+
+        for lag, event in ((0, e3), (3, e4), (5, e5)):
+            at = step - 6 - lag
+            p = (2 * jnp.maximum(at, 0) + 1) // 5
+            p = jnp.where((5 * p) // 2 == at, p, p + 1)
+
+            @pl.when((at >= 0) & ((5 * p) // 2 == at) & (p < count))
+            def _(p=p, event=event):
+                event(p)
+
+        @pl.when((lax.rem(step, 2) == 0) & (step >= 2) & (step < t2(count)))
+        def _():
+            e2((step - 2) // 2)
+
+        for k in range(1, g):
+            @pl.when(turn == k * per)
+            def _(k=k):
+                dctx_copy(pair, k, me.s_from(k)).wait_recv()
+
+        span = pl.ds(pl.multiple_of(block * rows, rows), rows)
+        lane = lax.broadcasted_iota(jnp.int32, (rows, LANES), 1)
+        queries = q_s[span, :].astype(F32) * SCALE
+        upstream = do_s[pair, span, :].astype(F32)
+        dots = upstream * o_s[span, :].astype(F32)
+        q_wide, g_wide, q_mask, g_mask = [], [], [], []
         for head in range(2):
-            probs = jnp.exp(matmul_right(ka_ref[part, :], q_wide[head]))
-            d_scores = (probs * matmul_right(va_ref[part, :], g_wide[head])).astype(LOW)
-            p_list.append(probs.astype(LOW))
-            ds_list.append(d_scores)
-            dq_t[head] = dq_t[head] + matmul(kt_ref[:, part], d_scores)
-        dv_acc[part, :] += matmul(jnp.concatenate(p_list, 1), g_rows)
-        dk_acc[part, :] += matmul(jnp.concatenate(ds_list, 1), q_rows)
-    row = lax.broadcasted_iota(jnp.int32, (LANES, rows), 0)
-    both = jnp.where(row < HEAD_DIM, dq_t[0], dq_t[1]) * SCALE
-    dq_ref[...] = both.T.astype(LOW)
-
-    @pl.when(step == pl.num_programs(0) - 1)
-    def _():
-        dk_ref[...] = dk_acc[...].astype(LOW)
-        dv_ref[...] = dv_acc[...].astype(LOW)
+            mask = head_mask(rows, head)
+            masked = jnp.where(mask, queries, 0.0).astype(LOW)
+            g_masked = jnp.where(mask, upstream, 0.0).astype(LOW)
+            delta = jnp.sum(jnp.where(mask, dots, 0.0), -1, keepdims=True)
+            first, second, third = thirds(delta)
+            extra = jnp.where(
+                lane == 0, -first, jnp.where(lane == 1, -second, jnp.where(lane == 2, -third, 0.0))
+            ).astype(LOW)
+            q_mask.append(masked)
+            g_mask.append(g_masked)
+            q_wide.append(jnp.concatenate([masked, qx[head, span, :]], 1))
+            g_wide.append(jnp.concatenate([g_masked, extra], 1))
+        q_rows = jnp.concatenate(q_mask, 0)
+        g_rows = jnp.concatenate(g_mask, 0)
+        dq_t = [jnp.zeros((LANES, rows), F32) for _ in range(2)]
+        for start in range(0, length, chunk):
+            part = slice(start, start + chunk)
+            p_list, ds_list = [], []
+            for head in range(2):
+                probs = jnp.exp(matmul_right(ka[part, :], q_wide[head]))
+                d_scores = (probs * matmul_right(va[part, :], g_wide[head])).astype(LOW)
+                p_list.append(probs.astype(LOW))
+                ds_list.append(d_scores)
+                dq_t[head] = dq_t[head] + matmul(kt[:, part], d_scores)
+            dv_acc[part, :] += matmul(jnp.concatenate(p_list, 1), g_rows)
+            dk_acc[part, :] += matmul(jnp.concatenate(ds_list, 1), q_rows)
+        row = lax.broadcasted_iota(jnp.int32, (LANES, rows), 0)
+        both = jnp.where(row < HEAD_DIM, dq_t[0], dq_t[1]) * SCALE
+        dh[pair, span, :] = both.T.astype(LOW)
+
+        @pl.when(turn == blocks - 1)
+        def _():
+            dh[pairs + pair] = dk_acc[...].astype(LOW)
+            dh[2 * pairs + pair] = dv_acc[...].astype(LOW)
+        return carry
+
+    lax.fori_loop(0, steps, attend, 0)
+    for copy in tail_loads:
+        copy.wait()
+    for p in range(count):
+        if t2(p) >= steps:
+            if t2(p) - 1 >= steps:
+                e2_load(p)
+            e2(p)
+
+    def heads_of(slot, tile):
+        span = pl.ds(pl.multiple_of(slot * tok + tile * rows, rows), rows)
+        return jnp.concatenate([dh[i, span, :] for i in range(3 * pairs)], 1)
+
+    def core_part(k):
+        slot = lax.rem(me.y + k, ny) * 2 + 1 - me.c
+
+        def tile_of(tile, carry):
+            span = pl.ds(pl.multiple_of(tile * rows, rows), rows)
+            part_c[k, span, :] = matmul_right(heads_of(slot, tile), wq[...]).astype(LOW)
+            return carry
+
+        lax.fori_loop(0, per, tile_of, 0)
+        part_copy(k).start()
+
+    def part_copy(k):
+        return send_to(part_c.at[k], part_k.at[k], sk.at[0, k], sk.at[1, k], d, me.cpeer)
+
+    def far_copy(k):
+        return send_to(
+            part_b.at[k - 1], part_y.at[k - 1], sgq.at[0, 0, k], sgq.at[1, 0, k], d, me.y_to(k)
+        )
+
+    for k in range(1, ny):
+        core_part(k)
+    core_part(0)
+    for k in range(1, ny):
+        part_copy(k).wait_recv()
+        slot = lax.rem(me.y + k, ny) * 2 + me.c
+
+        def far_tile(tile, carry, k=k, slot=slot):
+            span = pl.ds(pl.multiple_of(tile * rows, rows), rows)
+            total = matmul_right(heads_of(slot, tile), wq[...]) + part_k[k, span, :].astype(F32)
+            part_b[k - 1, span, :] = total.astype(LOW)
+            return carry
+
+        lax.fori_loop(0, per, far_tile, 0)
+        far_copy(k).start()
+
+    sums = [jnp.zeros((1, LANES), F32) for _ in range(3 * pairs)]
+    for i in range(3 * pairs):
+        for j in range(g):
+            span = slice(j * tok, (j + 1) * tok)
+            sums[i] = sums[i] + jnp.sum(dh[i, span, :].astype(F32), 0, keepdims=True)
+    sums = jnp.concatenate(sums, 1)
+    row16 = lax.broadcasted_iota(jnp.int32, (16, 3 * gw), 0)
+    for j in range(n):
+        q_b[j, deep:, :] = (vec[j].astype(F32) + jnp.where(row16 == 0, sums, 0.0)).astype(LOW)
+
+    def qx_copy(j):
+        return send_to(
+            q_b.at[2 * j + 1 - me.x], xq.at[j], sxq.at[0, j], sxq.at[1, j], me.xpeer, s
+        )
+
+    def qz_copy(k):
+        return send_to(
+            tq.at[lax.rem(me.z + k, nz)], zq.at[k], szq.at[0, k], szq.at[1, k], me.z_to(k), s
+        )
+
+    def q_out_copy(k, source):
+        return send_to(rq, sq_out.at[source], sgq.at[0, 1, k], sgq.at[1, 1, k], d, me.s_to(k))
+
+    tile_w = 256
+    for base in range(0, width, tile_w):
+        total = jnp.zeros((tile_w, 3 * gw), F32)
+        for j in range(g):
+            right = jnp.concatenate(
+                [dh[i, j * tok : (j + 1) * tok, :] for i in range(3 * pairs)], 1
+            )
+            total = total + matmul_left(hid[j, :, base : base + tile_w], right)
+        for at in range(0, tile_w, deep):
+            q_b[(base + at) // deep, :deep, :] = total[at : at + deep, :].astype(LOW)
+        for j in range(base // deep // 2, (base + tile_w) // deep // 2):
+            qx_copy(j).start()
+    remaining = count
+
+    def own_tile(tile, carry):
+        span = pl.ds(pl.multiple_of(tile * rows, rows), rows)
+        din[span, :] = matmul_right(heads_of(s, tile), wq[...])
+        return carry
+
+    lax.fori_loop(0, per, own_tile, 0)
+
+    for event, lag in ((e3, 0), (e4, 3), (e5, 5)):
+        for p in range(remaining):
+            if t3(p) + lag >= steps:
+                event(p)
+
+    for j in range(nz):
+        qx_copy(j).wait_recv()
+        kept = q_b[2 * j + me.x].astype(F32) + xq[j].astype(F32)
+        tq[j] = kept.astype(LOW)
+    for k in range(1, nz):
+        qz_copy(k).start()
+    part_copy(0).wait_recv()
+    for k in range(1, nz):
+        qz_copy(k).wait_recv()
+    total = tq[me.z].astype(F32)
+    for k in range(1, nz):
+        total = total + zq[k].astype(F32)
+    rq[...] = total.astype(LOW)
+    for k in range(1, g):
+        q_out_copy(k, s).start()
+    keep_q = pltpu.make_async_copy(rq, sq_out.at[s], loc.at[9])
+    keep_q.start()
+    for k in range(1, ny):
+        far_copy(k).wait_recv()
+
+    def sum_tile(tile, carry):
+        span = pl.ds(pl.multiple_of(tile * rows, rows), rows)
+        total = din[span, :] + part_k[0, span, :].astype(F32)
+        for k in range(1, ny):
+            total = total + part_y[k - 1, span, :].astype(F32)
+        din[span, :] = total
+        return carry
+
+    lax.fori_loop(0, per, sum_tile, 0)
+    keep_d = pltpu.make_async_copy(din, din_out, loc.at[10])
+    keep_d.start()
+
+    for p in range(count):
+        core_copy(p).wait_send()
+        fin_landed(p).wait_recv()
+        fin_copy(p).wait_send()
+        fin_keep(p).wait()
+        for k in range(1, ny):
+            up_copy(p, k).wait_send()
+        if p >= count - 3:
+            side_copy(p).wait_send()
+            for k in range(1, nz):
+                line_copy(p, k).wait_send()
+    for pair in range(pairs):
+        for k in range(1, g):
+            dctx_copy(pair, k, s).wait_send()
+    for k in range(ny):
+        part_copy(k).wait_send()
+    for k in range(1, ny):
+        far_copy(k).wait_send()
+    for j in range(nz):
+        qx_copy(j).wait_send()
+    for k in range(1, nz):
+        qz_copy(k).wait_send()
+    for k in range(1, g):
+        q_out_copy(k, me.s_from(k)).wait_recv()
+        q_out_copy(k, s).wait_send()
+    keep_q.wait()
+    keep_d.wait()
 
 
 def cost(length, matmuls):
@@ -553,115 +943,144 @@
     )
 
 
-def attend_backward(queries, keys, values, bias_wide, q_extra, context, context_grad):
-    length = queries.shape[0]
-    rows = 256
+def attend_backward(d_context, queries, keys, values, q_extra, context, hidden, w_heads, vecs,
+                    g_out, g_up, g_down):
+    n, g = lax.axis_size("dp"), lax.axis_size("seq")
+    tok, width = d_context.shape
+    length, gw, deep = tok * g, width // g, width // n
+    pairs = gw // LANES
+    nz, ny = n // 2, max(g // 2, 2)
+    wide = min(1024, width)
+    size = piece_rows(n)
+    shares = [g.reshape(n, -1, g.shape[1]) for g in (g_out, g_up, g_down)]
+    count = len(grad_pieces([share.shape[1:] for share in shares], n, wide))
+    anyw = pl.BlockSpec(memory_space=pl.ANY)
+    low = lambda *shape: jax.ShapeDtypeStruct(shape, LOW)
+    vmem = lambda *shape: pltpu.VMEM(shape, LOW)
+    vmem32 = lambda *shape: pltpu.VMEM(shape, F32)
+    dma = lambda *shape: pltpu.SemaphoreType.DMA(shape)
     chunk = 768 if length % 768 == 0 else 256
-    tile = pl.BlockSpec((rows, LANES), lambda i: (i, 0))
-    whole = pl.BlockSpec((length, LANES), lambda i: (0, 0))
+    tall = deep + 16
     return pl.pallas_call(
-        functools.partial(backward_kernel, chunk=chunk),
-        grid=(length // rows,),
+        functools.partial(backward_kernel, n=n, g=g, rows=256, chunk=chunk),
+        in_specs=[anyw] * 12,
+        out_specs=[anyw] * 5,
+        out_shape=[
+            jax.ShapeDtypeStruct((tok, width), F32), low(count, 2, size, wide),
+            low(g, tall, 3 * gw), low(count, n, size, wide), low(count, nz, size, wide),
+        ],
+        scratch_shapes=[
+            vmem(length, LANES), vmem(length, 2 * LANES), vmem(length, 2 * LANES),
+            vmem(LANES, length), vmem(2, length, LANES), vmem(length, LANES),
+            vmem(pairs, length, LANES), vmem(3 * pairs, length, LANES), vmem32(length, LANES),
+            vmem32(length, LANES), vmem(g, tok, width), vmem(width, 3 * gw), vmem(n, 16, 3 * gw),
+            vmem(ny, tok, width), vmem(ny, tok, width), vmem(ny - 1, tok, width),
+            vmem(ny - 1, tok, width), vmem32(tok, width),
+            vmem(2, n, size, wide), vmem(2, n, size, wide), vmem(3, n, size, wide),
+            vmem(nz, size, wide), vmem(3, nz, size, wide), vmem(count, nz, size, wide),
+            vmem(count, size, wide), vmem(count, ny, size, wide), vmem(count, size, wide),
+            vmem(n, tall, 3 * gw), vmem(nz, tall, 3 * gw), vmem(nz, tall, 3 * gw),
+            vmem(nz, tall, 3 * gw), vmem(tall, 3 * gw),
+            dma(11), dma(2, 2), dma(2, pairs, g), dma(2, ny), dma(2, count, ny), dma(2, count),
+            dma(2, count), dma(2, count, nz), dma(count), dma(2, count), dma(pairs), dma(2, nz),
+            dma(2, nz), dma(2, 2, g),
+        ],
+        compiler_params=pltpu.CompilerParams(
+            vmem_limit_bytes=63 * 2**20, collective_id=1, has_side_effects=True
+        ),
+        cost_estimate=cost(length, 10),
+    )(d_context, queries, keys, values, q_extra, context, hidden, w_heads, vecs, *shares)
+
+
+def gelu_parts(pre):
+    size = jnp.abs(pre)
+    t = 1.0 / (1.0 + (0.3275911 * 0.7071067811865476) * size)
+    bell = jnp.exp(-0.5 * pre * pre)
+    poly = t * (0.127414796 + t * (-0.142248368 + t * (
+        0.7107068705 + t * (-0.7265760135 + t * 0.5307027145))))
+    tail = poly * bell
+    phi = jnp.where(pre >= 0, 1.0 - tail, tail)
+    return phi, bell * 0.3989422804014327
+
+
+def up_kernel(x_ref, wu_ref, bu_ref, wd_ref, act_ref, slope_ref, sum_ref):
+    pre = matmul(x_ref[...], wu_ref[...]) + bu_ref[...]
+    phi, density = gelu_parts(pre)
+    activ = (pre * phi).astype(LOW)
+    act_ref[...] = activ
+    slope_ref[...] = (phi + pre * density).astype(LOW)
+    part = matmul(activ, wd_ref[...])
+
+    @pl.when(pl.program_id(0) == 0)
+    def _():
+        sum_ref[...] = part
+
+    @pl.when(pl.program_id(0) > 0)
+    def _():
+        sum_ref[...] += part
+
+
+def feed_forward(normed_low, w_up, bias_up, w_down):
+    tok, width = normed_low.shape
+    ff = w_up.shape[1]
+    tile = 512
+    whole = pl.BlockSpec((tok, width), lambda i: (0, 0))
+    col = pl.BlockSpec((tok, tile), lambda i: (0, i))
+    return pl.pallas_call(
+        up_kernel,
+        grid=(ff // tile,),
         in_specs=[
-            tile, whole, whole, pl.BlockSpec((LANES, length), lambda i: (0, 0)), whole,
-            pl.BlockSpec((2, rows, LANES), lambda i: (0, i, 0)), tile, tile,
+            whole, pl.BlockSpec((width, tile), lambda i: (0, i)),
+            pl.BlockSpec((1, tile), lambda i: (0, i)), pl.BlockSpec((tile, width), lambda i: (i, 0)),
         ],
-        out_specs=[tile, whole, whole],
-        out_shape=[jax.ShapeDtypeStruct((length, LANES), LOW)] * 3,
-        scratch_shapes=[pltpu.VMEM((length, 2 * LANES), LOW)] * 2
-        + [pltpu.VMEM((length, LANES), F32)] * 2,
+        out_specs=[col, col, whole],
+        out_shape=[
+            jax.ShapeDtypeStruct((tok, ff), LOW), jax.ShapeDtypeStruct((tok, ff), LOW),
+            jax.ShapeDtypeStruct((tok, width), F32),
+        ],
         compiler_params=pltpu.CompilerParams(vmem_limit_bytes=48 * 2**20),
-        cost_estimate=cost(length, 5),
-    )(queries, keys, values, keys.T, bias_wide, q_extra, context, context_grad)
-
-
-def swap(array, name, mask):
-    return lax.ppermute(array, name, [(i, i ^ mask) for i in range(lax.axis_size(name))])
-
-
-def bits(name):
-    return lax.axis_size(name).bit_length() - 1
-
-
-def bit_order(last):
-    dp_bits = [("dp", k) for k in reversed(range(bits("dp")))]
-    seq_bits = [("seq", k) for k in reversed(range(1, bits("seq")))]
-    order = dp_bits + seq_bits
-    if last in order:
-        order.remove(last)
-        order.append(last)
-    return order + [("seq", 0)]
-
-
-def place(name, k):
-    return bits("dp") - 1 - k if name == "dp" else bits("dp") + bits("seq") - 1 - k
-
-
-def my_bit(name, k):
-    return (lax.axis_index(name) >> k) & 1
-
-
-def double(array, name, k):
-    other = swap(array, name, 1 << k)
-    at = place(name, k)
-    return jnp.where(
-        my_bit(name, k) == 0,
-        jnp.concatenate([array, other], at),
-        jnp.concatenate([other, array], at),
-    )
-
-
-def reduce_weight(grad, last):
-    count = bits("dp") + bits("seq")
-    rows = grad.shape[0] >> count
-    part = grad.astype(LOW).reshape((2,) * count + (rows, grad.shape[1]))
-    for name, k in reversed(bit_order(last)):
-        mine = my_bit(name, k)
-        away = lax.dynamic_index_in_dim(part, 1 - mine, place(name, k))
-        keep = lax.dynamic_index_in_dim(part, mine, place(name, k))
-        part = (keep.astype(F32) + swap(away, name, 1 << k).astype(F32)).astype(LOW)
-    for k in reversed(range(bits("seq"))):
-        part = double(part, "seq", k)
-    return part.reshape(-1, grad.shape[1]).astype(F32)
-
-
-def scatter(part, name, order):
-    tail = part.shape[1:]
-    part = part.reshape((2,) * bits(name) + tail)
-    for k in order:
-        at = bits(name) - 1 - k
-        mine = my_bit(name, k)
-        away = lax.dynamic_index_in_dim(part, 1 - mine, at)
-        keep = lax.dynamic_index_in_dim(part, mine, at)
-        part = keep.astype(F32) + swap(away.astype(LOW), name, 1 << k).astype(F32)
-    return part.reshape(tail)
-
-
-def gather_seq(part):
-    part = part.reshape((1,) * bits("seq") + part.shape)
-    for k in reversed(range(bits("seq"))):
-        other = swap(part, "seq", 1 << k)
-        at = bits("seq") - 1 - k
-        part = jnp.where(
-            my_bit("seq", k) == 0,
-            jnp.concatenate([part, other], at),
-            jnp.concatenate([other, part], at),
-        )
-    return part.reshape((-1,) + part.shape[bits("seq"):])
-
-
-def exchange(blocks):
-    return [block if t == 0 else swap(block, "seq", t) for t, block in enumerate(blocks)]
-
-
-def by_index(blocks):
-    count = len(blocks)
-    me = lax.axis_index("seq")
-    return [lax.select_n(me, *[blocks[i ^ j] for i in range(count)]) for j in range(count)]
-
-
-def columns(array, group, pair, group_width):
-    return lax.dynamic_slice_in_dim(array, group * group_width + pair * LANES, LANES, 1)
+    )(normed_low, w_up, bias_up[None], w_down)
+
+
+def down_kernel(
+    x_ref, e_ref, wu_ref, wd_ref, act_ref, slope_ref, gu_ref, gd_ref, gb_ref, sum_ref,
+):
+    up = e_ref[...]
+    d_pre = matmul_right(up, wd_ref[...]) * slope_ref[...].astype(F32)
+    gb_ref[...] = jnp.sum(d_pre, 0, keepdims=True)
+    d_low = d_pre.astype(LOW)
+    gd_ref[...] = matmul_left(act_ref[...], up).astype(LOW)
+    gu_ref[...] = matmul_left(x_ref[...], d_low).astype(LOW)
+    part = matmul_right(d_low, wu_ref[...])
+
+    @pl.when(pl.program_id(0) == 0)
+    def _():
+        sum_ref[...] = part
+
+    @pl.when(pl.program_id(0) > 0)
+    def _():
+        sum_ref[...] += part
+
+
+def feed_backward(normed_low, d_low, w_up, w_down, activ, slope):
+    tok, width = normed_low.shape
+    ff = w_up.shape[1]
+    tile = 512
+    whole = pl.BlockSpec((tok, width), lambda i: (0, 0))
+    col = pl.BlockSpec((tok, tile), lambda i: (0, i))
+    up = pl.BlockSpec((width, tile), lambda i: (0, i))
+    down = pl.BlockSpec((tile, width), lambda i: (i, 0))
+    return pl.pallas_call(
+        down_kernel,
+        grid=(ff // tile,),
+        in_specs=[whole, whole, up, down, col, col],
+        out_specs=[up, down, pl.BlockSpec((1, tile), lambda i: (0, i)), whole],
+        out_shape=[
+            jax.ShapeDtypeStruct((width, ff), LOW), jax.ShapeDtypeStruct((ff, width), LOW),
+            jax.ShapeDtypeStruct((1, ff), F32), jax.ShapeDtypeStruct((tok, width), F32),
+        ],
+        compiler_params=pltpu.CompilerParams(vmem_limit_bytes=48 * 2**20),
+    )(normed_low, d_low, w_up, w_down, activ, slope)
 
 
 def own_columns(piece, width, group_width):
@@ -678,9 +1097,8 @@
     me = lax.axis_index("seq")
     tok_rows, width = hidden_in.shape
     group_width = width // groups
-    pairs = group_width // LANES
-    wide_y, wide_x, wide_z = ("seq", 1), ("dp", 0), ("dp", 1)
     deep = w_qkv.shape[0]
+    shares = lax.axis_size("dp")
 
     vectors = (
         bias_q, bias_v, bias_out, gain_attn, shift_attn, bias_down, gain_ffn, shift_ffn, bias_up,
@@ -698,12 +1116,11 @@
     blank = jnp.zeros((16 - 1 - packed.shape[0], 3 * group_width), LOW)
     chunk = jnp.concatenate([own_w, first_row, packed, blank], 0)
     bias_rows = jnp.broadcast_to(key_bias, (8, tok_rows))
-    (context, own_context, q_all, k_all, v_all, q_extra, hidden_all, w_heads, vec_all, f_w_out,
+    (context, own_context, q_all, ka_all, v_all, q_extra, hidden_all, w_heads, vec_all, f_w_out,
      f_w_up, f_w_down) = attend_forward(hidden_in, chunk, bias_rows, w_out, w_up, w_down)
     f_w_out = f_w_out.reshape(-1, w_out.shape[1])
     f_w_up = f_w_up.reshape(-1, w_up.shape[1])
     f_w_down = f_w_down.reshape(-1, w_down.shape[1])
-    hidden_all = hidden_all.reshape(-1, width)
     packed = vec_all[:, 1 : 1 + packed.shape[0]].reshape(vec_all.shape[0], -1).astype(F32)
     fulls, at = [], 0
     for vector in vectors:
@@ -711,15 +1128,12 @@
         at += vector.shape[0]
     (f_bias_q, f_bias_v, f_bias_out, f_gain_attn, f_shift_attn, f_bias_down, f_gain_ffn,
      f_shift_ffn, f_bias_up) = fulls
-    bias_col = jnp.concatenate(by_index(exchange([key_bias[0]] * groups)))
-    bias_wide = jnp.broadcast_to(bias_col[:, None], (bias_col.shape[0], LANES))
 
     attended = hidden_in.astype(F32) + matmul(context, f_w_out) + f_bias_out
     normed = layer_norm(attended, f_gain_attn, f_shift_attn)
     normed_low = normed.astype(LOW)
-    pre_act = matmul(normed_low, f_w_up) + f_bias_up
-    activ = gelu_exact(pre_act).astype(LOW)
-    branch_sum = normed + matmul(activ, f_w_down) + f_bias_down
+    activ, slope, branch = feed_forward(normed_low, f_w_up, f_bias_up, f_w_down)
+    branch_sum = normed + branch + f_bias_down
     output = layer_norm(branch_sum, f_gain_ffn, f_shift_ffn).astype(LOW)
 
     upstream = grad_out.astype(F32)
@@ -727,72 +1141,60 @@
     d_branch, g_gain_ffn, g_shift_ffn = norm_back(upstream)
     g_bias_down = jnp.sum(d_branch, 0)
     d_branch_low = d_branch.astype(LOW)
-    g_w_down = matmul_left(activ, d_branch_low).astype(LOW)
-    d_activ = matmul_right(d_branch_low, f_w_down)
-    _, gelu_back = jax.vjp(gelu_exact, pre_act)
-    d_pre = gelu_back(d_activ)[0]
-    g_bias_up = jnp.sum(d_pre, 0)
-    d_pre_low = d_pre.astype(LOW)
-    g_w_up = matmul_left(normed_low, d_pre_low).astype(LOW)
-    d_normed = d_branch + matmul_right(d_pre_low, f_w_up)
+    g_w_up, g_w_down, g_bias_up, d_up = feed_backward(
+        normed_low, d_branch_low, f_w_up, f_w_down, activ, slope
+    )
+    d_normed = d_branch + d_up
     _, attn_norm_back = jax.vjp(layer_norm, attended, f_gain_attn, f_shift_attn)
     d_attended, g_gain_attn, g_shift_attn = attn_norm_back(d_normed)
     g_bias_out = jnp.sum(d_attended, 0)
     d_attended_low = d_attended.astype(LOW)
     g_w_out = matmul_left(context, d_attended_low).astype(LOW)
     d_context = matmul_right(d_attended_low, f_w_out).astype(LOW)
-    d_context, g_w_down, g_w_up, g_w_out = lax.optimization_barrier(
-        (d_context, g_w_down, g_w_up, g_w_out)
+
+    vector_grads = (
+        g_bias_out, g_gain_attn, g_shift_attn, g_bias_down, g_gain_ffn, g_shift_ffn, g_bias_up,
     )
-    s_w_down = reduce_weight(g_w_down, wide_x)
-    s_w_up = reduce_weight(g_w_up, wide_y)
-    s_w_out = reduce_weight(g_w_out, wide_z)
-
-    grads = [[], [], []]
-    for pair in range(pairs):
-        got = jnp.concatenate(by_index(exchange(
-            [columns(d_context, me ^ t, pair, group_width) for t in range(groups)]
-        )))
-        done = attend_backward(
-            q_all[pair], k_all[pair], v_all[pair], bias_wide, q_extra[pair], own_context[pair], got
-        )
-        for i in range(3):
-            grads[i].append(done[i])
-    d_heads = jnp.concatenate(grads[0] + grads[1] + grads[2], 1)
-    d_in = matmul_right(d_heads, w_heads).astype(LOW).reshape(groups, tok_rows, width)
-    grad_in = d_attended + scatter(d_in, "seq", range(bits("seq")))
-    g_w_heads = matmul_left(hidden_all, d_heads).astype(LOW)
-    s_w_heads = scatter(
-        g_w_heads.reshape(-1, deep, 3 * group_width), "dp", range(bits("dp"))
-    ).astype(LOW)
-    s_w_qkv = gather_seq(s_w_heads).reshape(groups, deep, 3, group_width)
+    rows = jnp.concatenate([g.reshape(shares, -1) for g in vector_grads], 1).astype(LOW)
+    filled = rows.shape[1]
+    tall = -(-filled // (3 * group_width))
+    vecs = jnp.pad(rows, ((0, 0), (0, tall * 3 * group_width - filled)))
+    vecs = jnp.pad(vecs.reshape(shares, tall, -1), ((0, 0), (1, 15 - tall), (0, 0)))
+    d_in, sums, heads, _, _ = attend_backward(
+        d_context, q_all, ka_all, v_all, q_extra, own_context, hidden_all, w_heads, vecs,
+        g_w_out, g_w_up, g_w_down,
+    )
+    grad_in = d_attended + d_in
+    own_sums = []
+    wide, size = sums.shape[3], sums.shape[2]
+    pieces = grad_pieces([w.shape for w in (w_out, w_up, w_down)], shares, wide)
+    for index, w in enumerate((w_out, w_up, w_down)):
+        mine = [p for p, piece in enumerate(pieces) if piece[0] == index]
+        part = sums[mine[0] : mine[-1] + 1].reshape(
+            -1, w.shape[1] // wide, 2, size, wide
+        )
+        own_sums.append(part.transpose(2, 0, 3, 1, 4).reshape(w.shape).astype(F32))
+    s_w_out, s_w_up, s_w_down = own_sums
+    s_w_qkv = heads[:, :deep].reshape(groups, deep, 3, group_width)
     s_w_qkv = s_w_qkv.transpose(1, 2, 0, 3).reshape(deep, -1).astype(F32)
-    head_sums = jnp.sum(d_heads.astype(F32), 0)
-    zero = jnp.zeros((width,), F32)
-    g_bias_q = lax.dynamic_update_slice_in_dim(zero, head_sums[:group_width], me * group_width, 0)
-    g_bias_v = lax.dynamic_update_slice_in_dim(
-        zero, head_sums[2 * group_width :], me * group_width, 0
+    head_rows = heads[:, deep].astype(F32)
+    at = lax.axis_index("dp") * bias_q.shape[0]
+    s_bias_q = lax.dynamic_slice_in_dim(
+        head_rows[:, :group_width].reshape(-1), at, bias_q.shape[0], 0
     )
-
-    vector_grads = (
-        g_bias_q, g_bias_v, g_bias_out, g_gain_attn, g_shift_attn, g_bias_down, g_gain_ffn,
-        g_shift_ffn, g_bias_up,
+    s_bias_v = lax.dynamic_slice_in_dim(
+        head_rows[:, 2 * group_width :].reshape(-1), at, bias_v.shape[0], 0
     )
-    shares = lax.axis_size("dp")
-    rows = jnp.concatenate([g.reshape(shares, -1) for g in vector_grads], 1).astype(LOW)
-    own = lax.dynamic_index_in_dim(
-        lax.psum(rows, ("dp", "seq")), lax.axis_index("dp"), 0, False
-    ).astype(F32)
-    sums, at = [], 0
-    for vector in vectors:
-        sums.append(own[at : at + vector.shape[0]])
+    own = jnp.sum(heads[:, deep + 1 : deep + 1 + tall].astype(F32), 0).reshape(-1)
+    own_vectors, at = [], 0
+    for vector in vectors[2:]:
+        own_vectors.append(own[at : at + vector.shape[0]])
         at += vector.shape[0]
-    (s_bias_q, s_bias_v, s_bias_out, s_gain_attn, s_shift_attn, s_bias_down, s_gain_ffn,
-     s_shift_ffn, s_bias_up) = sums
+    (s_bias_out, s_gain_attn, s_shift_attn, s_bias_down, s_gain_ffn, s_shift_ffn,
+     s_bias_up) = own_vectors
     return (
-        output, grad_in, s_w_qkv, s_bias_q, s_bias_v, s_w_out,
-        s_bias_out, s_gain_attn, s_shift_attn, s_w_up, s_bias_up, s_w_down, s_bias_down,
-        s_gain_ffn, s_shift_ffn,
+        output, grad_in, s_w_qkv, s_bias_q, s_bias_v, s_w_out, s_bias_out, s_gain_attn,
+        s_shift_attn, s_w_up, s_bias_up, s_w_down, s_bias_down, s_gain_ffn, s_shift_ffn,
     )
 
 

time: 768 us -> 542 us (0.71)
  Pallas kernels: 286 us -> 470 us
  waiting for transfers between devices: 131 us -> 0 us
  matrix products: 124 us -> 11.6 us
  starting transfers between devices: 51.3 us -> 0 us
  blocking collectives: 47.3 us -> 0 us
  local copies, waits for them, and re-layouts: 67.1 us -> 24.5 us
  other arithmetic: 51.4 us -> 24.8 us
    pallas_call x2 -> x3, Pallas kernels: 117 us -> 306 us  [the longest x1 244 us: attend_backward(): pl.pallas_call(functools.partial(backward_kernel, n=n, g=g, rows=256, chu...]
    ppermute x37 -> x0, waiting for transfers between devices: 131 us -> none  [swap(): lax.ppermute(array, name, [(i, i ^ mask) for i in range(lax.axis_size(nam...]
    ppermute x37 -> x0, starting transfers between devices: 51.3 us -> none  [swap(): lax.ppermute(array, name, [(i, i ^ mask) for i in range(lax.axis_size(nam...]
    dot_general x3 -> x1, matrix products: 52.1 us -> 3.99 us  [matmul(): return jnp.dot(left, right, preferred_element_type=F32)]
    psum x1 -> x0, blocking collectives: 47.3 us -> none  [local(): lax.psum(rows, ('dp', 'seq'))]
    dot_general x4 -> x1, matrix products: 43.3 us -> 2.98 us  [matmul_right(): lax.dot_general(left, right, (((1,), (1,)), ((), ())), preferred_element_...]
    dot_general x4 -> x1, matrix products: 28.6 us -> 4.62 us  [matmul_left(): lax.dot_general(left, right, (((0,), (0,)), ((), ())), preferred_element_...]
    dynamic_slice x18 -> x2, local copies, waits for them, and re-layouts: 20.1 us -> 1.17 us  [the longest x1 0.59 us: local(): lax.dynamic_slice_in_dim(head_rows[:, :group_width].reshape(-1), at, bias...]
  transfers between devices with their start and end apart: 37 -> 0, of which waited for: 14 -> 0; matrix products, arithmetic and copies ran while one was open for 31% -> 0% of each run, Pallas kernels for 38% -> 0%
where the time goes in v2:
time: 542 us; the launch traced here: 533 us
  Pallas kernels  470 us (87%)
  other arithmetic  24.8 us (5%)
  local copies, waits for them, and re-layouts  24.5 us (5%)
  matrix products  11.6 us (2%)
    pallas_call x1, Pallas kernels, attend_backward(): pl.pallas_call(functools.partial(backward_kernel, n=n, g=g, rows=256, chu...  244 us
    pallas_call x1, Pallas kernels, attend_forward(): pl.pallas_call(functools.partial(forward_kernel, n=n, g=g, rows=256), in_...  164 us
    pallas_call x1, Pallas kernels, feed_backward(): pl.pallas_call(down_kernel, grid=(ff // tile,), in_specs=[whole, whole, u...  34.6 us
    pallas_call x1, Pallas kernels, feed_forward(): pl.pallas_call(up_kernel, grid=(ff // tile,), in_specs=[whole, pl.BlockSp...  27.7 us
    unnamed x33, local copies, waits for them, and re-layouts  12.9 us

profile of v2, /device:TPU:11, one launch (start us, length us, event | category | flops | bytes accessed | tf_op | source)
XLA Modules:
  0.0 532.7 jit_solution(14463222413303412928)
XLA Ops:
  0.7 0.9 dynamic-update-slice.7
  1.5 0.8 dynamic-update-slice.8
  2.3 0.8 dynamic-update-slice.9
  3.2 0.8 dynamic-update-slice.10
  4.0 0.8 dynamic-update-slice.11
  4.8 0.8 dynamic-update-slice.12
  5.7 0.8 dynamic-update-slice.13
  6.5 0.8 dynamic-update-slice.14
  7.3 0.7 constant_dynamic-update-slice_fusion.7
  8.1 0.8 dynamic_update_slice.7
  8.9 0.1 dynamic_slice.25
  9.0 0.8 dynamic_update_slice.6
  9.8 0.1 dynamic_slice.24
  9.9 0.9 constant_dynamic-slice_fusion.2
  10.9 0.1 pad.15.clone
  10.9 0.8 maximum_maximum_fusion.wch_ref
  11.7 0.7 reduce.1
  12.4 0.6 broadcast_in_dim.40.kb_ref
  13.1 163.9 %shard_map.271 = (bf16[768,1024]{1,0:T(8,128)(2,1)}, bf16[2,3072,128]{2,1,0:T(8,128)(2,1)}, bf16[2,3072,128]{2,1,0:T(8,128)(2,1)}, bf16[2,3072,256]{2,1,0:T(8,12...) custom-call(bf16[768,1024]{1,0:T(8,128)(2,1)} %hid_ref.1, ...), custom_call_target="tpu_custom_call" | custom-call | flops 38654705664 | bytes 7864320 | tf_op jit(solution)/shard_map/pallas_call | solution.py:466
  177.0 0.9 convert_bitcast_fusion.2
  177.9 0.0 copy-done.3
  177.9 4.0 fusion.11
  181.9 0.4 multiply_reduce_fusion.3
  182.4 0.6 fusion.4.x_ref
  183.0 27.7 %shard_map.272 = (bf16[768,4096]{1,0:T(8,128)(2,1)}, bf16[768,4096]{1,0:T(8,128)(2,1)}, f32[768,1024]{1,0:T(8,128)S(1)}) custom-call(bf16[768,1024]{1,0:T(8,128)(2,1)S(1)} %fusion.4.x_ref, bf16[1024,4096]{1,0:T(8,128)(2,1)} %bitcast.73, f32[1,4096]{1,0:T(1,128)S(1)} %bitcast.72, bf16[4096,1024]{1,0:T(8,128)(2,1)} %bitcast.75), custom_call_target="tpu_custom_call" | custom-call | tf_op jit(solution)/shard_map/pallas_call | solution.py:1029
  210.7 1.0 fusion.9
  211.7 0.0 copy-start.1
  211.8 0.4 multiply_reduce_fusion.2
  212.2 0.9 copy-done.1
  213.2 1.2 fusion.3
  214.4 2.6 fusion.8
  217.0 0.3 add_reduce_fusion.1
  217.3 34.6 %shard_map.273 = (bf16[1024,4096]{1,0:T(8,128)(2,1)}, bf16[4096,1024]{1,0:T(8,128)(2,1)}, f32[1,4096]{1,0:T(1,128)S(1)}, f32[768,1024]{1,0:T(8,128)}) custom-call(bf16[768,1024]{1,0:T(8,128)(2,1)S(1)} %fusion.4.x_ref, bf16[768,1024]{1,0:T(8,128)(2,1)S(1)} %get-tuple-element.88.e_ref, bf16[1024,4096]{1,0:T(8,128)(2,1)} %bitcast.74, ...), custom_call_target="tpu_custom_call" | custom-call | tf_op jit(solution)/shard_map/pallas_call | solution.py:1073
  252.0 3.3 multiply_reduce_fusion
  255.2 0.0 copy-start.4
  255.2 0.9 fusion.7
  256.2 0.0 copy-start
  256.2 0.6 copy-done.4
  256.8 3.0 convolution_convert_fusion.1.dctx_ref
  259.8 0.3 add_reduce_fusion
  260.2 1.7 reduce
  261.9 0.1 convert_reduce_fusion.1
  262.0 0.7 pad.9.vec_ref
  262.7 0.0 copy-done
  262.7 4.6 convolution_convert_fusion
  267.3 244.0 %shard_map.274 = (f32[768,1024]{1,0:T(8,128)}, bf16[9,2,64,1024]{3,2,1,0:T(8,128)(2,1)}, bf16[4,144,768]{2,1,0:T(8,128)(2,1)}, bf16[9,8,64,1024]{3,2,1,0:T(8,128)(2,1)}, bf16[9,4,64,1024]{3,2,1,0:T(8,128)(2,1)}) custom-call(bf16[768,1024]{1,0:T(8,128)(2,1)} %convolution_convert_fusion.1.dctx_ref, bf16[2,3072,128]{2,1,0:T(8,128)(2,1)} %get-tuple-element.46.q_ref, ...), custom_call_target="tpu_custom_call" | custom-call | flops 96636764160 | bytes 7864320 | tf_op jit(solution)/shard_map/pallas_call | solution.py:964
  511.4 0.0 copy-start.2
  511.4 5.0 add_add_fusion.4
  516.3 0.1 slice_convert_fusion
  516.4 0.5 copy.35
  516.9 0.1 copy.36
  517.0 1.6 copy.39
  518.7 0.8 slice_convert_fusion.1
  519.5 0.6 dynamic_slice.26
  520.1 0.6 dynamic_slice.27
  520.7 1.0 slice.81
  521.6 0.9 bitcast_convert_fusion
  522.5 0.8 convert_reduce_fusion
  523.3 0.5 fusion.10
  523.9 2.0 convert_bitcast_fusion
  525.9 1.4 copy.37
  527.2 3.0 copy.45
  530.2 0.6 slice.104
  530.8 1.5 copy.38
  (37 shorter events, 0.3 us)
Async XLA Ops:
  13.1 164.9 %copy-start.3 = (bf16[768,1024]{1,0:T(8,128)(2,1)S(1)}, bf16[768,1024]{1,0:T(8,128)(2,1)}, u32[]{:S(2)}) copy-start(bf16[768,1024]{1,0:T(8,128)(2,1)} %hid_ref.1) | copy-start | bytes 4718596
  211.7 1.4 copy-start.1
  255.2 1.6 copy-start.4
  256.2 6.5 %copy-start = (f32[768,1024]{1,0:T(8,128)}, f32[768,1024]{1,0:T(8,128)S(1)}, u32[]{:S(2)}) copy-start(f32[768,1024]{1,0:T(8,128)S(1)} %get-tuple-element.80) | copy-start | bytes 9437188
  511.4 5.0 copy-start.2

commit v3 on v2

--- a/solution.py
+++ b/solution.py
@@ -11,6 +11,7 @@
 LANES = 128
 SCALE = HEAD_DIM**-0.5
 norm_eps = 1e-05
+PIECE_GAP = 3.5
 F32 = jnp.float32
 LOW = jnp.bfloat16
 
@@ -101,25 +102,22 @@
         pl.semaphore_wait(sem, len(targets))
 
 
-def pieces_of(half):
-    return 2 if half % 64 == 0 and half >= 64 else 1
-
-
-def weight_pieces(shapes):
+def weight_pieces(shapes, g):
     out = []
-    for index, rows in enumerate(shapes):
-        half = rows // 2
-        count = pieces_of(half) if index else 1
-        for part in range(count):
-            out.append((index, part * (half // count), half // count))
-    return out
+    for index, (rows, cols) in enumerate(shapes):
+        quarter = rows % (16 * g) == 0 and index == 2
+        own = rows // g if quarter else rows // 2
+        size = min(own, max(16, 65536 // cols))
+        for off in range(0, own, size):
+            out.append((index, off, size, own, quarter))
+    return sorted(out, key=lambda piece: not piece[4])
 
 
 def forward_kernel(
     hid_ref, wch_ref, kb_ref, wo_ref, wu_ref, wd_ref,
     ctx_out, own_ctx, q_out, ka_out, v_out, qx_out, hid_out, wq_out, vec_out, wo_out, wu_out, wd_out,
     hid, wch, wq, kb, q_s, k_s, v_s, ka, va, ctx, qx,
-    loc, hy, hc, hf, kbs, wz, wx, pz, px, pc, cs, kx,
+    loc, hy, hc, hf, kbs, wz, wx, pz, px, pc, py, pf, cs, kx,
     *, n, g, rows,
 ):
     me = Peers(n, g)
@@ -132,7 +130,7 @@
     cut = tok // 3
     shards = (wo_ref, wu_ref, wd_ref)
     fulls = (wo_out, wu_out, wd_out)
-    pieces = weight_pieces([ref.shape[0] for ref in shards])
+    pieces = weight_pieces([ref.shape for ref in shards], g)
     me.barrier()
 
     local = [
@@ -187,36 +185,59 @@
     for copy in keep:
         copy.start()
 
-    def span_of(p):
-        index, off, size = pieces[p]
-        return index, pl.ds(pl.multiple_of(me.c * (shards[index].shape[0] // 2) + off, 16), size)
-
-    def other_span(p):
-        index, off, size = pieces[p]
-        return index, pl.ds(
-            pl.multiple_of((1 - me.c) * (shards[index].shape[0] // 2) + off, 16), size
-        )
+    def span_of(p, seq):
+        index, off, size, own, quarter = pieces[p]
+        part = seq if quarter else lax.rem(seq, 2)
+        return index, pl.ds(pl.multiple_of(part * own + off, 16), size)
+
+    def block_of(k, side):
+        slot = me.z_from(k) if k else d
+        if side:
+            slot = me.side(slot)
+        return slot
 
     def pz_copy(p, k, slot):
-        index, span = span_of(p)
+        index, span = span_of(p, s)
         return send_to(
             shards[index].at[span], fulls[index].at[slot, span], pz.at[0, p, k], pz.at[1, p, k],
             me.z_to(k), s,
         )
 
     def px_copy(p, k, slot):
-        index, span = span_of(p)
+        index, span = span_of(p, s)
         src = shards[index].at[span] if k == 0 else fulls[index].at[slot, span]
         return send_to(
             src, fulls[index].at[slot, span], px.at[0, p, k], px.at[1, p, k], me.xpeer, s
         )
 
-    def pc_copy(p, k, side, slot, mine):
-        index, span = span_of(p) if mine else other_span(p)
-        return send_to(
-            fulls[index].at[slot, span], fulls[index].at[slot, span], pc.at[0, p, k, side],
-            pc.at[1, p, k, side], d, me.cpeer,
-        )
+    def pc_copy(p, k, side, seq):
+        index, span = span_of(p, seq)
+        ref = fulls[index].at[block_of(k, side), span]
+        return send_to(
+            ref, ref, pc.at[0, p, k, side], pc.at[1, p, k, side], d, me.cpeer
+        )
+
+    def py_copy(p, j, k, side, seq):
+        index, span = span_of(p, seq)
+        ref = fulls[index].at[block_of(k, side), span]
+        return send_to(
+            ref, ref, py.at[0, p, j, k, side], py.at[1, p, j, k, side], d, me.y_to(j)
+        )
+
+    def pf_copy(p, j, k, side, seq):
+        index, span = span_of(p, seq)
+        ref = fulls[index].at[block_of(k, side), span]
+        return send_to(
+            ref, ref, pf.at[0, p, j, k, side], pf.at[1, p, j, k, side], d, me.cpeer
+        )
+
+    moves = [(k, 0) for k in range(1, nz)] + [(k, 1) for k in range(nz)]
+
+    def spread(p, k, side):
+        if pieces[p][4]:
+            for j in range(1, ny):
+                py_copy(p, j, k, side, s).start()
+        pc_copy(p, k, side, s).start()
 
     def piece_send(p):
         for k in range(1, nz):
@@ -228,25 +249,33 @@
             slot = me.z_from(k)
             pz_copy(p, k, slot).wait_recv()
             px_copy(p, k, slot).start()
-            pc_copy(p, k, 0, slot, True).start()
+            spread(p, k, 0)
 
     def piece_share(p):
         for k in range(nz):
-            slot = me.side(me.z_from(k)) if k else me.xpeer
-            px_copy(p, k, slot).wait_recv()
-            pc_copy(p, k, 1, slot, True).start()
+            px_copy(p, k, block_of(k, 1)).wait_recv()
+            spread(p, k, 1)
+
+    def piece_far(p):
+        if pieces[p][4]:
+            for j in range(1, ny):
+                for k, side in moves:
+                    py_copy(p, j, k, side, me.y_from(j)).wait_recv()
+                    pf_copy(p, j, k, side, me.y_from(j)).start()
 
     def piece_end(p):
-        for k in range(1, nz):
-            pc_copy(p, k, 0, me.z_from(k), False).wait_recv()
-        for k in range(nz):
-            pc_copy(p, k, 1, me.side(me.z_from(k)) if k else me.xpeer, False).wait_recv()
+        for k, side in moves:
+            pc_copy(p, k, side, me.cpeer).wait_recv()
+            pc_copy(p, k, side, s).wait_send()
+            if pieces[p][4]:
+                for j in range(1, ny):
+                    pf_copy(p, j, k, side, c_of_y(j)).wait_recv()
+                    pf_copy(p, j, k, side, me.y_from(j)).wait_send()
+                    py_copy(p, j, k, side, s).wait_send()
         for k in range(1, nz):
             pz_copy(p, k, d).wait_send()
-            pc_copy(p, k, 0, me.z_from(k), True).wait_send()
         for k in range(nz):
-            px_copy(p, k, me.z_from(k) if k else d).wait_send()
-            pc_copy(p, k, 1, me.side(me.z_from(k)) if k else me.xpeer, True).wait_send()
+            px_copy(p, k, block_of(k, 0)).wait_send()
 
     for k in range(1, nz):
         slot = me.z_from(k)
@@ -283,6 +312,8 @@
         for k in range(1, ny):
             @pl.when(step == 2 * k * tiles)
             def _(k=k):
+                if k == 1 and len(pieces) > 2:
+                    piece_send(2)
                 for sub in range(3):
                     y_copy(k, sub, me.y_from(k)).wait_recv()
                     f_copy(k, sub, me.y_from(k)).start()
@@ -339,12 +370,14 @@
         return pltpu.make_async_copy(ka, ka_out.at[pair], loc.at[10])
 
     events = {}
-    every = max(1, steps // (len(pieces) + 1))
+    gap = PIECE_GAP
     for p in range(len(pieces)):
-        if p >= 2:
-            events.setdefault((p - 2) * every, []).append(lambda p=p: piece_send(p))
-        events.setdefault((p + 1) * every - 1, []).append(lambda p=p: piece_pass(p))
-        events.setdefault((p + 1) * every + 1, []).append(lambda p=p: piece_share(p))
+        if p >= 3:
+            events.setdefault(int(gap * (p - 3)), []).append(lambda p=p: piece_send(p))
+        at = int(max(0, gap * (p - 1) + 1))
+        events.setdefault(at, []).append(lambda p=p: piece_pass(p))
+        events.setdefault(at + 3, []).append(lambda p=p: piece_share(p))
+        events.setdefault(at + 7, []).append(lambda p=p: piece_far(p))
     late = [e for t in sorted(events) if t >= steps for e in events[t]]
 
     def attend(step, carry):
@@ -451,7 +484,7 @@
     tok, width = hidden.shape
     length, gw, deep = tok * g, width // g, width // n
     pairs = gw // LANES
-    count = len(weight_pieces([w.shape[0] for w in (w_out, w_up, w_down)]))
+    count = len(weight_pieces([w.shape for w in (w_out, w_up, w_down)], g))
     anyw = pl.BlockSpec(memory_space=pl.ANY)
     low = lambda *shape: jax.ShapeDtypeStruct(shape, LOW)
     out_shape = [
@@ -474,8 +507,8 @@
             vmem((pairs, length, LANES)), vmem((length, 2 * LANES)), vmem((length, 2 * LANES)),
             vmem((pairs, length, LANES)), vmem((pairs, 2, length, LANES)),
             dma(14), dma(2, ny, 3), dma(2), dma(2, ny, 3), dma(2, g), dma(2, nz), dma(2, nz),
-            dma(2, count, nz), dma(2, count, nz), dma(2, count, nz, 2), dma(2, pairs, g),
-            dma(pairs),
+            dma(2, count, nz), dma(2, count, nz), dma(2, count, nz, 2),
+            dma(2, count, ny, nz, 2), dma(2, count, ny, nz, 2), dma(2, pairs, g), dma(pairs),
         ],
         compiler_params=pltpu.CompilerParams(
             vmem_limit_bytes=56 * 2**20, collective_id=0, has_side_effects=True
@@ -488,25 +521,53 @@
     return max(16, 512 // n)
 
 
-def grad_pieces(shapes, n, wide):
-    out = []
+def grad_pieces(shapes, n, g, wide):
+    halves, quarters = [], []
     for index, (rows, cols) in enumerate(shapes):
-        half = rows // 2
-        size = min(half, piece_rows(n))
-        for off in range(0, half, size):
+        quarter = rows % (16 * g) == 0 and index == 2
+        own = rows // g if quarter else rows // 2
+        size = min(own, piece_rows(n))
+        for off in range(0, own, size):
             for col in range(0, cols, wide):
-                out.append((index, off, col))
-    return out
+                (quarters if quarter else halves).append((index, off, col, quarter))
+    out = halves[:3]
+    rest = halves[3:]
+    for piece in quarters:
+        out.append(piece)
+        out += rest[:1]
+        rest = rest[1:]
+    return out + rest
+
+
+def grad_times(pieces):
+    times, lines, x_free, z_free = [], [], 0.0, 0.0
+    y_free = 5.0
+    at = 2
+    for piece in pieces:
+        first = None
+        if piece[3]:
+            first = 3 if not lines else lines[-1] + 2
+            lines.append(first)
+            y_free = max(y_free, first) + 5.0
+            at = max(at, int(y_free) + 1)
+        start = max(at, int(x_free - 1.0))
+        x_free = max(x_free, start) + 2.5
+        side = int(x_free + 0.9)
+        z_free = max(z_free, side) + 2.5
+        line = int(z_free + 0.9)
+        times.append((first, start, side, line, line + 2))
+        at = start + 2
+    return times
 
 
 def backward_kernel(
     dctx_ref, q_ref, ka_ref, v_ref, qx_ref, o_ref, hid_ref, wq_ref, vec_ref, go_ref, gu_ref,
     gd_ref,
-    din_out, sum_out, sq_out, c_land, x_land,
+    din_out, so_out, su_out, sd_out, sq_out, extra_out, c_land, x_land,
     q_s, ka, va, kt, qx, o_s, do_s, dh, dk_acc, dv_acc, hid, wq, vec,
     part_c, part_k, part_y, part_b, din, own_b, c_b, s_b, x_b, t_b, z_b, u_b, y_b, f_b,
-    q_b, xq, tq, zq, rq,
-    loc, ld, sd, sk, sy, sc, sx, sz, sg, sf, sl, sxq, szq, sgq,
+    q_b, xq, tq, zq, rq, far_b, far_l,
+    loc, ld, sd, sk, sy, sc, sx, sz, sg, sf, sl, sxq, szq, sgq, sfar, sfr,
     *, n, g, rows, chunk,
 ):
     me = Peers(n, g)
@@ -519,8 +580,16 @@
     grads = (go_ref, gu_ref, gd_ref)
     wide = own_b.shape[3]
     size = own_b.shape[2]
-    pieces = grad_pieces([ref.shape[1:] for ref in grads], n, wide)
+    outs = (so_out, su_out, sd_out)
+    pieces = grad_pieces([ref.shape[1:] for ref in grads], n, g, wide)
+    times = grad_times(pieces)
     count = len(pieces)
+    lands, spots = [], {}
+    for p, piece in enumerate(pieces):
+        for r in range(ny if piece[3] else 1):
+            spots[p, r] = len(lands)
+            lands.append((p, r))
+    fars = [p for p in range(count) if pieces[p][3]]
     blocks = length // rows
     per = tok // rows
     steps = pairs * blocks
@@ -555,35 +624,47 @@
         pltpu.make_async_copy(vec_ref, vec, loc.at[7]),
     ]
 
-    def part_of(p, core):
-        index, off, col = pieces[p]
-        ref = grads[index]
-        row = pl.multiple_of(core * (ref.shape[1] // 2) + off, 16)
-        return ref.at[:, pl.ds(row, size), pl.ds(col, wide)]
-
-    def core_copy(p):
-        return send_to(
-            part_of(p, 1 - me.c), c_land.at[p], sc.at[0, p], sc.at[1, p], d, me.cpeer
-        )
-
-    def core_landed(p):
-        return send_to(
-            c_land.at[p], c_land.at[p], sc.at[0, p], sc.at[1, p], d, me.cpeer
-        )
-
-    def own_load(p):
-        return pltpu.make_async_copy(part_of(p, me.c), own_b.at[p % 2], ld.at[0, p % 2])
+    def row_of(p, core, y_at):
+        index, off, col, quarter = pieces[p]
+        own = grads[index].shape[1] // 2
+        at = core * own + off
+        if quarter:
+            at = at + y_at * (own // ny)
+        return pl.multiple_of(at, 16)
+
+    def part_of(p, r, core):
+        index, off, col, quarter = pieces[p]
+        row = row_of(p, core, lax.rem(me.y + r, ny))
+        return grads[index].at[:, pl.ds(row, size), pl.ds(col, wide)]
+
+    def core_copy(p, r):
+        i = spots[p, r]
+        return send_to(
+            part_of(p, r, 1 - me.c), c_land.at[i], sc.at[0, i], sc.at[1, i], d, me.cpeer
+        )
+
+    def own_load(p, r):
+        i = spots[p, r] % 2
+        return pltpu.make_async_copy(part_of(p, r, me.c), own_b.at[i], ld.at[0, i])
+
+    def core_load(p, r):
+        i = spots[p, r] % 2
+        return pltpu.make_async_copy(c_land.at[spots[p, r]], c_b.at[i], ld.at[1, i])
+
+    def y_copy(p, r):
+        i = fars.index(p)
+        return send_to(
+            far_b.at[i], far_l.at[i, r - 1], sfar.at[0, i, r], sfar.at[1, i, r], d, me.y_to(r)
+        )
 
     def side_copy(p):
-        slot = lax.rem(p, 3)
-        return send_to(
-            s_b.at[slot, pl.ds(0, nz)], x_land.at[p], sx.at[0, p], sx.at[1, p], me.xpeer, s
+        return send_to(
+            s_b.at[p % 3, pl.ds(0, nz)], x_land.at[p], sx.at[0, p], sx.at[1, p], me.xpeer, s
         )
 
     def line_copy(p, k):
-        slot = lax.rem(p, 3)
-        return send_to(
-            t_b.at[slot, lax.rem(me.z + k, nz)], z_b.at[p, k], sz.at[0, p, k], sz.at[1, p, k],
+        return send_to(
+            t_b.at[p % 3, lax.rem(me.z + k, nz)], z_b.at[p, k - 1], sz.at[0, p, k], sz.at[1, p, k],
             me.z_to(k), s,
         )
 
@@ -592,37 +673,57 @@
             u_b.at[p], y_b.at[p, k], sy.at[0, p, k], sy.at[1, p, k], d, me.y_to(k)
         )
 
-    def fin_copy(p):
-        return send_to(
-            f_b.at[p], sum_out.at[p, me.c], sf.at[0, p], sf.at[1, p], d, me.cpeer
-        )
-
-    def fin_landed(p):
-        return send_to(
-            f_b.at[p], sum_out.at[p, 1 - me.c], sf.at[0, p], sf.at[1, p], d, me.cpeer
-        )
+    def done_at(p, seq):
+        index, off, col, quarter = pieces[p]
+        row = row_of(p, lax.rem(seq, 2), seq // 2)
+        return outs[index].at[pl.ds(row, size), pl.ds(col, wide)]
+
+    def fin_hops(p):
+        return range(1, g) if pieces[p][3] else (0,)
+
+    def fin_copy(p, k, seq):
+        to = me.s_to(k) if k else me.cpeer
+        return send_to(f_b.at[p], done_at(p, seq), sf.at[0, p, k], sf.at[1, p, k], d, to)
 
     def fin_keep(p):
-        return pltpu.make_async_copy(f_b.at[p], sum_out.at[p, me.c], sg.at[p])
-
-    def e2_load(p):
-        own_load(p).start()
-        core_landed(p).wait_recv()
-        pltpu.make_async_copy(c_land.at[p], c_b.at[p % 2], ld.at[1, p % 2]).start()
+        return pltpu.make_async_copy(f_b.at[p], done_at(p, s), sg.at[p])
+
+    def load(p, r):
+        own_load(p, r).start()
+        core_copy(p, r).wait_recv()
+        core_load(p, r).start()
+
+    def far_sum(p):
+        for r in range(1, ny):
+            i = spots[p, r] % 2
+            own_load(p, r).wait()
+            core_load(p, r).wait()
+
+            def add(j, carry, i=i):
+                total = own_b[i, j].astype(F32) + c_b[i, j].astype(F32)
+                far_b[fars.index(p), j] = total.astype(LOW)
+                return carry
+
+            lax.fori_loop(0, n, add, 0)
+            y_copy(p, r).start()
 
     def e2(p):
-        slot, two = lax.rem(p, 3), lax.rem(p, 2)
-        pltpu.make_async_copy(c_land.at[p], own_b.at[two], ld.at[0, two]).wait()
-        pltpu.make_async_copy(c_land.at[p], c_b.at[two], ld.at[1, two]).wait()
-
-        @pl.when(p >= 3)
-        def _():
+        slot, i = p % 3, spots[p, 0] % 2
+        own_load(p, 0).wait()
+        core_load(p, 0).wait()
+        if pieces[p][3]:
+            for r in range(1, ny):
+                y_copy(p, r).wait_recv()
+        if p >= 3:
             side_copy(p - 3).wait_send()
 
         def add(j, carry):
             for part in range(2):
                 at = 2 * j + (1 - me.x if part == 0 else me.x)
-                total = own_b[two, at].astype(F32) + c_b[two, at].astype(F32)
+                total = own_b[i, at].astype(F32) + c_b[i, at].astype(F32)
+                if pieces[p][3]:
+                    for r in range(1, ny):
+                        total = total + far_l[fars.index(p), r - 1, at].astype(F32)
                 s_b[slot, part * nz + j] = total.astype(LOW)
             return carry
 
@@ -630,17 +731,14 @@
         side_copy(p).start()
 
     def e3(p):
-        slot = lax.rem(p, 3)
+        slot = p % 3
         side_copy(p).wait_recv()
-        load = pltpu.make_async_copy(x_land.at[p], x_b, loc.at[8])
-        load.start()
-
-        @pl.when(p >= 3)
-        def _():
+        get = pltpu.make_async_copy(x_land.at[p], x_b, loc.at[8])
+        get.start()
+        if p >= 3:
             for k in range(1, nz):
                 line_copy(p - 3, k).wait_send()
-
-        load.wait()
+        get.wait()
 
         def add(j, carry):
             total = s_b[slot, nz + j].astype(F32) + x_b[j].astype(F32)
@@ -651,26 +749,50 @@
         for k in range(1, nz):
             line_copy(p, k).start()
 
+    def finish(p):
+        for k in fin_hops(p):
+            fin_copy(p, k, s).start()
+        fin_keep(p).start()
+
     def e4(p):
-        slot = lax.rem(p, 3)
+        slot = p % 3
         for k in range(1, nz):
             line_copy(p, k).wait_recv()
         total = t_b[slot, me.z].astype(F32)
         for k in range(1, nz):
-            total = total + z_b[p, k].astype(F32)
-        u_b[p] = total.astype(LOW)
-        for k in range(1, ny):
-            up_copy(p, k).start()
+            total = total + z_b[p, k - 1].astype(F32)
+        if pieces[p][3]:
+            f_b[p] = total.astype(LOW)
+            finish(p)
+        else:
+            u_b[p] = total.astype(LOW)
+            for k in range(1, ny):
+                up_copy(p, k).start()
 
     def e5(p):
+        if pieces[p][3]:
+            return
         for k in range(1, ny):
             up_copy(p, k).wait_recv()
         total = u_b[p].astype(F32)
         for k in range(1, ny):
             total = total + y_b[p, k].astype(F32)
         f_b[p] = total.astype(LOW)
-        fin_copy(p).start()
-        fin_keep(p).start()
+        finish(p)
+
+    plan = []
+    for p in range(count):
+        first, start, side, line, end = times[p]
+        if first is not None:
+            for r in range(1, ny):
+                plan.append((first - 1, 5, lambda p=p, r=r: load(p, r)))
+            plan.append((first, 4, lambda p=p: far_sum(p)))
+        plan.append((start - 1, 5, lambda p=p: load(p, 0)))
+        plan.append((start, 3, lambda p=p: e2(p)))
+        plan.append((side, 2, lambda p=p: e3(p)))
+        plan.append((line, 1, lambda p=p: e4(p)))
+        plan.append((end, 0, lambda p=p: e5(p)))
+    plan.sort(key=lambda item: item[:2])
 
     for pair in range(pairs):
         dctx_own(pair).start()
@@ -678,17 +800,11 @@
             dctx_copy(pair, k, s).start()
     for copy in tail_loads:
         copy.start()
-    for p in range(count):
-        core_copy(p).start()
+    for p, r in sorted(lands, key=lambda i: times[i[0]][1] if i[1] == 0 else times[i[0]][0]):
+        core_copy(p, r).start()
     lane_l = lax.broadcasted_iota(jnp.int32, (tok, LANES), 1)
     for j in range(g):
         va[j * tok : (j + 1) * tok, LANES:] = jnp.where(lane_l < 3, 1.0, 0.0).astype(LOW)
-
-    def t2(p):
-        return 2 * p + 2
-
-    def t3(p):
-        return (5 * p) // 2 + 6
 
     def attend(step, carry):
         pair = step // blocks
@@ -711,23 +827,13 @@
                 part = slice(j * chunk, (j + 1) * chunk)
                 kt[:, part] = ka[part, :LANES].astype(F32).T.astype(LOW)
 
-        for p in range(count):
-            @pl.when(step == t2(p) - 1)
-            def _(p=p):
-                e2_load(p)
-
-        for lag, event in ((0, e3), (3, e4), (5, e5)):
-            at = step - 6 - lag
-            p = (2 * jnp.maximum(at, 0) + 1) // 5
-            p = jnp.where((5 * p) // 2 == at, p, p + 1)
-
-            @pl.when((at >= 0) & ((5 * p) // 2 == at) & (p < count))
-            def _(p=p, event=event):
-                event(p)
-
-        @pl.when((lax.rem(step, 2) == 0) & (step >= 2) & (step < t2(count)))
-        def _():
-            e2((step - 2) // 2)
+        for t in sorted({item[0] for item in plan}):
+            if t < steps:
+                @pl.when(step == t)
+                def _(t=t):
+                    for at, order, event in plan:
+                        if at == t:
+                            event()
 
         for k in range(1, g):
             @pl.when(turn == k * per)
@@ -780,50 +886,54 @@
     lax.fori_loop(0, steps, attend, 0)
     for copy in tail_loads:
         copy.wait()
-    for p in range(count):
-        if t2(p) >= steps:
-            if t2(p) - 1 >= steps:
-                e2_load(p)
-            e2(p)
+    for at, order, event in plan:
+        if at >= steps and order in (3, 4, 5):
+            event()
 
     def heads_of(slot, tile):
         span = pl.ds(pl.multiple_of(slot * tok + tile * rows, rows), rows)
         return jnp.concatenate([dh[i, span, :] for i in range(3 * pairs)], 1)
 
+    def part_copy(k, tile):
+        span = pl.ds(pl.multiple_of(tile * rows, rows), rows)
+        return send_to(
+            part_c.at[k, span], part_k.at[k, span], sk.at[0, k, tile], sk.at[1, k, tile], d,
+            me.cpeer,
+        )
+
+    def far_copy(k, tile):
+        span = pl.ds(pl.multiple_of(tile * rows, rows), rows)
+        return send_to(
+            part_b.at[k - 1, span], part_y.at[k - 1, span], sfr.at[0, k, tile], sfr.at[1, k, tile],
+            d, me.y_to(k),
+        )
+
     def core_part(k):
         slot = lax.rem(me.y + k, ny) * 2 + 1 - me.c
 
         def tile_of(tile, carry):
             span = pl.ds(pl.multiple_of(tile * rows, rows), rows)
             part_c[k, span, :] = matmul_right(heads_of(slot, tile), wq[...]).astype(LOW)
+            part_copy(k, tile).start()
             return carry
 
         lax.fori_loop(0, per, tile_of, 0)
-        part_copy(k).start()
-
-    def part_copy(k):
-        return send_to(part_c.at[k], part_k.at[k], sk.at[0, k], sk.at[1, k], d, me.cpeer)
-
-    def far_copy(k):
-        return send_to(
-            part_b.at[k - 1], part_y.at[k - 1], sgq.at[0, 0, k], sgq.at[1, 0, k], d, me.y_to(k)
-        )
 
     for k in range(1, ny):
         core_part(k)
-    core_part(0)
     for k in range(1, ny):
-        part_copy(k).wait_recv()
         slot = lax.rem(me.y + k, ny) * 2 + me.c
 
         def far_tile(tile, carry, k=k, slot=slot):
             span = pl.ds(pl.multiple_of(tile * rows, rows), rows)
-            total = matmul_right(heads_of(slot, tile), wq[...]) + part_k[k, span, :].astype(F32)
+            total = matmul_right(heads_of(slot, tile), wq[...])
+            part_copy(k, tile).wait_recv()
+            total = total + part_k[k, span, :].astype(F32)
             part_b[k - 1, span, :] = total.astype(LOW)
+            far_copy(k, tile).start()
             return carry
 
         lax.fori_loop(0, per, far_tile, 0)
-        far_copy(k).start()
 
     sums = [jnp.zeros((1, LANES), F32) for _ in range(3 * pairs)]
     for i in range(3 * pairs):
@@ -845,8 +955,18 @@
             tq.at[lax.rem(me.z + k, nz)], zq.at[k], szq.at[0, k], szq.at[1, k], me.z_to(k), s
         )
 
-    def q_out_copy(k, source):
-        return send_to(rq, sq_out.at[source], sgq.at[0, 1, k], sgq.at[1, 1, k], d, me.s_to(k))
+    def q_parts(source):
+        parts = [(rq.at[pl.ds(deep, 16)], extra_out.at[source])]
+        for i in range(3):
+            at = pl.ds(pl.multiple_of(i * width + source * gw, LANES), gw)
+            parts.append((rq.at[pl.ds(0, deep), pl.ds(i * gw, gw)], sq_out.at[:, at]))
+        return parts
+
+    def q_out_copies(k, source):
+        return [
+            send_to(src, dst, sgq.at[0, i, k], sgq.at[1, i, k], d, me.s_to(k))
+            for i, (src, dst) in enumerate(q_parts(source))
+        ]
 
     tile_w = 256
     for base in range(0, width, tile_w):
@@ -860,7 +980,7 @@
             q_b[(base + at) // deep, :deep, :] = total[at : at + deep, :].astype(LOW)
         for j in range(base // deep // 2, (base + tile_w) // deep // 2):
             qx_copy(j).start()
-    remaining = count
+    core_part(0)
 
     def own_tile(tile, carry):
         span = pl.ds(pl.multiple_of(tile * rows, rows), rows)
@@ -869,10 +989,9 @@
 
     lax.fori_loop(0, per, own_tile, 0)
 
-    for event, lag in ((e3, 0), (e4, 3), (e5, 5)):
-        for p in range(remaining):
-            if t3(p) + lag >= steps:
-                event(p)
+    for at, order, event in plan:
+        if at >= steps and order in (0, 1, 2):
+            event()
 
     for j in range(nz):
         qx_copy(j).wait_recv()
@@ -880,7 +999,6 @@
         tq[j] = kept.astype(LOW)
     for k in range(1, nz):
         qz_copy(k).start()
-    part_copy(0).wait_recv()
     for k in range(1, nz):
         qz_copy(k).wait_recv()
     total = tq[me.z].astype(F32)
@@ -888,14 +1006,20 @@
         total = total + zq[k].astype(F32)
     rq[...] = total.astype(LOW)
     for k in range(1, g):
-        q_out_copy(k, s).start()
-    keep_q = pltpu.make_async_copy(rq, sq_out.at[s], loc.at[9])
-    keep_q.start()
-    for k in range(1, ny):
-        far_copy(k).wait_recv()
+        for copy in q_out_copies(k, s):
+            copy.start()
+    keep_q = [
+        pltpu.make_async_copy(src, dst, loc.at[11 + i])
+        for i, (src, dst) in enumerate(q_parts(s))
+    ]
+    for copy in keep_q:
+        copy.start()
 
     def sum_tile(tile, carry):
         span = pl.ds(pl.multiple_of(tile * rows, rows), rows)
+        part_copy(0, tile).wait_recv()
+        for k in range(1, ny):
+            far_copy(k, tile).wait_recv()
         total = din[span, :] + part_k[0, span, :].astype(F32)
         for k in range(1, ny):
             total = total + part_y[k - 1, span, :].astype(F32)
@@ -906,13 +1030,18 @@
     keep_d = pltpu.make_async_copy(din, din_out, loc.at[10])
     keep_d.start()
 
+    for p, r in lands:
+        core_copy(p, r).wait_send()
+        if r:
+            y_copy(p, r).wait_send()
     for p in range(count):
-        core_copy(p).wait_send()
-        fin_landed(p).wait_recv()
-        fin_copy(p).wait_send()
+        for k in fin_hops(p):
+            fin_copy(p, k, me.s_from(k) if k else me.cpeer).wait_recv()
+            fin_copy(p, k, s).wait_send()
         fin_keep(p).wait()
-        for k in range(1, ny):
-            up_copy(p, k).wait_send()
+        if not pieces[p][3]:
+            for k in range(1, ny):
+                up_copy(p, k).wait_send()
         if p >= count - 3:
             side_copy(p).wait_send()
             for k in range(1, nz):
@@ -920,18 +1049,22 @@
     for pair in range(pairs):
         for k in range(1, g):
             dctx_copy(pair, k, s).wait_send()
-    for k in range(ny):
-        part_copy(k).wait_send()
-    for k in range(1, ny):
-        far_copy(k).wait_send()
+    for tile in range(per):
+        for k in range(ny):
+            part_copy(k, tile).wait_send()
+        for k in range(1, ny):
+            far_copy(k, tile).wait_send()
     for j in range(nz):
         qx_copy(j).wait_send()
     for k in range(1, nz):
         qz_copy(k).wait_send()
     for k in range(1, g):
-        q_out_copy(k, me.s_from(k)).wait_recv()
-        q_out_copy(k, s).wait_send()
-    keep_q.wait()
+        for copy in q_out_copies(k, me.s_from(k)):
+            copy.wait_recv()
+        for copy in q_out_copies(k, s):
+            copy.wait_send()
+    for copy in keep_q:
+        copy.wait()
     keep_d.wait()
 
 
@@ -953,7 +1086,10 @@
     wide = min(1024, width)
     size = piece_rows(n)
     shares = [g.reshape(n, -1, g.shape[1]) for g in (g_out, g_up, g_down)]
-    count = len(grad_pieces([share.shape[1:] for share in shares], n, wide))
+    pieces = grad_pieces([share.shape[1:] for share in shares], n, g, wide)
+    count = len(pieces)
+    far = max(1, sum(piece[3] for piece in pieces))
+    lands = count + (g // 2 - 1) * sum(piece[3] for piece in pieces)
     anyw = pl.BlockSpec(memory_space=pl.ANY)
     low = lambda *shape: jax.ShapeDtypeStruct(shape, LOW)
     vmem = lambda *shape: pltpu.VMEM(shape, LOW)
@@ -964,10 +1100,11 @@
     return pl.pallas_call(
         functools.partial(backward_kernel, n=n, g=g, rows=256, chunk=chunk),
         in_specs=[anyw] * 12,
-        out_specs=[anyw] * 5,
+        out_specs=[anyw] * 8,
         out_shape=[
-            jax.ShapeDtypeStruct((tok, width), F32), low(count, 2, size, wide),
-            low(g, tall, 3 * gw), low(count, n, size, wide), low(count, nz, size, wide),
+            jax.ShapeDtypeStruct((tok, width), F32), *(low(*share.shape[1:]) for share in shares),
+            low(deep, 3 * width), low(g, 16, 3 * gw), low(lands, n, size, wide),
+            low(count, nz, size, wide),
         ],
         scratch_shapes=[
             vmem(length, LANES), vmem(length, 2 * LANES), vmem(length, 2 * LANES),
@@ -977,13 +1114,15 @@
             vmem(ny, tok, width), vmem(ny, tok, width), vmem(ny - 1, tok, width),
             vmem(ny - 1, tok, width), vmem32(tok, width),
             vmem(2, n, size, wide), vmem(2, n, size, wide), vmem(3, n, size, wide),
-            vmem(nz, size, wide), vmem(3, nz, size, wide), vmem(count, nz, size, wide),
+            vmem(nz, size, wide), vmem(3, nz, size, wide), vmem(count, nz - 1, size, wide),
             vmem(count, size, wide), vmem(count, ny, size, wide), vmem(count, size, wide),
             vmem(n, tall, 3 * gw), vmem(nz, tall, 3 * gw), vmem(nz, tall, 3 * gw),
-            vmem(nz, tall, 3 * gw), vmem(tall, 3 * gw),
-            dma(11), dma(2, 2), dma(2, pairs, g), dma(2, ny), dma(2, count, ny), dma(2, count),
-            dma(2, count), dma(2, count, nz), dma(count), dma(2, count), dma(pairs), dma(2, nz),
-            dma(2, nz), dma(2, 2, g),
+            vmem(nz, tall, 3 * gw), vmem(tall, 3 * gw), vmem(far, n, size, wide),
+            vmem(far, ny - 1, n, size, wide),
+            dma(15), dma(2, 2), dma(2, pairs, g), dma(2, ny, tok // 256), dma(2, count, ny),
+            dma(2, lands), dma(2, count), dma(2, count, nz), dma(count), dma(2, count, g),
+            dma(pairs), dma(2, nz), dma(2, nz), dma(2, 4, g), dma(2, far, ny),
+            dma(2, ny, tok // 256),
         ],
         compiler_params=pltpu.CompilerParams(
             vmem_limit_bytes=63 * 2**20, collective_id=1, has_side_effects=True
@@ -1084,9 +1223,20 @@
 
 
 def own_columns(piece, width, group_width):
-    at = lax.axis_index("dp") * piece.shape[0]
-    row = lax.dynamic_update_slice_in_dim(jnp.zeros((width,), LOW), piece, at, 0)
+    count = width // piece.shape[0]
+    mine = lax.broadcasted_iota(jnp.int32, (count, piece.shape[0]), 0) == lax.axis_index("dp")
+    row = jnp.where(mine, piece[None], jnp.zeros((), LOW)).reshape(-1)
     return lax.dynamic_slice_in_dim(row, lax.axis_index("seq") * group_width, group_width, 0)
+
+
+def laid(parts, total):
+    out, at = None, 0
+    for part in parts:
+        if part is not None:
+            one = jnp.pad(part, (at, total - at - part.shape[0]))
+            out = one if out is None else out + one
+            at += part.shape[0]
+    return out
 
 
 def local(
@@ -1103,25 +1253,25 @@
     vectors = (
         bias_q, bias_v, bias_out, gain_attn, shift_attn, bias_down, gain_ffn, shift_ffn, bias_up,
     )
-    packed = jnp.concatenate(vectors)
-    fill = -packed.shape[0] % (3 * group_width)
-    packed = jnp.pad(packed, (0, fill)).reshape(-1, 3 * group_width)
-    first_row = jnp.concatenate([
-        own_columns(bias_q, width, group_width), jnp.zeros((group_width,), LOW),
-        own_columns(bias_v, width, group_width),
-    ])[None]
+    line = 3 * group_width
+    filled = sum(vector.shape[0] for vector in vectors)
+    tall = -(-filled // line)
+    packed = laid(vectors, 15 * line)
+    first_row = laid([own_columns(bias_q, width, group_width)], line) + jnp.pad(
+        own_columns(bias_v, width, group_width), (2 * group_width, 0)
+    )
+    rows16 = jnp.concatenate([first_row, packed]).reshape(16, line)
     own_w = jnp.concatenate(
         [lax.dynamic_slice_in_dim(w_qkv, i * width + me * group_width, group_width, 1) for i in range(3)], 1
     )
-    blank = jnp.zeros((16 - 1 - packed.shape[0], 3 * group_width), LOW)
-    chunk = jnp.concatenate([own_w, first_row, packed, blank], 0)
+    chunk = jnp.concatenate([own_w, rows16], 0)
     bias_rows = jnp.broadcast_to(key_bias, (8, tok_rows))
     (context, own_context, q_all, ka_all, v_all, q_extra, hidden_all, w_heads, vec_all, f_w_out,
      f_w_up, f_w_down) = attend_forward(hidden_in, chunk, bias_rows, w_out, w_up, w_down)
     f_w_out = f_w_out.reshape(-1, w_out.shape[1])
     f_w_up = f_w_up.reshape(-1, w_up.shape[1])
     f_w_down = f_w_down.reshape(-1, w_down.shape[1])
-    packed = vec_all[:, 1 : 1 + packed.shape[0]].reshape(vec_all.shape[0], -1).astype(F32)
+    packed = vec_all[:, 1 : 1 + tall].reshape(vec_all.shape[0], -1).astype(F32)
     fulls, at = [], 0
     for vector in vectors:
         fulls.append(packed[:, at : at + vector.shape[0]].reshape(-1))
@@ -1160,24 +1310,15 @@
     tall = -(-filled // (3 * group_width))
     vecs = jnp.pad(rows, ((0, 0), (0, tall * 3 * group_width - filled)))
     vecs = jnp.pad(vecs.reshape(shares, tall, -1), ((0, 0), (1, 15 - tall), (0, 0)))
-    d_in, sums, heads, _, _ = attend_backward(
+    d_in, s_w_out, s_w_up, s_w_down, s_w_qkv, heads, _, _ = attend_backward(
         d_context, q_all, ka_all, v_all, q_extra, own_context, hidden_all, w_heads, vecs,
         g_w_out, g_w_up, g_w_down,
     )
     grad_in = d_attended + d_in
-    own_sums = []
-    wide, size = sums.shape[3], sums.shape[2]
-    pieces = grad_pieces([w.shape for w in (w_out, w_up, w_down)], shares, wide)
-    for index, w in enumerate((w_out, w_up, w_down)):
-        mine = [p for p, piece in enumerate(pieces) if piece[0] == index]
-        part = sums[mine[0] : mine[-1] + 1].reshape(
-            -1, w.shape[1] // wide, 2, size, wide
-        )
-        own_sums.append(part.transpose(2, 0, 3, 1, 4).reshape(w.shape).astype(F32))
-    s_w_out, s_w_up, s_w_down = own_sums
-    s_w_qkv = heads[:, :deep].reshape(groups, deep, 3, group_width)
-    s_w_qkv = s_w_qkv.transpose(1, 2, 0, 3).reshape(deep, -1).astype(F32)
-    head_rows = heads[:, deep].astype(F32)
+    s_w_out, s_w_up, s_w_down, s_w_qkv = (
+        grad.astype(F32) for grad in (s_w_out, s_w_up, s_w_down, s_w_qkv)
+    )
+    head_rows = heads[:, 0].astype(F32)
     at = lax.axis_index("dp") * bias_q.shape[0]
     s_bias_q = lax.dynamic_slice_in_dim(
         head_rows[:, :group_width].reshape(-1), at, bias_q.shape[0], 0
@@ -1185,7 +1326,7 @@
     s_bias_v = lax.dynamic_slice_in_dim(
         head_rows[:, 2 * group_width :].reshape(-1), at, bias_v.shape[0], 0
     )
-    own = jnp.sum(heads[:, deep + 1 : deep + 1 + tall].astype(F32), 0).reshape(-1)
+    own = jnp.sum(heads[:, 1 : 1 + tall].astype(F32), 0).reshape(-1)
     own_vectors, at = [], 0
     for vector in vectors[2:]:
         own_vectors.append(own[at : at + vector.shape[0]])

time: 542 us -> 498 us (0.919)
  the two profiles are of different devices: /device:TPU:11 before, /device:TPU:29 now
where the time goes in v3:
time: 498 us; the launch traced here: 490 us
  Pallas kernels  442 us (89%)
  other arithmetic  28.6 us (6%)
  matrix products  11.6 us (2%)
  local copies, waits for them, and re-layouts  6.5 us (1%)
    pallas_call x1, Pallas kernels, attend_backward(): pl.pallas_call(functools.partial(backward_kernel, n=n, g=g, rows=256, chu...  230 us
    pallas_call x1, Pallas kernels, attend_forward(): pl.pallas_call(functools.partial(forward_kernel, n=n, g=g, rows=256), in_...  149 us
    pallas_call x1, Pallas kernels, feed_backward(): pl.pallas_call(down_kernel, grid=(ff // tile,), in_specs=[whole, whole, u...  34.6 us
    pallas_call x1, Pallas kernels, feed_forward(): pl.pallas_call(up_kernel, grid=(ff // tile,), in_specs=[whole, pl.BlockSp...  27.7 us

profile of v3, /device:TPU:29, one launch (start us, length us, event | category | flops | bytes accessed | tf_op | source)
XLA Modules:
  0.0 489.7 jit_solution(14769273220479185540)
XLA Ops:
  0.6 0.8 pad_add_fusion
  1.5 0.7 select_bitcast_fusion.1
  2.2 0.1 dynamic_slice.25
  2.3 0.1 dynamic_slice.24
  2.5 0.9 constant_dynamic-slice_fusion.2
  3.4 0.7 pad_maximum_fusion.wch_ref
  4.1 0.7 reduce.1
  4.8 0.6 broadcast_in_dim.51.kb_ref
  5.4 0.0 copy-start.6
  5.4 149.1 %shard_map.271 = (bf16[768,1024]{1,0:T(8,128)(2,1)}, bf16[2,3072,128]{2,1,0:T(8,128)(2,1)}, bf16[2,3072,128]{2,1,0:T(8,128)(2,1)}, bf16[2,3072,256]{2,1,0:T(8,12...) custom-call(bf16[768,1024]{1,0:T(8,128)(2,1)} %hid_ref.1, ...), custom_call_target="tpu_custom_call" | custom-call | flops 38654705664 | bytes 7864320 | tf_op jit(solution)/shard_map/pallas_call | solution.py:499
  154.6 0.9 convert_bitcast_fusion
  155.5 0.0 copy-done.6
  155.5 4.0 fusion.11
  159.5 0.4 multiply_reduce_fusion.3
  160.0 0.6 fusion.4.x_ref
  160.6 27.7 %shard_map.272 = (bf16[768,4096]{1,0:T(8,128)(2,1)}, bf16[768,4096]{1,0:T(8,128)(2,1)}, f32[768,1024]{1,0:T(8,128)S(1)}) custom-call(bf16[768,1024]{1,0:T(8,128)(2,1)S(1)} %fusion.4.x_ref, bf16[1024,4096]{1,0:T(8,128)(2,1)} %bitcast.55, f32[1,4096]{1,0:T(1,128)S(1)} %bitcast.54, bf16[4096,1024]{1,0:T(8,128)(2,1)} %bitcast.57), custom_call_target="tpu_custom_call" | custom-call | tf_op jit(solution)/shard_map/pallas_call | solution.py:1168
  188.3 1.0 fusion.9
  189.3 0.0 copy-start.1
  189.3 0.4 multiply_reduce_fusion.2
  189.8 0.9 copy-done.1
  190.7 1.2 fusion.3
  192.0 2.6 fusion.8
  194.6 0.3 add_reduce_fusion.1
  194.9 34.6 %shard_map.273 = (bf16[1024,4096]{1,0:T(8,128)(2,1)}, bf16[4096,1024]{1,0:T(8,128)(2,1)}, f32[1,4096]{1,0:T(1,128)S(1)}, f32[768,1024]{1,0:T(8,128)}) custom-call(bf16[768,1024]{1,0:T(8,128)(2,1)S(1)} %fusion.4.x_ref, bf16[768,1024]{1,0:T(8,128)(2,1)S(1)} %get-tuple-element.79.e_ref, bf16[1024,4096]{1,0:T(8,128)(2,1)} %bitcast.56, ...), custom_call_target="tpu_custom_call" | custom-call | tf_op jit(solution)/shard_map/pallas_call | solution.py:1212
  229.5 3.3 multiply_reduce_fusion
  232.8 0.0 copy-start.7
  232.8 0.9 fusion.7
  233.7 0.0 copy-start
  233.8 0.6 copy-done.7
  234.4 3.0 convolution_convert_fusion.1.dctx_ref
  237.4 0.3 add_reduce_fusion
  237.7 1.7 reduce
  239.4 0.1 convert_reduce_fusion.1
  239.6 0.7 pad.64.vec_ref
  240.3 0.0 copy-done
  240.3 4.6 convolution_convert_fusion
  244.9 230.2 %shard_map.274 = (f32[768,1024]{1,0:T(8,128)}, bf16[128,1024]{1,0:T(8,128)(2,1)}, bf16[128,4096]{1,0:T(8,128)(2,1)}, bf16[512,1024]{1,0:T(8,128)(2,1)}, bf16[128...) custom-call(bf16[768,1024]{1,0:T(8,128)(2,1)} %convolution_convert_f, ...), custom_call_target="tpu_custom_call" | custom-call | flops 96636764160 | bytes 7864320 | tf_op jit(solution)/shard_map/pallas_call | solution.py:1100
  475.1 0.0 copy-start.4
  475.1 0.0 copy-start.5
  475.1 5.0 %add_add_fusion.4 = f32[768,1024]{1,0:T(8,128)} fusion(f32[768,1024]{1,0:T(8,128)} %get-tuple-element.59, f32[768,1024]{1,0:T(8,128)} %copy-done, f32[768]{0:T(1024)S(1)} %negate_multiply_fusion), kind=kLoop, calls=%fused_computation.16 | loop fusion | flops 1572864 | bytes 9440256 | tf_op jit(solution)/shard_map/add | solution.py:1317
  480.1 0.0 copy-start.3
  480.1 0.0 copy-done.4
  480.1 0.0 copy-start.2
  480.1 1.3 convert_element_type.88
  481.4 0.8 slice_convert_fusion
  482.2 0.6 dynamic_slice.26
  482.8 0.6 dynamic_slice.27
  483.4 0.0 copy-done.5
  483.4 0.8 convert_element_type.91
  484.2 0.8 convert_reduce_fusion
  485.1 0.5 fusion.10
  485.6 0.0 copy-done.3
  485.6 1.5 convert_element_type.93
  487.2 0.6 slice.88
  487.7 0.0 copy-done.2
  487.7 1.6 convert_element_type.94
  (31 shorter events, 0.3 us)
Async XLA Ops:
  5.4 150.1 %copy-start.6 = (bf16[768,1024]{1,0:T(8,128)(2,1)S(1)}, bf16[768,1024]{1,0:T(8,128)(2,1)}, u32[]{:S(2)}) copy-start(bf16[768,1024]{1,0:T(8,128)(2,1)} %hid_ref.1) | copy-start | bytes 4718596
  189.3 1.4 copy-start.1
  232.8 1.6 copy-start.7
  233.7 6.5 %copy-start = (f32[768,1024]{1,0:T(8,128)}, f32[768,1024]{1,0:T(8,128)S(1)}, u32[]{:S(2)}) copy-start(f32[768,1024]{1,0:T(8,128)S(1)} %get-tuple-element.71) | copy-start | bytes 9437188
  475.1 5.0 %copy-start.4 = (bf16[128,3072]{1,0:T(8,128)(2,1)S(1)}, bf16[128,3072]{1,0:T(8,128)(2,1)}, u32[]{:S(2)}) copy-start(bf16[128,3072]{1,0:T(8,128)(2,1)} %get-tuple-element.60) | copy-start | bytes 2359300
  475.1 8.3 %copy-start.5 = (bf16[128,1024]{1,0:T(8,128)(2,1)S(1)}, bf16[128,1024]{1,0:T(8,128)(2,1)}, u32[]{:S(2)}) copy-start(bf16[128,1024]{1,0:T(8,128)(2,1)} %get-tuple-element.62) | copy-start | bytes 786436
  480.1 5.5 %copy-start.3 = (bf16[128,4096]{1,0:T(8,128)(2,1)S(1)}, bf16[128,4096]{1,0:T(8,128)(2,1)}, u32[]{:S(2)}) copy-start(bf16[128,4096]{1,0:T(8,128)(2,1)} %get-tuple-element.63) | copy-start | bytes 3145732
  480.1 7.6 %copy-start.2 = (bf16[512,1024]{1,0:T(8,128)(2,1)S(1)}, bf16[512,1024]{1,0:T(8,128)(2,1)}, u32[]{:S(2)}) copy-start(bf16[512,1024]{1,0:T(8,128)(2,1)} %get-tuple-element.64) | copy-start | bytes 3145732

commit v4 on v3

--- a/solution.py
+++ b/solution.py
@@ -11,6 +11,7 @@
 LANES = 128
 SCALE = HEAD_DIM**-0.5
 norm_eps = 1e-05
+PIECE_STEPS = 3.2
 PIECE_GAP = 3.5
 F32 = jnp.float32
 LOW = jnp.bfloat16
@@ -551,9 +552,9 @@
             y_free = max(y_free, first) + 5.0
             at = max(at, int(y_free) + 1)
         start = max(at, int(x_free - 1.0))
-        x_free = max(x_free, start) + 2.5
+        x_free = max(x_free, start) + PIECE_STEPS
         side = int(x_free + 0.9)
-        z_free = max(z_free, side) + 2.5
+        z_free = max(z_free, side) + PIECE_STEPS
         line = int(z_free + 0.9)
         times.append((first, start, side, line, line + 2))
         at = start + 2
@@ -788,6 +789,9 @@
                 plan.append((first - 1, 5, lambda p=p, r=r: load(p, r)))
             plan.append((first, 4, lambda p=p: far_sum(p)))
         plan.append((start - 1, 5, lambda p=p: load(p, 0)))
+        for r in range(ny if first is not None else 1):
+            at = start if r == 0 else first
+            plan.append((at - 3, 6, lambda p=p, r=r: core_copy(p, r).start()))
         plan.append((start, 3, lambda p=p: e2(p)))
         plan.append((side, 2, lambda p=p: e3(p)))
         plan.append((line, 1, lambda p=p: e4(p)))
@@ -800,46 +804,28 @@
             dctx_copy(pair, k, s).start()
     for copy in tail_loads:
         copy.start()
-    for p, r in sorted(lands, key=lambda i: times[i[0]][1] if i[1] == 0 else times[i[0]][0]):
-        core_copy(p, r).start()
+    for at, order, event in plan:
+        if at < 0:
+            event()
     lane_l = lax.broadcasted_iota(jnp.int32, (tok, LANES), 1)
     for j in range(g):
         va[j * tok : (j + 1) * tok, LANES:] = jnp.where(lane_l < 3, 1.0, 0.0).astype(LOW)
 
-    def attend(step, carry):
-        pair = step // blocks
-        turn = lax.rem(step, blocks)
-        rel = turn // per
-        owner = lax.rem(s + g - rel, g)
-        block = owner * per + lax.rem(turn, per)
-
-        @pl.when(turn == 0)
-        def _():
-            loads = pair_loads(pair)
-            for copy in loads:
-                copy.start()
-            dk_acc[...] = jnp.zeros_like(dk_acc)
-            dv_acc[...] = jnp.zeros_like(dv_acc)
-            dctx_own(pair).wait()
-            for copy in loads:
-                copy.wait()
-            for j in range(length // chunk):
-                part = slice(j * chunk, (j + 1) * chunk)
-                kt[:, part] = ka[part, :LANES].astype(F32).T.astype(LOW)
-
+    near = [me.y * 2, me.y * 2 + 1]
+    far_slots = [lax.rem(me.y + k, ny) * 2 + i for k in range(1, ny) for i in range(2)]
+    near_blocks = 2 * per
+    full = steps - near_blocks
+
+    def run_events(step):
         for t in sorted({item[0] for item in plan}):
-            if t < steps:
+            if 0 <= t < steps:
                 @pl.when(step == t)
                 def _(t=t):
                     for at, order, event in plan:
                         if at == t:
                             event()
 
-        for k in range(1, g):
-            @pl.when(turn == k * per)
-            def _(k=k):
-                dctx_copy(pair, k, me.s_from(k)).wait_recv()
-
+    def block_pass(pair, block, slots):
         span = pl.ds(pl.multiple_of(block * rows, rows), rows)
         lane = lax.broadcasted_iota(jnp.int32, (rows, LANES), 1)
         queries = q_s[span, :].astype(F32) * SCALE
@@ -862,20 +848,54 @@
         q_rows = jnp.concatenate(q_mask, 0)
         g_rows = jnp.concatenate(g_mask, 0)
         dq_t = [jnp.zeros((LANES, rows), F32) for _ in range(2)]
-        for start in range(0, length, chunk):
-            part = slice(start, start + chunk)
-            p_list, ds_list = [], []
-            for head in range(2):
-                probs = jnp.exp(matmul_right(ka[part, :], q_wide[head]))
-                d_scores = (probs * matmul_right(va[part, :], g_wide[head])).astype(LOW)
-                p_list.append(probs.astype(LOW))
-                ds_list.append(d_scores)
-                dq_t[head] = dq_t[head] + matmul(kt[:, part], d_scores)
-            dv_acc[part, :] += matmul(jnp.concatenate(p_list, 1), g_rows)
-            dk_acc[part, :] += matmul(jnp.concatenate(ds_list, 1), q_rows)
+        for slot in slots:
+            for base in range(0, tok, chunk):
+                at = slot * tok + base
+                part = slice(at, at + chunk)
+                if not isinstance(at, int):
+                    part = pl.ds(pl.multiple_of(at, LANES), chunk)
+                p_list, ds_list = [], []
+                for head in range(2):
+                    probs = jnp.exp(matmul_right(ka[part, :], q_wide[head]))
+                    d_scores = (probs * matmul_right(va[part, :], g_wide[head])).astype(LOW)
+                    p_list.append(probs.astype(LOW))
+                    ds_list.append(d_scores)
+                    dq_t[head] = dq_t[head] + matmul(kt[:, part], d_scores)
+                dv_acc[part, :] += matmul(jnp.concatenate(p_list, 1), g_rows)
+                dk_acc[part, :] += matmul(jnp.concatenate(ds_list, 1), q_rows)
         row = lax.broadcasted_iota(jnp.int32, (LANES, rows), 0)
-        both = jnp.where(row < HEAD_DIM, dq_t[0], dq_t[1]) * SCALE
-        dh[pair, span, :] = both.T.astype(LOW)
+        return jnp.where(row < HEAD_DIM, dq_t[0], dq_t[1]) * SCALE
+
+    def attend(step, carry):
+        pair = step // blocks
+        turn = lax.rem(step, blocks)
+        rel = turn // per
+        owner = lax.rem(s + g - rel, g)
+        owner = jnp.where(pair == pairs - 1, lax.rem(me.y * 2 + 2 + rel, g), owner)
+        block = owner * per + lax.rem(turn, per)
+
+        @pl.when(turn == 0)
+        def _():
+            loads = pair_loads(pair)
+            for copy in loads:
+                copy.start()
+            dk_acc[...] = jnp.zeros_like(dk_acc)
+            dv_acc[...] = jnp.zeros_like(dv_acc)
+            dctx_own(pair).wait()
+            for copy in loads:
+                copy.wait()
+            for j in range(length // chunk):
+                part = slice(j * chunk, (j + 1) * chunk)
+                kt[:, part] = ka[part, :LANES].astype(F32).T.astype(LOW)
+
+        run_events(step)
+        for k in range(1, g):
+            @pl.when(turn == jnp.where(pair == pairs - 1, 0, k * per))
+            def _(k=k):
+                dctx_copy(pair, k, me.s_from(k)).wait_recv()
+
+        both = block_pass(pair, block, range(g))
+        dh[pair, pl.ds(pl.multiple_of(block * rows, rows), rows), :] = both.T.astype(LOW)
 
         @pl.when(turn == blocks - 1)
         def _():
@@ -883,13 +903,39 @@
             dh[2 * pairs + pair] = dv_acc[...].astype(LOW)
         return carry
 
-    lax.fori_loop(0, steps, attend, 0)
+    lax.fori_loop(0, full, attend, 0)
+    last = pairs - 1
+
+    def keep_heads(slots):
+        for slot in slots:
+            span = pl.ds(pl.multiple_of(slot * tok, tok), tok)
+            dh[pairs + last, span, :] = dk_acc[span, :].astype(LOW)
+            dh[2 * pairs + last, span, :] = dv_acc[span, :].astype(LOW)
+
+    def far_keys(i, carry):
+        @pl.when(lax.rem(i, 2) == 0)
+        def _():
+            run_events(full + i // 2)
+
+        both = block_pass(last, me.y * near_blocks + i, far_slots)
+        din[pl.ds(pl.multiple_of(i * LANES, LANES), LANES), :rows] = both
+        return carry
+
+    def near_keys(i, carry):
+        @pl.when(lax.rem(i, 2) == 0)
+        def _():
+            run_events(full + (near_blocks + i) // 2)
+
+        block = me.y * near_blocks + i
+        both = block_pass(last, block, near)
+        both = both + din[pl.ds(pl.multiple_of(i * LANES, LANES), LANES), :rows]
+        dh[last, pl.ds(pl.multiple_of(block * rows, rows), rows), :] = both.T.astype(LOW)
+        return carry
+
+    lax.fori_loop(0, near_blocks, far_keys, 0)
+    keep_heads(far_slots)
     for copy in tail_loads:
         copy.wait()
-    for at, order, event in plan:
-        if at >= steps and order in (3, 4, 5):
-            event()
-
     def heads_of(slot, tile):
         span = pl.ds(pl.multiple_of(slot * tok + tile * rows, rows), rows)
         return jnp.concatenate([dh[i, span, :] for i in range(3 * pairs)], 1)
@@ -934,6 +980,16 @@
             return carry
 
         lax.fori_loop(0, per, far_tile, 0)
+
+    lax.fori_loop(0, near_blocks, near_keys, 0)
+    keep_heads(near)
+    for at, order, event in plan:
+        if at >= steps and order in (3, 4, 5, 6):
+            event()
+
+    for at, order, event in plan:
+        if at >= steps and order == 2:
+            event()
 
     sums = [jnp.zeros((1, LANES), F32) for _ in range(3 * pairs)]
     for i in range(3 * pairs):
@@ -990,7 +1046,7 @@
     lax.fori_loop(0, per, own_tile, 0)
 
     for at, order, event in plan:
-        if at >= steps and order in (0, 1, 2):
+        if at >= steps and order in (0, 1):
             event()
 
     for j in range(nz):

time: 498 us -> 481 us (0.966)
  the two profiles are of different devices: /device:TPU:29 before, /device:TPU:11 now
where the time goes in v4:
time: 481 us; the launch traced here: 473 us
  Pallas kernels  425 us (88%)
  other arithmetic  28.5 us (6%)
  matrix products  11.6 us (2%)
  local copies, waits for them, and re-layouts  6.5 us (1%)
    pallas_call x1, Pallas kernels, attend_backward(): pl.pallas_call(functools.partial(backward_kernel, n=n, g=g, rows=256, chu...  216 us
    pallas_call x1, Pallas kernels, attend_forward(): pl.pallas_call(functools.partial(forward_kernel, n=n, g=g, rows=256), in_...  147 us
    pallas_call x1, Pallas kernels, feed_backward(): pl.pallas_call(down_kernel, grid=(ff // tile,), in_specs=[whole, whole, u...  34.6 us
    pallas_call x1, Pallas kernels, feed_forward(): pl.pallas_call(up_kernel, grid=(ff // tile,), in_specs=[whole, pl.BlockSp...  28 us

profile of v4, /device:TPU:11, one launch (start us, length us, event | category | flops | bytes accessed | tf_op | source)
XLA Modules:
  0.0 473.3 jit_solution(8094618855020725769)
XLA Ops:
  0.6 0.8 pad_add_fusion
  1.5 0.7 select_bitcast_fusion.1
  2.2 0.1 dynamic_slice.25
  2.3 0.1 dynamic_slice.24
  2.5 0.9 constant_dynamic-slice_fusion.2
  3.4 0.7 pad_maximum_fusion.wch_ref
  4.1 0.7 reduce.1
  4.8 0.6 broadcast_in_dim.51.kb_ref
  5.4 0.0 copy-start.6
  5.4 147.0 %shard_map.271 = (bf16[768,1024]{1,0:T(8,128)(2,1)}, bf16[2,3072,128]{2,1,0:T(8,128)(2,1)}, bf16[2,3072,128]{2,1,0:T(8,128)(2,1)}, bf16[2,3072,256]{2,1,0:T(8,12...) custom-call(bf16[768,1024]{1,0:T(8,128)(2,1)} %hid_ref.1, ...), custom_call_target="tpu_custom_call" | custom-call | flops 38654705664 | bytes 7864320 | tf_op jit(solution)/shard_map/pallas_call | solution.py:500
  152.4 0.9 convert_bitcast_fusion
  153.3 0.0 copy-done.6
  153.3 4.0 fusion.11
  157.3 0.4 multiply_reduce_fusion.3
  157.8 0.6 fusion.4.x_ref
  158.4 28.0 %shard_map.272 = (bf16[768,4096]{1,0:T(8,128)(2,1)}, bf16[768,4096]{1,0:T(8,128)(2,1)}, f32[768,1024]{1,0:T(8,128)S(1)}) custom-call(bf16[768,1024]{1,0:T(8,128)(2,1)S(1)} %fusion.4.x_ref, bf16[1024,4096]{1,0:T(8,128)(2,1)} %bitcast.55, f32[1,4096]{1,0:T(1,128)S(1)} %bitcast.54, bf16[4096,1024]{1,0:T(8,128)(2,1)} %bitcast.57), custom_call_target="tpu_custom_call" | custom-call | tf_op jit(solution)/shard_map/pallas_call | solution.py:1224
  186.4 1.0 fusion.9
  187.4 0.0 copy-start.1
  187.5 0.4 multiply_reduce_fusion.2
  187.9 0.9 copy-done.1
  188.9 1.2 fusion.3
  190.1 2.6 fusion.8
  192.7 0.3 add_reduce_fusion.1
  193.0 34.6 %shard_map.273 = (bf16[1024,4096]{1,0:T(8,128)(2,1)}, bf16[4096,1024]{1,0:T(8,128)(2,1)}, f32[1,4096]{1,0:T(1,128)S(1)}, f32[768,1024]{1,0:T(8,128)}) custom-call(bf16[768,1024]{1,0:T(8,128)(2,1)S(1)} %fusion.4.x_ref, bf16[768,1024]{1,0:T(8,128)(2,1)S(1)} %get-tuple-element.79.e_ref, bf16[1024,4096]{1,0:T(8,128)(2,1)} %bitcast.56, ...), custom_call_target="tpu_custom_call" | custom-call | tf_op jit(solution)/shard_map/pallas_call | solution.py:1268
  227.7 3.2 multiply_reduce_fusion
  230.9 0.0 copy-start.7
  230.9 0.9 fusion.7
  231.8 0.0 copy-start
  231.8 0.6 copy-done.7
  232.5 3.0 convolution_convert_fusion.1.dctx_ref
  235.5 0.3 add_reduce_fusion
  235.8 1.7 reduce
  237.5 0.1 convert_reduce_fusion.1
  237.6 0.7 pad.64.vec_ref
  238.3 0.0 copy-done
  238.4 4.6 convolution_convert_fusion
  243.0 215.7 %shard_map.274 = (f32[768,1024]{1,0:T(8,128)}, bf16[128,1024]{1,0:T(8,128)(2,1)}, bf16[128,4096]{1,0:T(8,128)(2,1)}, bf16[512,1024]{1,0:T(8,128)(2,1)}, bf16[128...) custom-call(bf16[768,1024]{1,0:T(8,128)(2,1)} %convolution_convert_f, ...), custom_call_target="tpu_custom_call" | custom-call | flops 96636764160 | bytes 7864320 | tf_op jit(solution)/shard_map/pallas_call | solution.py:1156
  458.7 0.0 copy-start.4
  458.7 0.0 copy-start.5
  458.7 5.0 %add_add_fusion.4 = f32[768,1024]{1,0:T(8,128)} fusion(f32[768,1024]{1,0:T(8,128)} %get-tuple-element.59, f32[768,1024]{1,0:T(8,128)} %copy-done, f32[768]{0:T(1024)S(1)} %negate_multiply_fusion), kind=kLoop, calls=%fused_computation.16 | loop fusion | flops 1572864 | bytes 9440256 | tf_op jit(solution)/shard_map/add | solution.py:1373
  463.6 0.0 copy-start.3
  463.6 0.0 copy-done.4
  463.6 0.0 copy-start.2
  463.6 1.3 convert_element_type.88
  464.9 0.8 slice_convert_fusion
  465.8 0.6 dynamic_slice.26
  466.4 0.6 dynamic_slice.27
  466.9 0.0 copy-done.5
  466.9 0.8 convert_element_type.91
  467.8 0.8 convert_reduce_fusion
  468.6 0.5 fusion.10
  469.2 0.0 copy-done.3
  469.2 1.5 convert_element_type.93
  470.7 0.6 slice.88
  471.3 0.0 copy-done.2
  471.3 1.6 convert_element_type.94
  (31 shorter events, 0.3 us)
Async XLA Ops:
  5.4 147.9 %copy-start.6 = (bf16[768,1024]{1,0:T(8,128)(2,1)S(1)}, bf16[768,1024]{1,0:T(8,128)(2,1)}, u32[]{:S(2)}) copy-start(bf16[768,1024]{1,0:T(8,128)(2,1)} %hid_ref.1) | copy-start | bytes 4718596
  187.4 1.4 copy-start.1
  230.9 1.6 copy-start.7
  231.8 6.5 %copy-start = (f32[768,1024]{1,0:T(8,128)}, f32[768,1024]{1,0:T(8,128)S(1)}, u32[]{:S(2)}) copy-start(f32[768,1024]{1,0:T(8,128)S(1)} %get-tuple-element.71) | copy-start | bytes 9437188
  458.7 5.0 %copy-start.4 = (bf16[128,3072]{1,0:T(8,128)(2,1)S(1)}, bf16[128,3072]{1,0:T(8,128)(2,1)}, u32[]{:S(2)}) copy-start(bf16[128,3072]{1,0:T(8,128)(2,1)} %get-tuple-element.60) | copy-start | bytes 2359300
  458.7 8.3 %copy-start.5 = (bf16[128,1024]{1,0:T(8,128)(2,1)S(1)}, bf16[128,1024]{1,0:T(8,128)(2,1)}, u32[]{:S(2)}) copy-start(bf16[128,1024]{1,0:T(8,128)(2,1)} %get-tuple-element.62) | copy-start | bytes 786436
  463.6 5.5 %copy-start.3 = (bf16[128,4096]{1,0:T(8,128)(2,1)S(1)}, bf16[128,4096]{1,0:T(8,128)(2,1)}, u32[]{:S(2)}) copy-start(bf16[128,4096]{1,0:T(8,128)(2,1)} %get-tuple-element.63) | copy-start | bytes 3145732
  463.6 7.6 %copy-start.2 = (bf16[512,1024]{1,0:T(8,128)(2,1)S(1)}, bf16[512,1024]{1,0:T(8,128)(2,1)}, u32[]{:S(2)}) copy-start(bf16[512,1024]{1,0:T(8,128)(2,1)} %get-tuple-element.64) | copy-start | bytes 3145732

commit v5 on v4

--- a/solution.py
+++ b/solution.py
@@ -987,10 +987,6 @@
         if at >= steps and order in (3, 4, 5, 6):
             event()
 
-    for at, order, event in plan:
-        if at >= steps and order == 2:
-            event()
-
     sums = [jnp.zeros((1, LANES), F32) for _ in range(3 * pairs)]
     for i in range(3 * pairs):
         for j in range(g):
@@ -1036,6 +1032,10 @@
             q_b[(base + at) // deep, :deep, :] = total[at : at + deep, :].astype(LOW)
         for j in range(base // deep // 2, (base + tile_w) // deep // 2):
             qx_copy(j).start()
+    for at, order, event in plan:
+        if at >= steps and order == 2:
+            event()
+
     core_part(0)
 
     def own_tile(tile, carry):

time: 481 us -> 481 us (level)
  no operation moved by 1% of the time
where the time goes in v5:
time: 481 us; the launch traced here: 473 us
  Pallas kernels  425 us (88%)
  other arithmetic  28.5 us (6%)
  matrix products  11.6 us (2%)
  local copies, waits for them, and re-layouts  6.5 us (1%)
    pallas_call x1, Pallas kernels, attend_backward(): pl.pallas_call(functools.partial(backward_kernel, n=n, g=g, rows=256, chu...  216 us
    pallas_call x1, Pallas kernels, attend_forward(): pl.pallas_call(functools.partial(forward_kernel, n=n, g=g, rows=256), in_...  147 us
    pallas_call x1, Pallas kernels, feed_backward(): pl.pallas_call(down_kernel, grid=(ff // tile,), in_specs=[whole, whole, u...  34.6 us
    pallas_call x1, Pallas kernels, feed_forward(): pl.pallas_call(up_kernel, grid=(ff // tile,), in_specs=[whole, pl.BlockSp...  28 us

profile of v5, /device:TPU:11, one launch (start us, length us, event | category | flops | bytes accessed | tf_op | source)
XLA Modules:
  0.0 473.3 jit_solution(4222310892199364707)
XLA Ops:
  0.6 0.8 pad_add_fusion
  1.5 0.7 select_bitcast_fusion.1
  2.2 0.1 dynamic_slice.25
  2.3 0.1 dynamic_slice.24
  2.5 0.9 constant_dynamic-slice_fusion.2
  3.4 0.7 pad_maximum_fusion.wch_ref
  4.1 0.7 reduce.1
  4.8 0.6 broadcast_in_dim.51.kb_ref
  5.4 0.0 copy-start.6
  5.4 147.0 %shard_map.271 = (bf16[768,1024]{1,0:T(8,128)(2,1)}, bf16[2,3072,128]{2,1,0:T(8,128)(2,1)}, bf16[2,3072,128]{2,1,0:T(8,128)(2,1)}, bf16[2,3072,256]{2,1,0:T(8,12...) custom-call(bf16[768,1024]{1,0:T(8,128)(2,1)} %hid_ref.1, ...), custom_call_target="tpu_custom_call" | custom-call | flops 38654705664 | bytes 7864320 | tf_op jit(solution)/shard_map/pallas_call | solution.py:500
  152.4 0.9 convert_bitcast_fusion
  153.3 0.0 copy-done.6
  153.3 4.0 fusion.11
  157.3 0.4 multiply_reduce_fusion.3
  157.8 0.6 fusion.4.x_ref
  158.4 28.0 %shard_map.272 = (bf16[768,4096]{1,0:T(8,128)(2,1)}, bf16[768,4096]{1,0:T(8,128)(2,1)}, f32[768,1024]{1,0:T(8,128)S(1)}) custom-call(bf16[768,1024]{1,0:T(8,128)(2,1)S(1)} %fusion.4.x_ref, bf16[1024,4096]{1,0:T(8,128)(2,1)} %bitcast.55, f32[1,4096]{1,0:T(1,128)S(1)} %bitcast.54, bf16[4096,1024]{1,0:T(8,128)(2,1)} %bitcast.57), custom_call_target="tpu_custom_call" | custom-call | tf_op jit(solution)/shard_map/pallas_call | solution.py:1224
  186.4 1.0 fusion.9
  187.4 0.0 copy-start.1
  187.5 0.4 multiply_reduce_fusion.2
  187.9 0.9 copy-done.1
  188.9 1.2 fusion.3
  190.1 2.6 fusion.8
  192.7 0.3 add_reduce_fusion.1
  193.0 34.6 %shard_map.273 = (bf16[1024,4096]{1,0:T(8,128)(2,1)}, bf16[4096,1024]{1,0:T(8,128)(2,1)}, f32[1,4096]{1,0:T(1,128)S(1)}, f32[768,1024]{1,0:T(8,128)}) custom-call(bf16[768,1024]{1,0:T(8,128)(2,1)S(1)} %fusion.4.x_ref, bf16[768,1024]{1,0:T(8,128)(2,1)S(1)} %get-tuple-element.79.e_ref, bf16[1024,4096]{1,0:T(8,128)(2,1)} %bitcast.56, ...), custom_call_target="tpu_custom_call" | custom-call | tf_op jit(solution)/shard_map/pallas_call | solution.py:1268
  227.7 3.2 multiply_reduce_fusion
  230.9 0.0 copy-start.7
  230.9 0.9 fusion.7
  231.8 0.0 copy-start
  231.8 0.6 copy-done.7
  232.5 3.0 convolution_convert_fusion.1.dctx_ref
  235.5 0.3 add_reduce_fusion
  235.8 1.7 reduce
  237.5 0.1 convert_reduce_fusion.1
  237.6 0.7 pad.64.vec_ref
  238.3 0.0 copy-done
  238.4 4.6 convolution_convert_fusion
  243.0 215.6 %shard_map.274 = (f32[768,1024]{1,0:T(8,128)}, bf16[128,1024]{1,0:T(8,128)(2,1)}, bf16[128,4096]{1,0:T(8,128)(2,1)}, bf16[512,1024]{1,0:T(8,128)(2,1)}, bf16[128...) custom-call(bf16[768,1024]{1,0:T(8,128)(2,1)} %convolution_convert_f, ...), custom_call_target="tpu_custom_call" | custom-call | flops 96636764160 | bytes 7864320 | tf_op jit(solution)/shard_map/pallas_call | solution.py:1156
  458.6 0.0 copy-start.4
  458.6 0.0 copy-start.5
  458.6 5.0 %add_add_fusion.4 = f32[768,1024]{1,0:T(8,128)} fusion(f32[768,1024]{1,0:T(8,128)} %get-tuple-element.59, f32[768,1024]{1,0:T(8,128)} %copy-done, f32[768]{0:T(1024)S(1)} %negate_multiply_fusion), kind=kLoop, calls=%fused_computation.16 | loop fusion | flops 1572864 | bytes 9440256 | tf_op jit(solution)/shard_map/add | solution.py:1373
  463.6 0.0 copy-start.3
  463.6 0.0 copy-done.4
  463.6 0.0 copy-start.2
  463.6 1.3 convert_element_type.88
  464.9 0.8 slice_convert_fusion
  465.7 0.6 dynamic_slice.26
  466.3 0.6 dynamic_slice.27
  466.9 0.0 copy-done.5
  466.9 0.8 convert_element_type.91
  467.8 0.8 convert_reduce_fusion
  468.6 0.5 fusion.10
  469.1 0.0 copy-done.3
  469.1 1.5 convert_element_type.93
  470.7 0.6 slice.88
  471.2 0.0 copy-done.2
  471.3 1.6 convert_element_type.94
  (31 shorter events, 0.3 us)
Async XLA Ops:
  5.4 147.9 %copy-start.6 = (bf16[768,1024]{1,0:T(8,128)(2,1)S(1)}, bf16[768,1024]{1,0:T(8,128)(2,1)}, u32[]{:S(2)}) copy-start(bf16[768,1024]{1,0:T(8,128)(2,1)} %hid_ref.1) | copy-start | bytes 4718596
  187.4 1.4 copy-start.1
  230.9 1.6 copy-start.7
  231.8 6.5 %copy-start = (f32[768,1024]{1,0:T(8,128)}, f32[768,1024]{1,0:T(8,128)S(1)}, u32[]{:S(2)}) copy-start(f32[768,1024]{1,0:T(8,128)S(1)} %get-tuple-element.71) | copy-start | bytes 9437188
  458.6 5.0 %copy-start.4 = (bf16[128,3072]{1,0:T(8,128)(2,1)S(1)}, bf16[128,3072]{1,0:T(8,128)(2,1)}, u32[]{:S(2)}) copy-start(bf16[128,3072]{1,0:T(8,128)(2,1)} %get-tuple-element.60) | copy-start | bytes 2359300
  458.6 8.3 %copy-start.5 = (bf16[128,1024]{1,0:T(8,128)(2,1)S(1)}, bf16[128,1024]{1,0:T(8,128)(2,1)}, u32[]{:S(2)}) copy-start(bf16[128,1024]{1,0:T(8,128)(2,1)} %get-tuple-element.62) | copy-start | bytes 786436
  463.6 5.5 %copy-start.3 = (bf16[128,4096]{1,0:T(8,128)(2,1)S(1)}, bf16[128,4096]{1,0:T(8,128)(2,1)}, u32[]{:S(2)}) copy-start(bf16[128,4096]{1,0:T(8,128)(2,1)} %get-tuple-element.63) | copy-start | bytes 3145732
  463.6 7.6 %copy-start.2 = (bf16[512,1024]{1,0:T(8,128)(2,1)S(1)}, bf16[512,1024]{1,0:T(8,128)(2,1)}, u32[]{:S(2)}) copy-start(bf16[512,1024]{1,0:T(8,128)(2,1)} %get-tuple-element.64) | copy-start | bytes 3145732
